TPU v7x, 32 devices: a whole 2x2x4 slice. The times are simulated.
32 devices in a mesh: pair: 8 (over z, x), fac: 4 (over y, core).
Axes of the slice: x: 2, y: 2, z: 4, core: 2. Of those that a mesh axis runs over, the one named last changes fastest.
Arguments:
- amplitudes: bfloat16 [32, 1024, 1024], P(('pair', 'fac')), may hold values from -6 to 6
- mirror_slot: int32 [32], P(('pair', 'fac')), may hold values from 0 to 0, as said below
- d_values: bfloat16 [4, 16, 64, 64], P('fac'), may hold values from -0.375 to 0.375
- d_cols: int32 [4, 16], P('fac'), may hold values from 0 to 15
- b_values: bfloat16 [4, 16, 64, 64], P('fac'), may hold values from -0.375 to 0.375
- b_cols: int32 [4, 16], P('fac'), may hold values from 0 to 15
Outputs:
- residual: bfloat16 [32, 1024, 1024], P(('pair', 'fac'))
Inputs may be any that keep to these rules, and one draw needn't show every extreme that they name: Mirrors are mutual: the pairs on device pair index p and fac index f have their mirrors on pair index (p + 8/2) mod 8 with the same fac index, and m(m(n)) = n; on each device mirror_slot is a permutation of its 1 slots.
All inputs are finite; a program needn't handle non-finite values.
Results may differ from a plain program's by a relative error of at most 0.0059.
Values may be sent and summed in bfloat16 or wider, within the bound.
No kernel may reach another device: no remote copies, remote signals or barrier semaphores. Data moves between devices by JAX's collectives and lax.ppermute only.
A program may use at most 128 MiB of HBM per device.

v0:
```python
import jax
import jax.numpy as jnp
from jax import lax
from jax.sharding import PartitionSpec as P


def from_behind(shard, axis, by):
    count = lax.axis_size(axis)
    return lax.ppermute(shard, axis, [(i, (i + by) % count) for i in range(count)])


def pick_columns(columns, index):
    return jnp.take(columns, index, axis=2)


def dress_pairs(source, d_block, d_col, b_block, b_col):
    count = source.shape[0]
    size_v = source.shape[1]
    factors = d_col.shape[0]
    blocks = d_col.shape[1]
    width = size_v // blocks
    tiles = source.reshape(count, blocks, width, size_v)
    picked = jnp.take(tiles, d_col, axis=1)
    left = jnp.einsum("frab,pfrbv->pfrav", d_block, picked, preferred_element_type=jnp.bfloat16)
    columns = left.reshape(count, factors, size_v, blocks, width)
    chosen = jax.vmap(pick_columns, in_axes=(1, 0), out_axes=1)(columns, b_col)
    right = jnp.einsum("pfarb,frcb->parc", chosen, b_block, preferred_element_type=jnp.float32)
    return right.reshape(count, size_v, size_v)


def shards(amplitudes, mirror_slot, d_values, d_cols, b_values, b_cols):
    half = lax.axis_size("pair") // 2
    d_piece = lax.all_gather(d_values, "fac", axis=0, tiled=True)
    dcol_piece = lax.all_gather(d_cols, "fac", axis=0, tiled=True)
    b_piece = lax.all_gather(b_values, "fac", axis=0, tiled=True)
    bcol_piece = lax.all_gather(b_cols, "fac", axis=0, tiled=True)
    summed = dress_pairs(amplitudes, d_piece, dcol_piece, b_piece, bcol_piece)
    dressed = summed.astype(jnp.bfloat16)
    partner = from_behind(dressed, "pair", half)
    matched = jnp.take(partner, mirror_slot, axis=0)
    result = dressed.astype(jnp.float32) + jnp.swapaxes(matched, 1, 2).astype(jnp.float32)
    return result.astype(jnp.bfloat16)


def solution(mesh):
    placed = (
        P(("pair", "fac"), None, None),
        P(("pair", "fac")),
        P("fac", None, None, None),
        P("fac", None),
        P("fac", None, None, None),
        P("fac", None),
    )
    return jax.shard_map(
        shards,
        mesh=mesh,
        in_specs=placed,
        out_specs=P(("pair", "fac"), None, None),
        check_vma=False,
    )
```

profile of v0, /device:TPU:0, one launch (start us, length us, event | category | flops | bytes accessed | tf_op | source)
XLA Modules:
  0.0 202.5 jit_solution(7975662897309268609)
XLA Ops:
  0.0 0.0 copy-start
  0.0 6.3 %all-gather.1 = s32[4,1,16]{2,1,0:T(1,128)S(1)} all-gather(s32[1,1,16]{2,1,0:T(1,128)} %bitcast.47), channel_id=1, replica_groups=mesh['pair'=8,'fac'=4] {'fac'}, dimensions={0}, use_global_device_ids=true | all-gather | bytes 320 | tf_op jit(solution)/shard_map/all_gather | solution.py:34
  6.3 5.4 %all-gather = s32[4,1,16]{2,1,0:T(1,128)S(1)} all-gather(s32[1,1,16]{2,1,0:T(1,128)} %bitcast.48), channel_id=1, replica_groups=mesh['pair'=8,'fac'=4] {'fac'}, dimensions={0}, use_global_device_ids=true | all-gather | bytes 320 | tf_op jit(solution)/shard_map/all_gather | solution.py:36
  11.7 0.1 reshape.74
  11.8 10.5 %all_gather.14 = bf16[4,16,64,64]{3,2,1,0:T(8,128)(2,1)S(1)} all-gather(bf16[1,16,64,64]{3,2,1,0:T(8,128)(2,1)} %param.8), channel_id=1, replica_groups=mesh['pair'=8,'fac'=4] {'fac'}, dimensions={0}, use_global_device_ids=true | all-gather | bytes 655360 | tf_op jit(solution)/shard_map/all_gather | solution.py:33
  22.3 0.0 copy-done
  22.3 5.5 %gather_fusion = bf16[64,64,1024]{2,1,0:T(8,128)(2,1)} fusion(bf16[16,64,1024]{2,1,0:T(8,128)(2,1)S(1)} %bitcast.40, s32[1024]{0:T(1024)S(1)} %pad_clamp_fusion), kind=kCustom, calls=%fused_computation | custom fusion | bytes 16777472 | tf_op jit(solution)/shard_map/jit(_take)/gather | solution.py:23
  27.8 9.0 %fusion.7 = bf16[1,4,16,64,1024]{4,3,2,1,0:T(8,128)(2,1)} fusion(bf16[4,16,64,64]{3,2,1,0:T(8,128)(2,1)S(1)} %all_gather.14, bf16[4,16,64,1024]{3,2,1,0:T(8,128)(2,1)} %bitcast.42, pred[4,16]{1,0:T(4,128)(4,1)S(1)} %compare_and_fusion), kind=kOutput, calls=%fused_computation.9 | convolution fusion | flops 541065216 | bytes 17301568 | tf_op jit(solution)/shard_map/frab,pfrbv->pfrav/dot_general | solution.py:24
  36.8 22.1 %reshape.80 = bf16[4,1024,16,64]{3,2,1,0:T(8,128)(2,1)} reshape(bf16[1,4,16,64,1024]{4,3,2,1,0:T(8,128)(2,1)} %fusion.7) | data formatting | bytes 16777216 | tf_op jit(solution)/shard_map/vmap(jit(_take))/transpose | solution.py:13
  58.9 0.0 copy-start.2
  58.9 18.4 %copy.16 = bf16[4,1024,16,64]{1,3,2,0:T(8,128)(2,1)} copy(bf16[4,1024,16,64]{3,2,1,0:T(8,128)(2,1)} %reshape.80) | data formatting | bytes 16777216 | tf_op jit(solution)/shard_map/vmap(jit(_take))/transpose | solution.py:13
  77.3 0.1 reshape.82
  77.3 0.0 copy-done.2
  77.3 10.1 %all_gather.15 = bf16[4,16,64,64]{3,2,1,0:T(8,128)(2,1)S(1)} all-gather(bf16[1,16,64,64]{3,2,1,0:T(8,128)(2,1)S(1)} %copy-done.2), channel_id=1, replica_groups=mesh['pair'=8,'fac'=4] {'fac'}, dimensions={0}, use_global_device_ids=true | all-gather | bytes 655360 | tf_op jit(solution)/shard_map/all_gather | solution.py:35
  87.5 9.2 %gather_fusion.1 = bf16[64,1024,64]{1,2,0:T(8,128)(2,1)} fusion(bf16[4,1024,16,64]{1,3,2,0:T(8,128)(2,1)} %copy.16, s32[64]{0:T(128)S(1)} %reshape.82), kind=kCustom, calls=%fused_computation.1 | custom fusion | bytes 16777728 | tf_op jit(solution)/shard_map/vmap(jit(_take))/gather | solution.py:13
  96.7 6.8 %bitcast_convert_fusion = bf16[16,1024,64]{1,2,0:T(8,128)(2,1)} fusion(bf16[4,16,64,64]{3,2,1,0:T(8,128)(2,1)S(1)} %all_gather.15, bf16[4,16,1024,64]{2,3,1,0:T(8,128)(2,1)} %bitcast.41, pred[4,16]{1,0:T(4,128)(4,1)S(1)} %compare_and_fusion.1), kind=kOutput, calls=%fused_computation.12 | convolution fusion | flops 542113792 | bytes 11010112 | tf_op jit(solution)/shard_map/pfarb,frcb->parc/dot_general | solution.py:27
  103.5 2.6 %collective-permute-start = (bf16[1,1024,1024]{1,2,0:T(8,128)(2,1)}, bf16[1,1024,1024]{1,2,0:T(8,128)(2,1)}, u32[]{:S(2)}, u32[]{:S(2)}) collective-permute-start(bf16[1,1024,1024]{1,2,0:T(8,128)(2,1)} %bitcast.15), channel_id=1, source_target_pairs={{0,16},{4,20},{8,24},{12,28},{16,0},{20,4},{24,8},{28,12},{1,17},{... | collective-permute-start | bytes 6291464 | tf_op jit(solution)/shard_map/ppermute | solution.py:9
  106.8 0.0 copy-start.1
  106.8 4.2 %bitcast_convert_fusion.1 = f32[1,1024,1024]{1,2,0:T(8,128)} fusion(bf16[1,1024,1024]{1,2,0:T(8,128)(2,1)} %bitcast.39), kind=kLoop, calls=%fused_computation.21 | loop fusion | flops 1048576 | bytes 6291456 | tf_op jit(solution)/shard_map/convert_element_type | solution.py:41
  111.0 5.4 %copy.17 = f32[1,1024,1024]{2,1,0:T(8,128)} copy(f32[1,1024,1024]{1,2,0:T(8,128)} %bitcast_convert_fusion.1) | data formatting | bytes 8388608 | tf_op jit(solution)/shard_map/convert_element_type | solution.py:41
  116.3 81.2 %collective-permute-done = bf16[1,1024,1024]{1,2,0:T(8,128)(2,1)} collective-permute-done((bf16[1,1024,1024]{1,2,0:T(8,128)(2,1)}, bf16[1,1024,1024]{1,2,0:T(8,128)(2,1)}, u32[]{:S(2)}, u32[]{:S(2)}) %collective-permute-start) | collective-permute-done | bytes 2097184 | tf_op jit(solution)/shard_map/ppermute | solution.py:9
  197.5 5.0 %fusion.10 = bf16[1,1024,1024]{2,1,0:T(8,128)(2,1)} fusion(f32[1,1024,1024]{2,1,0:T(8,128)} %copy.17, bf16[1,1024,1024]{1,2,0:T(8,128)(2,1)} %collective-permute-done, pred[]{:T(512)} %bitcast.16), kind=kLoop, calls=%fused_computation.11 | loop fusion | flops 4194304 | bytes 8388609 | tf_op jit(solution)/shard_map/convert_element_type | solution.py:42
  202.5 0.0 copy-done.1
  (5 shorter events, 0.0 us)
Async XLA Ops:
  0.0 22.3 %copy-start = (bf16[1,1024,1024]{2,1,0:T(8,128)(2,1)S(1)}, bf16[1,1024,1024]{2,1,0:T(8,128)(2,1)}, u32[]{:S(2)}) copy-start(bf16[1,1024,1024]{2,1,0:T(8,128)(2,1)} %param.6) | copy-start | bytes 6291460
  58.9 18.5 %copy-start.2 = (bf16[1,16,64,64]{3,2,1,0:T(8,128)(2,1)S(1)}, bf16[1,16,64,64]{3,2,1,0:T(8,128)(2,1)}, u32[]{:S(2)}) copy-start(bf16[1,16,64,64]{3,2,1,0:T(8,128)(2,1)} %param.10) | copy-start | bytes 393220
  103.5 94.0 %collective-permute-start = (bf16[1,1024,1024]{1,2,0:T(8,128)(2,1)}, bf16[1,1024,1024]{1,2,0:T(8,128)(2,1)}, u32[]{:S(2)}, u32[]{:S(2)}) collective-permute-start(bf16[1,1024,1024]{1,2,0:T(8,128)(2,1)} %bitcast.15), channel_id=1, source_target_pairs={{0,16},{4,20},{8,24},{12,28},{16,0},{20,4},{24,8},{28,12},{1,17},{... | collective-permute-start | bytes 6291464 | tf_op jit(solution)/shard_map/ppermute | solution.py:9
  106.8 95.7 %copy-start.1 = (bf16[1,1024,1024]{2,1,0:T(8,128)(2,1)S(1)}, bf16[1,1024,1024]{2,1,0:T(8,128)(2,1)}, u32[]{:S(2)}) copy-start(bf16[1,1024,1024]{2,1,0:T(8,128)(2,1)} %param.6) | copy-start | bytes 6291460
where the time goes:
time: 204 us; the launch traced here: 203 us
  waiting for transfers between devices  81.2 us (40%)
  local copies, waits for them, and re-layouts  60.7 us (30%)
  blocking collectives  32.3 us (16%)
  matrix products  15.8 us (8%)
  other arithmetic  9.17 us (4%)
  starting transfers between devices  2.64 us (1%)
    ppermute x1, waiting for transfers between devices, from_behind(): lax.ppermute(shard, axis, [(i, (i + by) % count) for i in range(count)])  81.2 us
    transpose x2, local copies, waits for them, and re-layouts, pick_columns(): return jnp.take(columns, index, axis=2)  40.5 us
    all_gather x1, blocking collectives, shards(): d_piece = lax.all_gather(d_values, 'fac', axis=0, tiled=True)  10.5 us
    all_gather x1, blocking collectives, shards(): b_piece = lax.all_gather(b_values, 'fac', axis=0, tiled=True)  10.1 us
    gather x2, local copies, waits for them, and re-layouts, pick_columns(): return jnp.take(columns, index, axis=2)  9.3 us
    dot_general x1, matrix products, dress_pairs(): jnp.einsum('frab,pfrbv->pfrav', d_block, picked, preferred_element_type=j...  9 us
    dot_general x1, matrix products, dress_pairs(): jnp.einsum('pfarb,frcb->parc', chosen, b_block, preferred_element_type=jn...  6.8 us
    all_gather x1, blocking collectives, shards(): dcol_piece = lax.all_gather(d_cols, 'fac', axis=0, tiled=True)  6.29 us
  transfers between devices with their start and end apart: 1, of which 1 were waited for; matrix products, arithmetic and copies ran while one was open for 5% of the time, Pallas kernels for 0%

commit v1 on v0

v1 whole, which is shorter than its diff:
```python
import functools

import jax
import jax.numpy as jnp
from jax import lax
from jax.experimental import pallas as pl
from jax.experimental.pallas import tpu as pltpu
from jax.sharding import PartitionSpec as P

LANES = 128
BF16, F32 = jnp.bfloat16, jnp.float32
WHOLE = pl.BlockSpec(memory_space=pltpu.VMEM)
SCALARS = pl.BlockSpec(memory_space=pltpu.SMEM)
ANYWHERE = pl.BlockSpec(memory_space=pl.ANY)
VMEM_BYTES = 28 << 20


def params():
    return pltpu.CompilerParams(vmem_limit_bytes=VMEM_BYTES)


def turn_kernel(marks, source, *turned):
    for lo in range(marks[0], marks[-1], LANES):
        strip = source[0, :, lo - marks[0] : lo - marks[0] + LANES].T
        for first, last, piece in zip(marks, marks[1:], turned):
            a, b = max(lo, first), min(lo + LANES, last)
            if a < b:
                piece[0, a - first : b - first, :] = strip[a - lo : b - lo, :]


def turn(amplitudes, marks):
    size = amplitudes.shape[1]
    return pl.pallas_call(
        functools.partial(turn_kernel, marks),
        in_specs=[WHOLE],
        out_specs=[WHOLE] * (len(marks) - 1),
        out_shape=[jax.ShapeDtypeStruct((1, b - a, size), BF16) for a, b in zip(marks, marks[1:])],
        compiler_params=params(),
        name="turn",
    )(amplitudes[:, :, marks[0] : marks[-1]])


def spread_right(values, columns, side, spread):
    factors, blocks, width = values.shape[0], values.shape[1], values.shape[2]
    spread[...] = jnp.zeros(spread.shape, BF16)

    def one(group, carry):
        for q in range(factors):
            for i in range(2):
                s = 2 * group + i
                row = i * LANES + (columns[q, side, s] % 2) * width
                block = values[q, s].T
                spread[q, group, pl.ds(pl.multiple_of(row, width), width), i * width : (i + 1) * width] = block
        return carry

    lax.fori_loop(0, blocks // 2, one, 0)


def join_left(values, joined):
    factors, blocks, width = values.shape[0], values.shape[1], values.shape[2]

    def one(r, carry):
        for q in range(factors):
            joined[r, :, q * width : (q + 1) * width] = values[q, r]
        return carry

    lax.fori_loop(0, blocks, one, 0)


def apply_right(source, columns, side, spread, middle, first, rows, step):
    factors, groups = spread.shape[0], spread.shape[1]

    def one(q, carry):
        for g in range(groups):
            a = pl.multiple_of(columns[q, side, 2 * g] // 2 * LANES, LANES)
            b = pl.multiple_of(columns[q, side, 2 * g + 1] // 2 * LANES, LANES)
            weights = spread[q, g]
            for m in range(0, rows, step):
                picked = jnp.concatenate([source(m, step, a), source(m, step, b)], axis=1)
                product = jnp.dot(picked, weights, preferred_element_type=F32)
                middle[q, first + m : first + m + step, g * LANES : (g + 1) * LANES] = product.astype(BF16)
        return carry

    lax.fori_loop(0, factors, one, 0)


def apply_left(r, joined, columns, side, middle):
    factors = middle.shape[0]
    width = joined.shape[1]
    picked = [
        middle[q, pl.ds(pl.multiple_of(columns[q, side, r] * width, width), width), :] for q in range(factors)
    ]
    return jnp.dot(joined[r], jnp.concatenate(picked, axis=0), preferred_element_type=F32)


def own_kernel(columns, d_all, b_all, source, dressed, spread_d, joined_b, spread_b, joined_d, middle):
    blocks, width = d_all.shape[1], d_all.shape[2]
    size = source.shape[1]
    spread_right(b_all, columns, 1, spread_b)
    join_left(d_all, joined_d)
    spread_right(d_all, columns, 0, spread_d)
    join_left(b_all, joined_b)
    step = min(256, size)
    apply_right(
        lambda m, rows, lane: source[0, m : m + rows, pl.ds(lane, LANES)], columns, 1, spread_b, middle, 0, size, step
    )

    def one(r, carry):
        block = apply_left(r, joined_d, columns, 0, middle)
        dressed[pl.ds(pl.multiple_of(r * width, width), width), :] = block.astype(BF16)
        return carry

    lax.fori_loop(0, blocks, one, 0)


def own_pair(columns, d_all, b_all, amplitudes):
    factors, blocks, width = d_all.shape[:3]
    size = amplitudes.shape[1]
    spread = (factors, blocks // 2, 2 * LANES, LANES)
    joined = (blocks, width, factors * width)
    return pl.pallas_call(
        own_kernel,
        in_specs=[SCALARS, WHOLE, WHOLE, WHOLE],
        out_specs=[WHOLE] * 3,
        out_shape=[
            pltpu.VMEM((size, size), BF16),
            pltpu.VMEM(spread, BF16),
            pltpu.VMEM(joined, BF16),
        ],
        scratch_shapes=[
            pltpu.VMEM(spread, BF16),
            pltpu.VMEM(joined, BF16),
            pltpu.VMEM((factors, size, size), BF16),
        ],
        compiler_params=params(),
        name="own",
    )(columns, d_all, b_all, amplitudes)


def mirror_kernel(lo, hi, again, columns, slot, piece, spread_d, joined_b, dressed, *rest):
    middle, out, ready, sems = rest[2:] if again else rest
    factors, blocks, width = spread_d.shape[0], joined_b.shape[0], joined_b.shape[1]
    rows = (hi - lo) * width
    step = min(256, rows)
    while rows % step:
        step //= 2
    which = slot[0]
    apply_right(
        lambda m, n, lane: piece[which, m : m + n, pl.ds(lane, LANES)],
        columns,
        0,
        spread_d,
        middle,
        lo * width,
        rows,
        step,
    )

    def last_of(r):
        last = columns[0, 1, r]
        for q in range(1, factors):
            last = jnp.maximum(last, columns[q, 1, r])
        return jnp.logical_and(last >= lo, last < hi)

    def place(r):
        rows = pl.ds(pl.multiple_of(r * width, width), width)
        return pltpu.make_async_copy(ready.at[r], out.at[rows, :], sems.at[r])

    def one(r, carry):
        @pl.when(last_of(r))
        def _():
            rows = pl.ds(pl.multiple_of(r * width, width), width)
            mirrored = apply_left(r, joined_b, columns, 1, middle).astype(BF16)
            ready[r] = (dressed[rows, :].astype(F32) + mirrored.astype(F32)).astype(BF16)
            place(r).start()

        return carry

    def wait(r, carry):
        @pl.when(last_of(r))
        def _():
            place(r).wait()

        return carry

    lax.fori_loop(0, blocks, one, 0)
    lax.fori_loop(0, blocks, wait, 0)


def mirror_piece(lo, hi, columns, slot, piece, spread_d, joined_b, dressed, state):
    factors, blocks, width = spread_d.shape[0], joined_b.shape[0], joined_b.shape[1]
    size = dressed.shape[0]
    again = state is not None
    state = state or ()
    middle = pltpu.VMEM((factors, size, size), BF16)
    return pl.pallas_call(
        functools.partial(mirror_kernel, lo, hi, again),
        in_specs=[SCALARS, SCALARS, WHOLE, WHOLE, WHOLE, WHOLE] + ([WHOLE, ANYWHERE] if again else []),
        out_specs=[WHOLE, ANYWHERE],
        out_shape=[middle, jax.ShapeDtypeStruct((size, size), BF16)],
        scratch_shapes=[pltpu.VMEM((blocks, width, size), BF16), pltpu.SemaphoreType.DMA((blocks,))],
        input_output_aliases={6: 0, 7: 1} if again else {},
        compiler_params=params(),
        name="mirror",
    )(columns, slot, piece, spread_d, joined_b, dressed, *state)


def cuts(blocks):
    marks = [0, 4, 10, 14, 15, 16]
    return [m * blocks // 16 for m in marks]


def shards(amplitudes, mirror_slot, d_values, d_cols, b_values, b_cols):
    pairs = lax.axis_size("pair")
    perm = [(i, (i + pairs // 2) % pairs) for i in range(pairs)]
    count, size = amplitudes.shape[0], amplitudes.shape[1]
    assert count == 1
    blocks, width = d_values.shape[1], d_values.shape[2]

    marks = cuts(blocks)
    lanes = [m * width for m in marks]
    turned = turn(amplitudes, lanes[:2]) + turn(amplitudes, lanes[1:])

    columns = jnp.stack([d_cols, b_cols], axis=1)
    turned, columns, d_values, b_values = lax.optimization_barrier((turned, columns, d_values, b_values))
    pieces = [lax.ppermute(piece, "pair", perm) for piece in turned]
    columns, d_all, b_all = (lax.all_gather(a, "fac", axis=0, tiled=True) for a in (columns, d_values, b_values))
    dressed, spread_d, joined_b = own_pair(columns, d_all, b_all, amplitudes)

    state = None
    for lo, hi, piece in zip(marks, marks[1:], pieces):
        state = mirror_piece(lo, hi, columns, mirror_slot, piece, spread_d, joined_b, dressed, state)
    return state[1][None]


def solution(mesh):
    placed = (
        P(("pair", "fac"), None, None),
        P(("pair", "fac")),
        P("fac", None, None, None),
        P("fac", None),
        P("fac", None, None, None),
        P("fac", None),
    )
    return jax.shard_map(
        shards,
        mesh=mesh,
        in_specs=placed,
        out_specs=P(("pair", "fac"), None, None),
        check_vma=False,
    )
```

time: 204 us -> 106 us (0.52)
  local copies, waits for them, and re-layouts: 60.7 us -> 2.62 us
  waiting for transfers between devices: 81.2 us -> 31.1 us
  Pallas kernels: 0 us -> 35.5 us
  matrix products: 15.8 us -> 0 us
  other arithmetic: 9.17 us -> 0.01 us
  starting transfers between devices: 2.64 us -> 9.95 us
  blocking collectives: 32.3 us -> 25.3 us
    ppermute x1 -> x5, waiting for transfers between devices: 81.2 us -> 31.1 us  [shards(): pieces = [lax.ppermute(piece, 'pair', perm) for piece in turned]]
    transpose x2 -> x0, local copies, waits for them, and re-layouts: 40.5 us -> none  [pick_columns(): return jnp.take(columns, index, axis=2)]
    pallas_call x0 -> x8, Pallas kernels: none -> 35.5 us  [the longest x5 19.6 us: mirror_piece(): pl.pallas_call(functools.partial(mirror_kernel, lo, hi, again), in_specs=...]
    dot_general x2 -> x0, matrix products: 15.8 us -> none  [the longest x1 9 us: dress_pairs(): jnp.einsum('frab,pfrbv->pfrav', d_block, picked, preferred_element_type=j...]
    gather x3 -> x0, local copies, waits for them, and re-layouts: 14.8 us -> none  [the longest x2 9.3 us: pick_columns(): return jnp.take(columns, index, axis=2)]
    convert_element_type x2 -> x0, other arithmetic: 9.14 us -> none  [the longest x1 4.96 us: shards(): return result.astype(jnp.bfloat16)]
    ppermute x1 -> x5, starting transfers between devices: 2.64 us -> 9.95 us  [shards(): pieces = [lax.ppermute(piece, 'pair', perm) for piece in turned]]
    all_gather x4 -> x3, blocking collectives: 32.3 us -> 25.3 us  [shards(): lax.all_gather(a, 'fac', axis=0, tiled=True)]
  transfers between devices with their start and end apart: 1 -> 5, of which waited for: 1 -> 2; matrix products, arithmetic and copies ran while one was open for 5% -> 0% of each run, Pallas kernels for 0% -> 29%
where the time goes in v1:
time: 106 us; the launch traced here: 105 us
  Pallas kernels  35.5 us (33%)
  waiting for transfers between devices  31.1 us (29%)
  blocking collectives  25.3 us (24%)
  starting transfers between devices  9.95 us (9%)
  local copies, waits for them, and re-layouts  2.62 us (2%)
    ppermute x5, waiting for transfers between devices, shards(): pieces = [lax.ppermute(piece, 'pair', perm) for piece in turned]  31.1 us
    all_gather x3, blocking collectives, shards(): lax.all_gather(a, 'fac', axis=0, tiled=True)  25.3 us
    pallas_call x5, Pallas kernels, mirror_piece(): pl.pallas_call(functools.partial(mirror_kernel, lo, hi, again), in_specs=...  19.6 us
    pallas_call x1, Pallas kernels, own_pair(): pl.pallas_call(own_kernel, in_specs=[SCALARS, WHOLE, WHOLE, WHOLE], out_s...  15.2 us
    ppermute x5, starting transfers between devices, shards(): pieces = [lax.ppermute(piece, 'pair', perm) for piece in turned]  9.95 us
    slice x2, local copies, waits for them, and re-layouts, turn(): amplitudes[:, :, marks[0]:marks[-1]]  2.59 us
  transfers between devices with their start and end apart: 5, of which 2 were waited for; matrix products, arithmetic and copies ran while one was open for 0% of the time, Pallas kernels for 29%

profile of v1, /device:TPU:0, one launch (start us, length us, event | category | flops | bytes accessed | tf_op | source)
XLA Modules:
  0.0 105.2 jit_solution(17238027373376610539)
XLA Ops:
  0.0 1.1 %slice.6.source = bf16[1,1024,256]{2,1,0:T(8,128)(2,1)S(1)} slice(bf16[1,1024,1024]{2,1,0:T(8,128)(2,1)} %source.1), slice={[0:1], [0:1024], [0:256]} | slice | bytes 1048576 | tf_op jit(solution)/shard_map/slice | solution.py:40
  1.1 1.5 %slice.7.source = bf16[1,1024,768]{2,1,0:T(8,128)(2,1)S(1)} slice(bf16[1,1024,1024]{2,1,0:T(8,128)(2,1)} %source.1), slice={[0:1], [0:1024], [256:1024]} | slice | bytes 3145728 | tf_op jit(solution)/shard_map/slice | solution.py:40
  2.6 0.0 copy-start.3
  2.6 0.0 copy-start.4
  2.6 0.0 copy-start.1
  2.6 0.0 copy-start.2
  2.6 0.2 turn.2
  2.8 0.0 copy-start
  2.8 0.5 turn.3
  3.3 0.0 copy-done.3
  3.3 0.0 copy-done.4
  3.3 4.1 %collective-permute-start.3 = (bf16[1,384,1024]{2,1,0:T(8,128)(2,1)S(1)}, bf16[1,384,1024]{2,1,0:T(8,128)(2,1)S(1)}, u32[]{:S(2)}, u32[]{:S(2)}) collective-permute-start(bf16[1,384,1024]{2,1,0:T(8,128)(2,1)S(1)} %get-tuple-element.42), channel_id=1, source_target_pairs={{0,16},{4,20},{8,24},{12,28},{16,0},{20,4},{24,8},{28,12},{1,17},{... | collective-permute-start | bytes 2359304 | tf_op jit(solution)/shard_map/ppermute | solution.py:226
  7.4 0.1 collective-permute-start.4
  7.5 2.8 %collective-permute-start.2 = (bf16[1,256,1024]{2,1,0:T(8,128)(2,1)S(1)}, bf16[1,256,1024]{2,1,0:T(8,128)(2,1)S(1)}, u32[]{:S(2)}, u32[]{:S(2)}) collective-permute-start(bf16[1,256,1024]{2,1,0:T(8,128)(2,1)S(1)} %get-tuple-element.41), channel_id=1, source_target_pairs={{0,16},{4,20},{8,24},{12,28},{16,0},{20,4},{24,8},{28,12},{1,17},{... | collective-permute-start | bytes 1572872 | tf_op jit(solution)/shard_map/ppermute | solution.py:226
  10.4 0.1 collective-permute-start
  10.5 2.8 %collective-permute-start.1 = (bf16[1,64,1024]{2,1,0:T(8,128)(2,1)S(1)}, bf16[1,64,1024]{2,1,0:T(8,128)(2,1)S(1)}, u32[]{:S(2)}, u32[]{:S(2)}) collective-permute-start(bf16[1,64,1024]{2,1,0:T(8,128)(2,1)S(1)} %get-tuple-element.40), channel_id=1, source_target_pairs={{0,16},{4,20},{8,24},{12,28},{16,0},{20,4},{24,8},{28,12},{1,17},{... | collective-permute-start | bytes 393224 | tf_op jit(solution)/shard_map/ppermute | solution.py:226
  14.0 5.1 %all_gather.9.columns = s32[4,2,16]{2,1,0:T(2,128)S(1)} all-gather(s32[1,2,16]{2,1,0:T(2,128)S(1)} %pad_add_fusion), channel_id=1, replica_groups=mesh['pair'=8,'fac'=4] {'fac'}, dimensions={0}, use_global_device_ids=true | all-gather | bytes 640 | tf_op jit(solution)/shard_map/all_gather | solution.py:227
  19.0 0.0 copy-done.1
  19.0 10.1 %all_gather.10.d_all = bf16[4,16,64,64]{3,2,1,0:T(8,128)(2,1)S(1)} all-gather(bf16[1,16,64,64]{3,2,1,0:T(8,128)(2,1)S(1)} %copy-done.1), channel_id=1, replica_groups=mesh['pair'=8,'fac'=4] {'fac'}, dimensions={0}, use_global_device_ids=true | all-gather | bytes 655360 | tf_op jit(solution)/shard_map/all_gather | solution.py:227
  29.1 0.0 copy-done.2
  29.1 10.1 %all_gather.11.b_all = bf16[4,16,64,64]{3,2,1,0:T(8,128)(2,1)S(1)} all-gather(bf16[1,16,64,64]{3,2,1,0:T(8,128)(2,1)S(1)} %copy-done.2), channel_id=1, replica_groups=mesh['pair'=8,'fac'=4] {'fac'}, dimensions={0}, use_global_device_ids=true | all-gather | bytes 655360 | tf_op jit(solution)/shard_map/all_gather | solution.py:227
  39.3 0.0 copy-done
  39.3 15.2 %own.1 = (bf16[1024,1024]{1,0:T(8,128)(2,1)S(1)}, bf16[4,8,256,128]{3,2,1,0:T(8,128)(2,1)S(1)}, bf16[16,64,256]{2,1,0:T(8,128)(2,1)S(1)}) custom-call(s32[4,2,16]{2,1,0:T(2,128)S(1)} %all_gather.9.columns, bf16[4,16,64,64]{3,2,1,0:T(8,128)(2,1)S(1)} %all_gather.10.d_all, bf16[4,16,64,64]{3,2,1,0:T(8,128)(2,1)S(1)} %all_gather.11.b_all, ...), custom_call_target="tpu_custom_call" | custom-call | tf_op jit(solution)/shard_map/own/pallas_call | solution.py:121
  54.5 27.5 %collective-permute-done.4.piece = bf16[1,256,1024]{2,1,0:T(8,128)(2,1)S(1)} collective-permute-done((bf16[1,256,1024]{2,1,0:T(8,128)(2,1)S(1)}, bf16[1,256,1024]{2,1,0:T(8,128)(2,1)S(1)}, u32[]{:S(2)}, u32[]{:S(2)}) %collective-permute-start.4) | collective-permute-done | bytes 524320 | tf_op jit(solution)/shard_map/ppermute | solution.py:226
  82.0 3.2 %mirror.5 = (bf16[4,1024,1024]{2,1,0:T(8,128)(2,1)S(1)}, bf16[1024,1024]{1,0:T(8,128)(2,1)}) custom-call(s32[4,2,16]{2,1,0:T(2,128)S(1)} %all_gather.9.columns, s32[1]{0:T(128)S(6)} %copy.23.slot, bf16[1,256,1024]{2,1,0:T(8,128)(2,1)S(1)} %collective-permute-done.4.piece, bf16[4,8,256,128]{3,2,1,0:T(8,128)(2,1)S(1)} %get-tuple-element.37.spread_d, ...), custom_call_target="tpu_custom_call" | custom-call | tf_op jit(solution)/shard_map/mirror/pallas_call | solution.py:196
  85.2 0.0 collective-permute-done.3.piece
  85.2 4.5 %mirror.6 = (bf16[4,1024,1024]{2,1,0:T(8,128)(2,1)S(1)}, bf16[1024,1024]{1,0:T(8,128)(2,1)}) custom-call(s32[4,2,16]{2,1,0:T(2,128)S(1)} %all_gather.9.columns, s32[1]{0:T(128)S(6)} %copy.23.slot, bf16[1,384,1024]{2,1,0:T(8,128)(2,1)S(1)} %collective-permute-done.3.piece, ...), custom_call_target="tpu_custom_call", output_to_operand_aliasing={{0}: (6, {}), {1}: (7, {})} | custom-call | tf_op jit(solution)/shard_map/mirror/pallas_call | solution.py:196
  89.7 3.6 %collective-permute-done.2.piece = bf16[1,256,1024]{2,1,0:T(8,128)(2,1)S(1)} collective-permute-done((bf16[1,256,1024]{2,1,0:T(8,128)(2,1)S(1)}, bf16[1,256,1024]{2,1,0:T(8,128)(2,1)S(1)}, u32[]{:S(2)}, u32[]{:S(2)}) %collective-permute-start.2) | collective-permute-done | bytes 524320 | tf_op jit(solution)/shard_map/ppermute | solution.py:226
  93.2 5.0 %mirror.7 = (bf16[4,1024,1024]{2,1,0:T(8,128)(2,1)S(1)}, bf16[1024,1024]{1,0:T(8,128)(2,1)}) custom-call(s32[4,2,16]{2,1,0:T(2,128)S(1)} %all_gather.9.columns, s32[1]{0:T(128)S(6)} %copy.23.slot, bf16[1,256,1024]{2,1,0:T(8,128)(2,1)S(1)} %collective-permute-done.2.piece, ...), custom_call_target="tpu_custom_call", output_to_operand_aliasing={{0}: (6, {}), {1}: (7, {})} | custom-call | tf_op jit(solution)/shard_map/mirror/pallas_call | solution.py:196
  98.2 0.0 collective-permute-done.1.piece
  98.2 3.0 %mirror.8 = (bf16[4,1024,1024]{2,1,0:T(8,128)(2,1)S(1)}, bf16[1024,1024]{1,0:T(8,128)(2,1)}) custom-call(s32[4,2,16]{2,1,0:T(2,128)S(1)} %all_gather.9.columns, s32[1]{0:T(128)S(6)} %copy.23.slot, bf16[1,64,1024]{2,1,0:T(8,128)(2,1)S(1)} %collective-permute-done.1.piece, ...), custom_call_target="tpu_custom_call", output_to_operand_aliasing={{0}: (6, {}), {1}: (7, {})} | custom-call | tf_op jit(solution)/shard_map/mirror/pallas_call | solution.py:196
  101.2 0.0 collective-permute-done.piece
  101.2 4.0 %mirror.9 = (bf16[4,1024,1024]{2,1,0:T(8,128)(2,1)S(1)}, bf16[1024,1024]{1,0:T(8,128)(2,1)}) custom-call(s32[4,2,16]{2,1,0:T(2,128)S(1)} %all_gather.9.columns, s32[1]{0:T(128)S(6)} %copy.23.slot, bf16[1,64,1024]{2,1,0:T(8,128)(2,1)S(1)} %collective-permute-done.piece, ...), custom_call_target="tpu_custom_call", output_to_operand_aliasing={{0}: (6, {}), {1}: (7, {})} | custom-call | tf_op jit(solution)/shard_map/mirror/pallas_call | solution.py:196
  (1 shorter events, 0.0 us)
Async XLA Ops:
  2.6 0.7 copy-start.3
  2.6 0.7 copy-start.4
  2.6 16.4 %copy-start.1 = (bf16[1,16,64,64]{3,2,1,0:T(8,128)(2,1)S(1)}, bf16[1,16,64,64]{3,2,1,0:T(8,128)(2,1)}, u32[]{:S(2)}) copy-start(bf16[1,16,64,64]{3,2,1,0:T(8,128)(2,1)} %param.8) | copy-start | bytes 393220
  2.6 26.5 %copy-start.2 = (bf16[1,16,64,64]{3,2,1,0:T(8,128)(2,1)S(1)}, bf16[1,16,64,64]{3,2,1,0:T(8,128)(2,1)}, u32[]{:S(2)}) copy-start(bf16[1,16,64,64]{3,2,1,0:T(8,128)(2,1)} %param.10) | copy-start | bytes 393220
  2.8 36.4 %copy-start = (bf16[1,1024,1024]{2,1,0:T(8,128)(2,1)S(1)}, bf16[1,1024,1024]{2,1,0:T(8,128)(2,1)}, u32[]{:S(2)}) copy-start(bf16[1,1024,1024]{2,1,0:T(8,128)(2,1)} %source.1) | copy-start | bytes 6291460
  3.3 81.8 %collective-permute-start.3 = (bf16[1,384,1024]{2,1,0:T(8,128)(2,1)S(1)}, bf16[1,384,1024]{2,1,0:T(8,128)(2,1)S(1)}, u32[]{:S(2)}, u32[]{:S(2)}) collective-permute-start(bf16[1,384,1024]{2,1,0:T(8,128)(2,1)S(1)} %get-tuple-element.42), channel_id=1, source_target_pairs={{0,16},{4,20},{8,24},{12,28},{16,0},{20,4},{24,8},{28,12},{1,17},{... | collective-permute-start | bytes 2359304 | tf_op jit(solution)/shard_map/ppermute | solution.py:226
  7.4 74.5 %collective-permute-start.4 = (bf16[1,256,1024]{2,1,0:T(8,128)(2,1)S(1)}, bf16[1,256,1024]{2,1,0:T(8,128)(2,1)S(1)}, u32[]{:S(2)}, u32[]{:S(2)}) collective-permute-start(bf16[1,256,1024]{2,1,0:T(8,128)(2,1)S(1)} %turn.2), channel_id=1, source_target_pairs={{0,16},{4,20},{8,24},{12,28},{16,0},{20,4},{24,8},{28,12},{1,17},{... | collective-permute-start | bytes 1572872 | tf_op jit(solution)/shard_map/ppermute | solution.py:226
  7.5 85.7 %collective-permute-start.2 = (bf16[1,256,1024]{2,1,0:T(8,128)(2,1)S(1)}, bf16[1,256,1024]{2,1,0:T(8,128)(2,1)S(1)}, u32[]{:S(2)}, u32[]{:S(2)}) collective-permute-start(bf16[1,256,1024]{2,1,0:T(8,128)(2,1)S(1)} %get-tuple-element.41), channel_id=1, source_target_pairs={{0,16},{4,20},{8,24},{12,28},{16,0},{20,4},{24,8},{28,12},{1,17},{... | collective-permute-start | bytes 1572872 | tf_op jit(solution)/shard_map/ppermute | solution.py:226
  10.4 90.9 %collective-permute-start = (bf16[1,64,1024]{2,1,0:T(8,128)(2,1)S(1)}, bf16[1,64,1024]{2,1,0:T(8,128)(2,1)S(1)}, u32[]{:S(2)}, u32[]{:S(2)}) collective-permute-start(bf16[1,64,1024]{2,1,0:T(8,128)(2,1)S(1)} %get-tuple-element.34), channel_id=1, source_target_pairs={{0,16},{4,20},{8,24},{12,28},{16,0},{20,4},{24,8},{28,12},{1,17},{... | collective-permute-start | bytes 393224 | tf_op jit(solution)/shard_map/ppermute | solution.py:226
  10.5 87.8 %collective-permute-start.1 = (bf16[1,64,1024]{2,1,0:T(8,128)(2,1)S(1)}, bf16[1,64,1024]{2,1,0:T(8,128)(2,1)S(1)}, u32[]{:S(2)}, u32[]{:S(2)}) collective-permute-start(bf16[1,64,1024]{2,1,0:T(8,128)(2,1)S(1)} %get-tuple-element.40), channel_id=1, source_target_pairs={{0,16},{4,20},{8,24},{12,28},{16,0},{20,4},{24,8},{28,12},{1,17},{... | collective-permute-start | bytes 393224 | tf_op jit(solution)/shard_map/ppermute | solution.py:226

commit v2 on v0

v2 whole, which is shorter than its diff:
```python
import functools

import jax
import jax.numpy as jnp
from jax import lax
from jax.experimental import pallas as pl
from jax.experimental.pallas import tpu as pltpu
from jax.sharding import PartitionSpec as P

LANES = 128
BF16, F32 = jnp.bfloat16, jnp.float32
WHOLE = pl.BlockSpec(memory_space=pltpu.VMEM)
SCALARS = pl.BlockSpec(memory_space=pltpu.SMEM)
FAR = pl.BlockSpec(memory_space=pltpu.HBM)
VMEM_BYTES = 28 << 20


def params():
    return pltpu.CompilerParams(vmem_limit_bytes=VMEM_BYTES)


def aligned(start, size):
    return pl.ds(pl.multiple_of(start, size), size)


def strips_of(marks):
    return range(marks[0] // LANES * LANES, marks[-1], LANES)


def turn_kernel(marks, source, *rest):
    turned, strips, sems = rest[:-2], rest[-2], rest[-1]
    starts = strips_of(marks)
    copies = [
        pltpu.make_async_copy(source.at[0, :, lo : lo + LANES], strips.at[i], sems.at[i]) for i, lo in enumerate(starts)
    ]
    for copy in copies:
        copy.start()
    for i, lo in enumerate(starts):
        copies[i].wait()
        strip = strips[i].T
        for first, last, piece in zip(marks, marks[1:], turned):
            a, b = max(lo, first), min(lo + LANES, last)
            if a < b:
                piece[0, a - first : b - first, :] = strip[a - lo : b - lo, :]


def turn(amplitudes, marks):
    size = amplitudes.shape[1]
    count = len(strips_of(marks))
    return pl.pallas_call(
        functools.partial(turn_kernel, marks),
        in_specs=[FAR],
        out_specs=[WHOLE] * (len(marks) - 1),
        out_shape=[jax.ShapeDtypeStruct((1, b - a, size), BF16) for a, b in zip(marks, marks[1:])],
        scratch_shapes=[pltpu.VMEM((count, size, LANES), BF16), pltpu.SemaphoreType.DMA((count,))],
        compiler_params=params(),
        name="turn",
    )(amplitudes)


def spread_right(values, columns, side, spread):
    factors, blocks, width = values.shape[:3]
    spread[...] = jnp.zeros(spread.shape, BF16)

    def one(group, carry):
        for q in range(factors):
            for i in range(2):
                s = 2 * group + i
                row = i * LANES + (columns[q, side, s] % 2) * width
                spread[q, group, aligned(row, width), i * width : (i + 1) * width] = values[q, s].T
        return carry

    lax.fori_loop(0, blocks // 2, one, 0)


def join_left(values, joined):
    factors, blocks, width = values.shape[:3]

    def one(r, carry):
        for q in range(factors):
            joined[r, :, q * width : (q + 1) * width] = values[q, r]
        return carry

    lax.fori_loop(0, blocks, one, 0)


def apply_right(pick, lanes, spread, q, middle, first, rows):
    for g in range(spread.shape[1]):
        picked = jnp.concatenate([pick(lanes(q, 2 * g)), pick(lanes(q, 2 * g + 1))], axis=1)
        product = jnp.dot(picked, spread[q, g], preferred_element_type=F32)
        middle[q, pl.ds(first, rows), g * LANES : (g + 1) * LANES] = product.astype(BF16)


def apply_left(r, joined, starts, middle):
    factors, width = middle.shape[0], joined.shape[1]
    picked = [middle[q, aligned(starts(q, r), width), :] for q in range(factors)]
    return jnp.dot(joined[r], jnp.concatenate(picked, axis=0), preferred_element_type=F32)


class Plan:
    def __init__(self, factors, blocks, pieces):
        self.blocks = blocks
        self.lanes = 0
        self.rows = factors * blocks
        self.order = 2 * factors * blocks
        self.begin = self.order + blocks
        self.slot = self.begin + pieces + 1
        self.size = self.slot + 1


def make_plan(marks, plan, columns, slot, scalars):
    factors, blocks = columns.shape[0], columns.shape[2]

    def offsets(s, carry):
        for q in range(factors):
            scalars[plan.lanes + q * blocks + s] = columns[q, 0, s] // 2 * LANES
            scalars[plan.rows + q * blocks + s] = columns[q, 1, s] * (LANES // 2)
        return carry

    lax.fori_loop(0, blocks, offsets, 0)
    place = jnp.int32(0)
    for j, (lo, hi) in enumerate(zip(marks, marks[1:])):
        scalars[plan.begin + j] = place

        def one(r, place, lo=lo, hi=hi):
            last = columns[0, 1, r]
            for q in range(1, factors):
                last = jnp.maximum(last, columns[q, 1, r])
            here = jnp.logical_and(last >= lo, last < hi)

            @pl.when(here)
            def _():
                scalars[plan.order + place] = r

            return place + here.astype(jnp.int32)

        place = lax.fori_loop(0, blocks, one, place)
    scalars[plan.begin + len(marks) - 1] = place
    scalars[plan.slot] = slot[0]


def own_kernel(
    marks, plan, columns, slot, d_all, b_all, source, dressed, spread_d, joined_b, scalars, spread_b, joined_d, middle
):
    factors, blocks, width = d_all.shape[:3]
    size = source.shape[1]
    make_plan(marks, plan, columns, slot, scalars)
    spread_right(b_all, columns, 1, spread_b)
    join_left(d_all, joined_d)
    spread_right(d_all, columns, 0, spread_d)
    join_left(b_all, joined_b)
    step = min(256, size)

    def right(q, carry):
        for m in range(0, size, step):
            apply_right(
                lambda lane: source[0, m : m + step, aligned(lane, LANES)],
                lambda q, s: columns[q, 1, s] // 2 * LANES,
                spread_b,
                q,
                middle,
                m,
                step,
            )
        return carry

    def left(r, carry):
        block = apply_left(r, joined_d, lambda q, r: columns[q, 0, r] * width, middle)
        dressed[aligned(r * width, width), :] = block.astype(BF16)
        return carry

    lax.fori_loop(0, factors, right, 0)
    lax.fori_loop(0, blocks, left, 0)


def own_pair(marks, plan, columns, slot, d_all, b_all, amplitudes):
    factors, blocks, width = d_all.shape[:3]
    size = amplitudes.shape[1]
    spread = (factors, blocks // 2, 2 * LANES, LANES)
    joined = (blocks, width, factors * width)
    return pl.pallas_call(
        functools.partial(own_kernel, marks, plan),
        in_specs=[SCALARS, SCALARS, WHOLE, WHOLE, WHOLE],
        out_specs=[WHOLE, WHOLE, WHOLE, SCALARS],
        out_shape=[
            pltpu.VMEM((size, size), BF16),
            pltpu.VMEM(spread, BF16),
            pltpu.VMEM(joined, BF16),
            jax.ShapeDtypeStruct((plan.size,), jnp.int32),
        ],
        scratch_shapes=[
            pltpu.VMEM(spread, BF16),
            pltpu.VMEM(joined, BF16),
            pltpu.VMEM((factors, size, size), BF16),
        ],
        compiler_params=params(),
        name="own",
    )(columns, slot, d_all, b_all, amplitudes)


def finish_rows(begin, end, plan, scalars, joined_b, dressed, middle, out, ready, sems):
    blocks, width = joined_b.shape[:2]

    def leave(i):
        r = scalars[plan.order + i]
        return pltpu.make_async_copy(ready.at[r], out.at[aligned(r * width, width), :], sems.at[r])

    def left(i, carry):
        r = scalars[plan.order + i]
        mirrored = apply_left(r, joined_b, lambda q, r: scalars[plan.rows + q * blocks + r], middle)
        own = dressed[aligned(r * width, width), :].astype(F32)
        ready[r] = (own + mirrored.astype(BF16).astype(F32)).astype(BF16)
        leave(i).start()
        return carry

    def wait(i, carry):
        leave(i).wait()
        return carry

    lax.fori_loop(begin, end, left, 0)
    lax.fori_loop(begin, end, wait, 0)


def take_in(q, piece, first, plan, scalars, spread_d, middle, step):
    slot, blocks = scalars[plan.slot], 2 * spread_d.shape[1]
    for m in range(0, piece.shape[1], step):
        rows = min(step, piece.shape[1] - m)
        apply_right(
            lambda lane: piece[slot, m : m + rows, aligned(lane, LANES)],
            lambda q, s: scalars[plan.lanes + q * blocks + s],
            spread_d,
            q,
            middle,
            first + m,
            rows,
        )


def mirror_kernel(j, marks, plan, scalars, piece, spread_d, joined_b, dressed, *rest):
    middle, out, ready, sems = rest[-4:]

    for q in range(spread_d.shape[0]):
        take_in(q, piece, marks[j] * joined_b.shape[1], plan, scalars, spread_d, middle, piece.shape[1])
    begin, end = scalars[plan.begin + j], scalars[plan.begin + j + 1]
    finish_rows(begin, end, plan, scalars, joined_b, dressed, middle, out, ready, sems)


def mirror_piece(j, marks, plan, scalars, piece, spread_d, joined_b, dressed, state):
    size = dressed.shape[0]
    blocks, width = joined_b.shape[:2]
    kept = pltpu.VMEM((spread_d.shape[0], size, size), BF16)
    return pl.pallas_call(
        functools.partial(mirror_kernel, j, marks, plan),
        in_specs=[SCALARS] + [WHOLE] * 4 + [WHOLE, FAR][: len(state)],
        out_specs=[WHOLE, FAR],
        out_shape=[kept, jax.ShapeDtypeStruct((size, size), BF16)],
        scratch_shapes=[pltpu.VMEM((blocks, width, size), BF16), pltpu.SemaphoreType.DMA((blocks,))],
        input_output_aliases={5: 0, 6: 1} if state else {},
        compiler_params=params(),
        name="mirror",
    )(scalars, piece, spread_d, joined_b, dressed, *state)


def cuts(blocks):
    return [m * blocks // 16 for m in (0, 6, 12, 14, 15, 16)]


def later(arrays, *after):
    return lax.optimization_barrier((arrays, after))[0]


def shards(amplitudes, mirror_slot, d_values, d_cols, b_values, b_cols):
    pairs = lax.axis_size("pair")
    perm = [(i, (i + pairs // 2) % pairs) for i in range(pairs)]
    assert amplitudes.shape[0] == 1
    blocks, width = d_values.shape[1], d_values.shape[2]

    marks = cuts(blocks)
    plan = Plan(lax.axis_size("fac") * d_cols.shape[0], blocks, len(marks) - 1)
    amplitudes = pltpu.with_memory_space_constraint(amplitudes, pltpu.HBM)

    def send(j, after):
        lanes = [m * width for m in marks[j : j + 2]]
        return lax.ppermute(turn(later(amplitudes, after), lanes)[0], "pair", perm)

    def gather(array):
        return lax.all_gather(array, "fac", axis=0, tiled=True)

    head = turn(amplitudes, [m * width for m in marks[:2]])[0]
    pieces = [lax.ppermute(head, "pair", perm), send(1, head)]
    columns, d_values, b_values = later((jnp.stack([d_cols, b_cols], axis=1), d_values, b_values), head)
    columns = gather(columns)
    pieces.append(send(2, columns))
    d_all = gather(later(d_values, columns))
    pieces.append(send(3, d_all))
    b_all = gather(later(b_values, d_all))
    pieces.append(send(4, b_all))
    dressed, spread_d, joined_b, scalars = own_pair(marks, plan, columns, mirror_slot, d_all, b_all, amplitudes)

    state = ()
    for j, piece in enumerate(pieces):
        state = mirror_piece(j, marks, plan, scalars, piece, spread_d, joined_b, dressed, state)
    return state[1][None]


def solution(mesh):
    placed = (
        P(("pair", "fac"), None, None),
        P(("pair", "fac")),
        P("fac", None, None, None),
        P("fac", None),
        P("fac", None, None, None),
        P("fac", None),
    )
    return jax.shard_map(
        shards,
        mesh=mesh,
        in_specs=placed,
        out_specs=P(("pair", "fac"), None, None),
        check_vma=False,
    )
```

time: 204 us -> 99.9 us (0.49)
  local copies, waits for them, and re-layouts: 60.7 us -> 0.03 us
  waiting for transfers between devices: 81.2 us -> 22.6 us
  Pallas kernels: 0 us -> 40.6 us
  matrix products: 15.8 us -> 0 us
  other arithmetic: 9.17 us -> 0.01 us
  starting transfers between devices: 2.64 us -> 10.2 us
  blocking collectives: 32.3 us -> 25 us
    ppermute x1 -> x5, waiting for transfers between devices: 81.2 us -> 22.6 us  [the longest x4 14.4 us: send(): return lax.ppermute(turn(later(amplitudes, after), lanes)[0], 'pair', perm)]
    pallas_call x0 -> x11, Pallas kernels: none -> 40.6 us  [the longest x1 18.8 us: own_pair(): pl.pallas_call(functools.partial(own_kernel, marks, plan), in_specs=[SCAL...]
    transpose x2 -> x0, local copies, waits for them, and re-layouts: 40.5 us -> none  [pick_columns(): return jnp.take(columns, index, axis=2)]
    dot_general x2 -> x0, matrix products: 15.8 us -> none  [the longest x1 9 us: dress_pairs(): jnp.einsum('frab,pfrbv->pfrav', d_block, picked, preferred_element_type=j...]
    gather x3 -> x0, local copies, waits for them, and re-layouts: 14.8 us -> none  [the longest x2 9.3 us: pick_columns(): return jnp.take(columns, index, axis=2)]
    convert_element_type x2 -> x0, other arithmetic: 9.14 us -> none  [the longest x1 4.96 us: shards(): return result.astype(jnp.bfloat16)]
    ppermute x1 -> x5, starting transfers between devices: 2.64 us -> 10.2 us  [the longest x4 6.1 us: send(): return lax.ppermute(turn(later(amplitudes, after), lanes)[0], 'pair', perm)]
    all_gather x4 -> x3, blocking collectives: 32.3 us -> 25 us  [gather(): return lax.all_gather(array, 'fac', axis=0, tiled=True)]
  transfers between devices with their start and end apart: 1 -> 5, of which waited for: 1 -> 4; matrix products, arithmetic and copies ran while one was open for 5% -> 0% of each run, Pallas kernels for 0% -> 37%
where the time goes in v2:
time: 99.9 us; the launch traced here: 99.2 us
  Pallas kernels  40.6 us (41%)
  blocking collectives  25 us (25%)
  waiting for transfers between devices  22.6 us (23%)
  starting transfers between devices  10.2 us (10%)
    all_gather x3, blocking collectives, gather(): return lax.all_gather(array, 'fac', axis=0, tiled=True)  25 us
    pallas_call x1, Pallas kernels, own_pair(): pl.pallas_call(functools.partial(own_kernel, marks, plan), in_specs=[SCAL...  18.8 us
    pallas_call x5, Pallas kernels, mirror_piece(): pl.pallas_call(functools.partial(mirror_kernel, j, marks, plan), in_specs...  15.9 us
    ppermute x4, waiting for transfers between devices, send(): return lax.ppermute(turn(later(amplitudes, after), lanes)[0], 'pair', perm)  14.4 us
    ppermute x1, waiting for transfers between devices, shards(): pieces = [lax.ppermute(head, 'pair', perm), send(1, head)]  8.11 us
    ppermute x4, starting transfers between devices, send(): return lax.ppermute(turn(later(amplitudes, after), lanes)[0], 'pair', perm)  6.1 us
    pallas_call x5, Pallas kernels, turn(): pl.pallas_call(functools.partial(turn_kernel, marks), in_specs=[FAR], out...  5.91 us
    ppermute x1, starting transfers between devices, shards(): pieces = [lax.ppermute(head, 'pair', perm), send(1, head)]  4.1 us
  transfers between devices with their start and end apart: 5, of which 4 were waited for; matrix products, arithmetic and copies ran while one was open for 0% of the time, Pallas kernels for 37%

profile of v2, /device:TPU:0, one launch (start us, length us, event | category | flops | bytes accessed | tf_op | source)
XLA Modules:
  0.0 99.2 jit_solution(10223924344431832401)
XLA Ops:
  0.0 1.3 %turn.5 = bf16[1,384,1024]{2,1,0:T(8,128)(2,1)S(1)} custom-call(bf16[1,1024,1024]{2,1,0:T(8,128)(2,1)} %source.7), custom_call_target="tpu_custom_call" | custom-call | tf_op jit(solution)/shard_map/turn/pallas_call | solution.py:50
  1.4 0.0 copy-start.2
  1.4 0.0 copy-start.3
  1.4 0.0 copy-start
  1.4 4.1 %collective-permute-start.4 = (bf16[1,384,1024]{2,1,0:T(8,128)(2,1)S(1)}, bf16[1,384,1024]{2,1,0:T(8,128)(2,1)S(1)}, u32[]{:S(2)}, u32[]{:S(2)}) collective-permute-start(bf16[1,384,1024]{2,1,0:T(8,128)(2,1)S(1)} %turn.5), channel_id=1, source_target_pairs={{0,16},{4,20},{8,24},{12,28},{16,0},{20,4},{24,8},{28,12},{1,17},{... | collective-permute-start | bytes 2359304 | tf_op jit(solution)/shard_map/ppermute | solution.py:290
  5.5 1.3 %turn.9 = bf16[1,384,1024]{2,1,0:T(8,128)(2,1)S(1)} custom-call(bf16[1,1024,1024]{2,1,0:T(8,128)(2,1)} %source.7), custom_call_target="tpu_custom_call" | custom-call | tf_op jit(solution)/shard_map/turn/pallas_call | solution.py:50
  6.8 0.1 collective-permute-start.3
  6.9 0.0 copy-done.2
  6.9 0.0 copy-done.3
  7.0 5.1 %all_gather.9.columns = s32[4,2,16]{2,1,0:T(2,128)S(1)} all-gather(s32[1,2,16]{2,1,0:T(2,128)S(1)} %pad_add_fusion), channel_id=1, replica_groups=mesh['pair'=8,'fac'=4] {'fac'}, dimensions={0}, use_global_device_ids=true | all-gather | bytes 640 | tf_op jit(solution)/shard_map/all_gather | solution.py:287
  12.0 1.1 %turn.8 = bf16[1,128,1024]{2,1,0:T(8,128)(2,1)S(1)} custom-call(bf16[1,1024,1024]{2,1,0:T(8,128)(2,1)} %source.7), custom_call_target="tpu_custom_call" | custom-call | tf_op jit(solution)/shard_map/turn/pallas_call | solution.py:50
  13.1 0.0 copy-start.1
  13.1 3.0 %collective-permute-start.2 = (bf16[1,128,1024]{2,1,0:T(8,128)(2,1)S(1)}, bf16[1,128,1024]{2,1,0:T(8,128)(2,1)S(1)}, u32[]{:S(2)}, u32[]{:S(2)}) collective-permute-start(bf16[1,128,1024]{2,1,0:T(8,128)(2,1)S(1)} %turn.8), channel_id=1, source_target_pairs={{0,16},{4,20},{8,24},{12,28},{16,0},{20,4},{24,8},{28,12},{1,17},{... | collective-permute-start | bytes 786440 | tf_op jit(solution)/shard_map/ppermute | solution.py:284
  16.1 0.0 copy-done
  16.1 10.0 %all_gather.10.d_all = bf16[4,16,64,64]{3,2,1,0:T(8,128)(2,1)S(1)} all-gather(bf16[1,16,64,64]{3,2,1,0:T(8,128)(2,1)S(1)} %copy-done), channel_id=1, replica_groups=mesh['pair'=8,'fac'=4] {'fac'}, dimensions={0}, use_global_device_ids=true | all-gather | bytes 655360 | tf_op jit(solution)/shard_map/all_gather | solution.py:287
  26.1 1.1 %turn.7 = bf16[1,64,1024]{2,1,0:T(8,128)(2,1)S(1)} custom-call(bf16[1,1024,1024]{2,1,0:T(8,128)(2,1)} %source.7), custom_call_target="tpu_custom_call" | custom-call | tf_op jit(solution)/shard_map/turn/pallas_call | solution.py:50
  27.2 0.4 collective-permute-start.1
  27.6 0.0 copy-done.1
  27.6 9.9 %all_gather.11.b_all = bf16[4,16,64,64]{3,2,1,0:T(8,128)(2,1)S(1)} all-gather(bf16[1,16,64,64]{3,2,1,0:T(8,128)(2,1)S(1)} %copy-done.1), channel_id=1, replica_groups=mesh['pair'=8,'fac'=4] {'fac'}, dimensions={0}, use_global_device_ids=true | all-gather | bytes 655360 | tf_op jit(solution)/shard_map/all_gather | solution.py:287
  37.5 1.1 %turn.6 = bf16[1,64,1024]{2,1,0:T(8,128)(2,1)S(1)} custom-call(bf16[1,1024,1024]{2,1,0:T(8,128)(2,1)} %source.7), custom_call_target="tpu_custom_call" | custom-call | tf_op jit(solution)/shard_map/turn/pallas_call | solution.py:50
  38.5 2.7 %collective-permute-start = (bf16[1,64,1024]{2,1,0:T(8,128)(2,1)S(1)}, bf16[1,64,1024]{2,1,0:T(8,128)(2,1)S(1)}, u32[]{:S(2)}, u32[]{:S(2)}) collective-permute-start(bf16[1,64,1024]{2,1,0:T(8,128)(2,1)S(1)} %turn.6), channel_id=1, source_target_pairs={{0,16},{4,20},{8,24},{12,28},{16,0},{20,4},{24,8},{28,12},{1,17},{... | collective-permute-start | bytes 393224 | tf_op jit(solution)/shard_map/ppermute | solution.py:284
  41.9 18.8 %own.1 = (bf16[1024,1024]{1,0:T(8,128)(2,1)S(1)}, bf16[4,8,256,128]{3,2,1,0:T(8,128)(2,1)S(1)}, bf16[16,64,256]{2,1,0:T(8,128)(2,1)S(1)}, s32[151]{0:T(256)S(1)}) custom-call(s32[4,2,16]{2,1,0:T(2,128)S(1)} %all_gather.9.columns, s32[1]{0:T(128)S(6)} %copy.23.slot, bf16[4,16,64,64]{3,2,1,0:T(8,128)(2,1)S(1)} %all_gather.10.d_all, ...), custom_call_target="tpu_custom_call" | custom-call | tf_op jit(solution)/shard_map/own/pallas_call | solution.py:181
  60.7 8.1 %collective-permute-done.4.piece = bf16[1,384,1024]{2,1,0:T(8,128)(2,1)S(1)} collective-permute-done((bf16[1,384,1024]{2,1,0:T(8,128)(2,1)S(1)}, bf16[1,384,1024]{2,1,0:T(8,128)(2,1)S(1)}, u32[]{:S(2)}, u32[]{:S(2)}) %collective-permute-start.4) | collective-permute-done | bytes 786464 | tf_op jit(solution)/shard_map/ppermute | solution.py:290
  68.8 3.5 %mirror.5 = (bf16[4,1024,1024]{2,1,0:T(8,128)(2,1)S(1)}, bf16[1024,1024]{1,0:T(8,128)(2,1)}) custom-call(s32[151]{0:T(256)S(1)} %get-tuple-element.32.scalars, bf16[1,384,1024]{2,1,0:T(8,128)(2,1)S(1)} %collective-permute-done.4.piece, bf16[4,8,256,128]{3,2,1,0:T(8,128)(2,1)S(1)} %get-tuple-element.34.spread_d, ...), custom_call_target="tpu_custom_call" | custom-call | tf_op jit(solution)/shard_map/mirror/pallas_call | solution.py:252
  72.3 13.4 %collective-permute-done.3.piece = bf16[1,384,1024]{2,1,0:T(8,128)(2,1)S(1)} collective-permute-done((bf16[1,384,1024]{2,1,0:T(8,128)(2,1)S(1)}, bf16[1,384,1024]{2,1,0:T(8,128)(2,1)S(1)}, u32[]{:S(2)}, u32[]{:S(2)}) %collective-permute-start.3) | collective-permute-done | bytes 786464 | tf_op jit(solution)/shard_map/ppermute | solution.py:284
  85.7 4.8 %mirror.6 = (bf16[4,1024,1024]{2,1,0:T(8,128)(2,1)S(1)}, bf16[1024,1024]{1,0:T(8,128)(2,1)}) custom-call(s32[151]{0:T(256)S(1)} %get-tuple-element.32.scalars, bf16[1,384,1024]{2,1,0:T(8,128)(2,1)S(1)} %collective-permute-done.3.piece, bf16[4,8,256,128]{3,2,1,0:T(8,128)(2,1)S(1)} %get-tuple-element.34.spread_d, ...), custom_call_target="tpu_custom_call", output_to_operand_aliasing={{0}: (5, {}), {1}: (6, {})} | custom-call | tf_op jit(solution)/shard_map/mirror/pallas_call | solution.py:252
  90.4 0.8 collective-permute-done.2.piece
  91.3 2.6 %mirror.7 = (bf16[4,1024,1024]{2,1,0:T(8,128)(2,1)S(1)}, bf16[1024,1024]{1,0:T(8,128)(2,1)}) custom-call(s32[151]{0:T(256)S(1)} %get-tuple-element.32.scalars, bf16[1,128,1024]{2,1,0:T(8,128)(2,1)S(1)} %collective-permute-done.2.piece, bf16[4,8,256,128]{3,2,1,0:T(8,128)(2,1)S(1)} %get-tuple-element.34.spread_d, ...), custom_call_target="tpu_custom_call", output_to_operand_aliasing={{0}: (5, {}), {1}: (6, {})} | custom-call | tf_op jit(solution)/shard_map/mirror/pallas_call | solution.py:252
  93.9 0.2 collective-permute-done.1.piece
  94.1 2.5 %mirror.8 = (bf16[4,1024,1024]{2,1,0:T(8,128)(2,1)S(1)}, bf16[1024,1024]{1,0:T(8,128)(2,1)}) custom-call(s32[151]{0:T(256)S(1)} %get-tuple-element.32.scalars, bf16[1,64,1024]{2,1,0:T(8,128)(2,1)S(1)} %collective-permute-done.1.piece, bf16[4,8,256,128]{3,2,1,0:T(8,128)(2,1)S(1)} %get-tuple-element.34.spread_d, ...), custom_call_target="tpu_custom_call", output_to_operand_aliasing={{0}: (5, {}), {1}: (6, {})} | custom-call | tf_op jit(solution)/shard_map/mirror/pallas_call | solution.py:252
  96.6 0.0 collective-permute-done.piece
  96.6 2.5 %mirror.9 = (bf16[4,1024,1024]{2,1,0:T(8,128)(2,1)S(1)}, bf16[1024,1024]{1,0:T(8,128)(2,1)}) custom-call(s32[151]{0:T(256)S(1)} %get-tuple-element.32.scalars, bf16[1,64,1024]{2,1,0:T(8,128)(2,1)S(1)} %collective-permute-done.piece, bf16[4,8,256,128]{3,2,1,0:T(8,128)(2,1)S(1)} %get-tuple-element.34.spread_d, ...), custom_call_target="tpu_custom_call", output_to_operand_aliasing={{0}: (5, {}), {1}: (6, {})} | custom-call | tf_op jit(solution)/shard_map/mirror/pallas_call | solution.py:252
  (1 shorter events, 0.0 us)
Async XLA Ops:
  1.4 5.6 %copy-start.2 = (s32[1,16]{1,0:T(1,128)S(1)}, s32[1,16]{1,0:T(1,128)}, u32[]{:S(2)}) copy-start(s32[1,16]{1,0:T(1,128)} %param.11) | copy-start | bytes 196
  1.4 5.6 %copy-start.3 = (s32[1,16]{1,0:T(1,128)S(1)}, s32[1,16]{1,0:T(1,128)}, u32[]{:S(2)}) copy-start(s32[1,16]{1,0:T(1,128)} %param.9) | copy-start | bytes 196
  1.4 14.7 %copy-start = (bf16[1,16,64,64]{3,2,1,0:T(8,128)(2,1)S(1)}, bf16[1,16,64,64]{3,2,1,0:T(8,128)(2,1)}, u32[]{:S(2)}) copy-start(bf16[1,16,64,64]{3,2,1,0:T(8,128)(2,1)} %param.8) | copy-start | bytes 393220
  1.4 67.4 %collective-permute-start.4 = (bf16[1,384,1024]{2,1,0:T(8,128)(2,1)S(1)}, bf16[1,384,1024]{2,1,0:T(8,128)(2,1)S(1)}, u32[]{:S(2)}, u32[]{:S(2)}) collective-permute-start(bf16[1,384,1024]{2,1,0:T(8,128)(2,1)S(1)} %turn.5), channel_id=1, source_target_pairs={{0,16},{4,20},{8,24},{12,28},{16,0},{20,4},{24,8},{28,12},{1,17},{... | collective-permute-start | bytes 2359304 | tf_op jit(solution)/shard_map/ppermute | solution.py:290
  6.8 78.8 %collective-permute-start.3 = (bf16[1,384,1024]{2,1,0:T(8,128)(2,1)S(1)}, bf16[1,384,1024]{2,1,0:T(8,128)(2,1)S(1)}, u32[]{:S(2)}, u32[]{:S(2)}) collective-permute-start(bf16[1,384,1024]{2,1,0:T(8,128)(2,1)S(1)} %turn.9), channel_id=1, source_target_pairs={{0,16},{4,20},{8,24},{12,28},{16,0},{20,4},{24,8},{28,12},{1,17},{... | collective-permute-start | bytes 2359304 | tf_op jit(solution)/shard_map/ppermute | solution.py:284
  13.1 14.5 %copy-start.1 = (bf16[1,16,64,64]{3,2,1,0:T(8,128)(2,1)S(1)}, bf16[1,16,64,64]{3,2,1,0:T(8,128)(2,1)}, u32[]{:S(2)}) copy-start(bf16[1,16,64,64]{3,2,1,0:T(8,128)(2,1)} %param.10) | copy-start | bytes 393220
  13.1 78.1 %collective-permute-start.2 = (bf16[1,128,1024]{2,1,0:T(8,128)(2,1)S(1)}, bf16[1,128,1024]{2,1,0:T(8,128)(2,1)S(1)}, u32[]{:S(2)}, u32[]{:S(2)}) collective-permute-start(bf16[1,128,1024]{2,1,0:T(8,128)(2,1)S(1)} %turn.8), channel_id=1, source_target_pairs={{0,16},{4,20},{8,24},{12,28},{16,0},{20,4},{24,8},{28,12},{1,17},{... | collective-permute-start | bytes 786440 | tf_op jit(solution)/shard_map/ppermute | solution.py:284
  27.2 66.9 %collective-permute-start.1 = (bf16[1,64,1024]{2,1,0:T(8,128)(2,1)S(1)}, bf16[1,64,1024]{2,1,0:T(8,128)(2,1)S(1)}, u32[]{:S(2)}, u32[]{:S(2)}) collective-permute-start(bf16[1,64,1024]{2,1,0:T(8,128)(2,1)S(1)} %turn.7), channel_id=1, source_target_pairs={{0,16},{4,20},{8,24},{12,28},{16,0},{20,4},{24,8},{28,12},{1,17},{... | collective-permute-start | bytes 393224 | tf_op jit(solution)/shard_map/ppermute | solution.py:284
  38.5 58.1 %collective-permute-start = (bf16[1,64,1024]{2,1,0:T(8,128)(2,1)S(1)}, bf16[1,64,1024]{2,1,0:T(8,128)(2,1)S(1)}, u32[]{:S(2)}, u32[]{:S(2)}) collective-permute-start(bf16[1,64,1024]{2,1,0:T(8,128)(2,1)S(1)} %turn.6), channel_id=1, source_target_pairs={{0,16},{4,20},{8,24},{12,28},{16,0},{20,4},{24,8},{28,12},{1,17},{... | collective-permute-start | bytes 393224 | tf_op jit(solution)/shard_map/ppermute | solution.py:284

commit v3 on v2

--- a/solution.py
+++ b/solution.py
@@ -58,6 +58,57 @@
     )(amplitudes)
 
 
+def pick_kernel(marks, columns, turned, place, *rest):
+    pieces, order, tally = rest[:-2], rest[-2], rest[-1]
+    factors, blocks = columns.shape[0], columns.shape[2]
+    fixed, width = marks[1], turned.shape[1] // (blocks - marks[1])
+
+    def clear(c, carry):
+        tally[c] = 0
+        place[c] = c
+        return carry
+
+    def count(r, carry):
+        for q in range(factors):
+            c = columns[q, 1, r]
+            tally[c] = tally[c] + 1
+        return carry
+
+    def select(at, carry):
+        def better(c, best):
+            wins = tally[c] > best[0]
+            return jnp.where(wins, tally[c], best[0]), jnp.where(wins, c, best[1])
+
+        c = lax.fori_loop(fixed, blocks, better, (jnp.int32(-1), jnp.int32(fixed)))[1]
+        tally[c] = -2
+        place[c] = at
+        order[at] = c
+        return carry
+
+    lax.fori_loop(0, blocks, clear, 0)
+    lax.fori_loop(0, blocks, count, 0)
+    lax.fori_loop(fixed, blocks, select, 0)
+    for lo, hi, piece in zip(marks[1:], marks[2:], pieces):
+        for at in range(lo, hi):
+            source = aligned((order[at] - fixed) * width, width)
+            piece[0, (at - lo) * width : (at - lo + 1) * width, :] = turned[0, source, :]
+
+
+def pick(marks, columns, turned):
+    blocks, size = columns.shape[2], turned.shape[2]
+    rows = [(hi - lo) * turned.shape[1] // (blocks - marks[1]) for lo, hi in zip(marks[1:], marks[2:])]
+    return pl.pallas_call(
+        functools.partial(pick_kernel, marks),
+        in_specs=[SCALARS, WHOLE],
+        out_specs=[SCALARS] + [WHOLE] * len(rows),
+        out_shape=[jax.ShapeDtypeStruct((blocks,), jnp.int32)]
+        + [jax.ShapeDtypeStruct((1, n, size), BF16) for n in rows],
+        scratch_shapes=[pltpu.SMEM((blocks,), jnp.int32), pltpu.SMEM((blocks,), jnp.int32)],
+        compiler_params=params(),
+        name="pick",
+    )(columns, turned)
+
+
 def spread_right(values, columns, side, spread):
     factors, blocks, width = values.shape[:3]
     spread[...] = jnp.zeros(spread.shape, BF16)
@@ -105,46 +156,67 @@
         self.order = 2 * factors * blocks
         self.begin = self.order + blocks
         self.slot = self.begin + pieces + 1
-        self.size = self.slot + 1
-
-
-def make_plan(marks, plan, columns, slot, scalars):
+        self.uses = self.slot + 1
+        self.size = self.uses + pieces * factors
+
+
+def make_plan(marks, plan, columns, place, slot, scalars):
     factors, blocks = columns.shape[0], columns.shape[2]
-
-    def offsets(s, carry):
+    spans = list(zip(marks, marks[1:]))
+
+    def offsets(s, uses):
         for q in range(factors):
+            at = place[columns[q, 1, s]]
             scalars[plan.lanes + q * blocks + s] = columns[q, 0, s] // 2 * LANES
-            scalars[plan.rows + q * blocks + s] = columns[q, 1, s] * (LANES // 2)
-        return carry
-
-    lax.fori_loop(0, blocks, offsets, 0)
-    place = jnp.int32(0)
-    for j, (lo, hi) in enumerate(zip(marks, marks[1:])):
-        scalars[plan.begin + j] = place
-
-        def one(r, place, lo=lo, hi=hi):
-            last = columns[0, 1, r]
+            scalars[plan.rows + q * blocks + s] = at * (LANES // 2)
+            here = [jnp.logical_and(at >= lo, at < hi).astype(jnp.int32) for lo, hi in spans]
+            uses = [n + here[i - q * len(spans)] if i // len(spans) == q else n for i, n in enumerate(uses)]
+        return uses
+
+    uses = lax.fori_loop(0, blocks, offsets, [jnp.int32(0)] * (factors * len(spans)))
+    for i, n in enumerate(uses):
+        scalars[plan.uses + i] = n
+    found = jnp.int32(0)
+    for j, (lo, hi) in enumerate(spans):
+        scalars[plan.begin + j] = found
+
+        def one(r, found, lo=lo, hi=hi):
+            last = place[columns[0, 1, r]]
             for q in range(1, factors):
-                last = jnp.maximum(last, columns[q, 1, r])
+                last = jnp.maximum(last, place[columns[q, 1, r]])
             here = jnp.logical_and(last >= lo, last < hi)
 
             @pl.when(here)
             def _():
-                scalars[plan.order + place] = r
-
-            return place + here.astype(jnp.int32)
-
-        place = lax.fori_loop(0, blocks, one, place)
-    scalars[plan.begin + len(marks) - 1] = place
+                scalars[plan.order + found] = r
+
+            return found + here.astype(jnp.int32)
+
+        found = lax.fori_loop(0, blocks, one, found)
+    scalars[plan.begin + len(spans)] = found
     scalars[plan.slot] = slot[0]
 
 
 def own_kernel(
-    marks, plan, columns, slot, d_all, b_all, source, dressed, spread_d, joined_b, scalars, spread_b, joined_d, middle
+    marks,
+    plan,
+    columns,
+    place,
+    slot,
+    d_all,
+    b_all,
+    source,
+    dressed,
+    spread_d,
+    joined_b,
+    scalars,
+    spread_b,
+    joined_d,
+    middle,
 ):
     factors, blocks, width = d_all.shape[:3]
     size = source.shape[1]
-    make_plan(marks, plan, columns, slot, scalars)
+    make_plan(marks, plan, columns, place, slot, scalars)
     spread_right(b_all, columns, 1, spread_b)
     join_left(d_all, joined_d)
     spread_right(d_all, columns, 0, spread_d)
@@ -173,14 +245,14 @@
     lax.fori_loop(0, blocks, left, 0)
 
 
-def own_pair(marks, plan, columns, slot, d_all, b_all, amplitudes):
+def own_pair(marks, plan, columns, place, slot, d_all, b_all, amplitudes):
     factors, blocks, width = d_all.shape[:3]
     size = amplitudes.shape[1]
     spread = (factors, blocks // 2, 2 * LANES, LANES)
     joined = (blocks, width, factors * width)
     return pl.pallas_call(
         functools.partial(own_kernel, marks, plan),
-        in_specs=[SCALARS, SCALARS, WHOLE, WHOLE, WHOLE],
+        in_specs=[SCALARS, SCALARS, SCALARS, WHOLE, WHOLE, WHOLE],
         out_specs=[WHOLE, WHOLE, WHOLE, SCALARS],
         out_shape=[
             pltpu.VMEM((size, size), BF16),
@@ -195,7 +267,7 @@
         ],
         compiler_params=params(),
         name="own",
-    )(columns, slot, d_all, b_all, amplitudes)
+    )(columns, place, slot, d_all, b_all, amplitudes)
 
 
 def finish_rows(begin, end, plan, scalars, joined_b, dressed, middle, out, ready, sems):
@@ -239,8 +311,13 @@
 def mirror_kernel(j, marks, plan, scalars, piece, spread_d, joined_b, dressed, *rest):
     middle, out, ready, sems = rest[-4:]
 
-    for q in range(spread_d.shape[0]):
-        take_in(q, piece, marks[j] * joined_b.shape[1], plan, scalars, spread_d, middle, piece.shape[1])
+    factors, width = spread_d.shape[0], joined_b.shape[1]
+    for q in range(factors):
+
+        @pl.when(scalars[plan.uses + q * (len(marks) - 1) + j] > 0)
+        def _(q=q):
+            take_in(q, piece, marks[j] * width, plan, scalars, spread_d, middle, piece.shape[1])
+
     begin, end = scalars[plan.begin + j], scalars[plan.begin + j + 1]
     finish_rows(begin, end, plan, scalars, joined_b, dressed, middle, out, ready, sems)
 
@@ -279,23 +356,26 @@
     plan = Plan(lax.axis_size("fac") * d_cols.shape[0], blocks, len(marks) - 1)
     amplitudes = pltpu.with_memory_space_constraint(amplitudes, pltpu.HBM)
 
-    def send(j, after):
-        lanes = [m * width for m in marks[j : j + 2]]
-        return lax.ppermute(turn(later(amplitudes, after), lanes)[0], "pair", perm)
+    def send(piece):
+        return lax.ppermute(piece, "pair", perm)
 
     def gather(array):
         return lax.all_gather(array, "fac", axis=0, tiled=True)
 
-    head = turn(amplitudes, [m * width for m in marks[:2]])[0]
-    pieces = [lax.ppermute(head, "pair", perm), send(1, head)]
-    columns, d_values, b_values = later((jnp.stack([d_cols, b_cols], axis=1), d_values, b_values), head)
-    columns = gather(columns)
-    pieces.append(send(2, columns))
-    d_all = gather(later(d_values, columns))
-    pieces.append(send(3, d_all))
+    lanes = [m * width for m in marks]
+    head = turn(amplitudes, lanes[:2])[0]
+    pieces = [send(head)]
+    rest = turn(later(amplitudes, head), [lanes[1], lanes[-1]])[0]
+    columns = gather(later(jnp.stack([d_cols, b_cols], axis=1), rest))
+    place, *picked = pick(marks, columns, rest)
+    pieces.append(send(picked[0]))
+    d_all = gather(later(d_values, picked))
+    pieces.append(send(later(picked[1], d_all)))
     b_all = gather(later(b_values, d_all))
-    pieces.append(send(4, b_all))
-    dressed, spread_d, joined_b, scalars = own_pair(marks, plan, columns, mirror_slot, d_all, b_all, amplitudes)
+    pieces.append(send(later(picked[2], b_all)))
+    own = own_pair(marks, plan, columns, place, mirror_slot, d_all, b_all, amplitudes)
+    dressed, spread_d, joined_b, scalars = own
+    pieces.append(send(later(picked[3], dressed)))
 
     state = ()
     for j, piece in enumerate(pieces):

time: 99.9 us -> 98.6 us (0.987)
  waiting for transfers between devices: 22.6 us -> 20.9 us
  Pallas kernels: 40.6 us -> 41.9 us
    pallas_call x5 -> x2, Pallas kernels: 5.91 us -> 2.95 us  [turn(): pl.pallas_call(functools.partial(turn_kernel, marks), in_specs=[FAR], out...]
    pallas_call x0 -> x1, Pallas kernels: none -> 2.8 us  [pick(): pl.pallas_call(functools.partial(pick_kernel, marks), in_specs=[SCALARS,...]
    ppermute x5, waiting for transfers between devices: 22.6 us -> 20.9 us  [send(): return lax.ppermute(piece, 'pair', perm)]
    pallas_call x1, Pallas kernels: 18.8 us -> 20 us  [own_pair(): pl.pallas_call(functools.partial(own_kernel, marks, plan), in_specs=[SCAL...]
  transfers between devices with their start and end apart: 5 -> 5, of which waited for: 4 -> 2; matrix products, arithmetic and copies ran while one was open for 0% -> 0% of each run, Pallas kernels for 37% -> 39%
where the time goes in v3:
time: 98.6 us; the launch traced here: 98.8 us
  Pallas kernels  41.9 us (42%)
  blocking collectives  25.4 us (26%)
  waiting for transfers between devices  20.9 us (21%)
  starting transfers between devices  9.76 us (10%)
    all_gather x3, blocking collectives, gather(): return lax.all_gather(array, 'fac', axis=0, tiled=True)  25.4 us
    ppermute x5, waiting for transfers between devices, send(): return lax.ppermute(piece, 'pair', perm)  20.9 us
    pallas_call x1, Pallas kernels, own_pair(): pl.pallas_call(functools.partial(own_kernel, marks, plan), in_specs=[SCAL...  20 us
    pallas_call x5, Pallas kernels, mirror_piece(): pl.pallas_call(functools.partial(mirror_kernel, j, marks, plan), in_specs...  16.2 us
    ppermute x5, starting transfers between devices, send(): return lax.ppermute(piece, 'pair', perm)  9.76 us
    pallas_call x2, Pallas kernels, turn(): pl.pallas_call(functools.partial(turn_kernel, marks), in_specs=[FAR], out...  2.95 us
    pallas_call x1, Pallas kernels, pick(): pl.pallas_call(functools.partial(pick_kernel, marks), in_specs=[SCALARS,...  2.8 us
  transfers between devices with their start and end apart: 5, of which 2 were waited for; matrix products, arithmetic and copies ran while one was open for 0% of the time, Pallas kernels for 39%

profile of v3, /device:TPU:0, one launch (start us, length us, event | category | flops | bytes accessed | tf_op | source)
XLA Modules:
  0.0 98.8 jit_solution(6641503338426361188)
XLA Ops:
  0.0 1.3 %turn.2 = bf16[1,384,1024]{2,1,0:T(8,128)(2,1)S(1)} custom-call(bf16[1,1024,1024]{2,1,0:T(8,128)(2,1)} %source.4), custom_call_target="tpu_custom_call" | custom-call | tf_op jit(solution)/shard_map/turn/pallas_call | solution.py:50
  1.4 0.0 copy-start.2
  1.4 0.0 copy-start.3
  1.4 0.0 copy-start
  1.4 4.1 %collective-permute-start.4 = (bf16[1,384,1024]{2,1,0:T(8,128)(2,1)S(1)}, bf16[1,384,1024]{2,1,0:T(8,128)(2,1)S(1)}, u32[]{:S(2)}, u32[]{:S(2)}) collective-permute-start(bf16[1,384,1024]{2,1,0:T(8,128)(2,1)S(1)} %turn.2), channel_id=1, source_target_pairs={{0,16},{4,20},{8,24},{12,28},{16,0},{20,4},{24,8},{28,12},{1,17},{... | collective-permute-start | bytes 2359304 | tf_op jit(solution)/shard_map/ppermute | solution.py:360
  5.5 1.6 %turn.3.turned = bf16[1,640,1024]{2,1,0:T(8,128)(2,1)S(1)} custom-call(bf16[1,1024,1024]{2,1,0:T(8,128)(2,1)} %source.4), custom_call_target="tpu_custom_call" | custom-call | tf_op jit(solution)/shard_map/turn/pallas_call | solution.py:50
  7.1 0.0 copy-start.1
  7.1 0.0 copy-done.2
  7.1 0.0 copy-done.3
  7.2 5.2 %all_gather.9.columns = s32[4,2,16]{2,1,0:T(2,128)S(1)} all-gather(s32[1,2,16]{2,1,0:T(2,128)S(1)} %pad_add_fusion), channel_id=1, replica_groups=mesh['pair'=8,'fac'=4] {'fac'}, dimensions={0}, use_global_device_ids=true | all-gather | bytes 640 | tf_op jit(solution)/shard_map/all_gather | solution.py:363
  12.4 2.8 %pick.1 = (s32[16]{0:T(128)S(1)}, bf16[1,384,1024]{2,1,0:T(8,128)(2,1)S(1)}, bf16[1,128,1024]{2,1,0:T(8,128)(2,1)S(1)}, bf16[1,64,1024]{2,1,0:T(8,128)(2,1)S(1)}, bf16[1,64,1024]{2,1,0:T(8,128)(2,1)S(1)}) custom-call(s32[4,2,16]{2,1,0:T(2,128)S(1)} %all_gather.9.columns, bf16[1,640,1024]{2,1,0:T(8,128)(2,1)S(1)} %turn.3.turned), custom_call_target="tpu_custom_call" | custom-call | tf_op jit(solution)/shard_map/pick/pallas_call | solution.py:100
  15.2 0.1 collective-permute-start.3
  15.2 0.0 copy-done
  15.3 10.4 %all_gather.10.d_all = bf16[4,16,64,64]{3,2,1,0:T(8,128)(2,1)S(1)} all-gather(bf16[1,16,64,64]{3,2,1,0:T(8,128)(2,1)S(1)} %copy-done), channel_id=1, replica_groups=mesh['pair'=8,'fac'=4] {'fac'}, dimensions={0}, use_global_device_ids=true | all-gather | bytes 655360 | tf_op jit(solution)/shard_map/all_gather | solution.py:363
  25.6 2.6 %collective-permute-start.2 = (bf16[1,128,1024]{2,1,0:T(8,128)(2,1)S(1)}, bf16[1,128,1024]{2,1,0:T(8,128)(2,1)S(1)}, u32[]{:S(2)}, u32[]{:S(2)}) collective-permute-start(bf16[1,128,1024]{2,1,0:T(8,128)(2,1)S(1)} %get-tuple-element.45), channel_id=1, source_target_pairs={{0,16},{4,20},{8,24},{12,28},{16,0},{20,4},{24,8},{28,12},{1,17},{... | collective-permute-start | bytes 786440 | tf_op jit(solution)/shard_map/ppermute | solution.py:360
  28.2 0.0 copy-done.1
  28.2 9.9 %all_gather.11.b_all = bf16[4,16,64,64]{3,2,1,0:T(8,128)(2,1)S(1)} all-gather(bf16[1,16,64,64]{3,2,1,0:T(8,128)(2,1)S(1)} %copy-done.1), channel_id=1, replica_groups=mesh['pair'=8,'fac'=4] {'fac'}, dimensions={0}, use_global_device_ids=true | all-gather | bytes 655360 | tf_op jit(solution)/shard_map/all_gather | solution.py:363
  38.1 0.3 collective-permute-start.1
  39.0 20.0 %own.1 = (bf16[1024,1024]{1,0:T(8,128)(2,1)S(1)}, bf16[4,8,256,128]{3,2,1,0:T(8,128)(2,1)S(1)}, bf16[16,64,256]{2,1,0:T(8,128)(2,1)S(1)}, s32[171]{0:T(256)S(1)}) custom-call(s32[4,2,16]{2,1,0:T(2,128)S(1)} %all_gather.9.columns, s32[16]{0:T(128)S(1)} %get-tuple-element.32.place, s32[1]{0:T(128)S(6)} %copy.23.slot, ...), custom_call_target="tpu_custom_call" | custom-call | tf_op jit(solution)/shard_map/own/pallas_call | solution.py:253
  59.0 2.7 %collective-permute-start = (bf16[1,64,1024]{2,1,0:T(8,128)(2,1)S(1)}, bf16[1,64,1024]{2,1,0:T(8,128)(2,1)S(1)}, u32[]{:S(2)}, u32[]{:S(2)}) collective-permute-start(bf16[1,64,1024]{2,1,0:T(8,128)(2,1)S(1)} %get-tuple-element.41), channel_id=1, source_target_pairs={{0,16},{4,20},{8,24},{12,28},{16,0},{20,4},{24,8},{28,12},{1,17},{... | collective-permute-start | bytes 393224 | tf_op jit(solution)/shard_map/ppermute | solution.py:360
  61.7 7.1 %collective-permute-done.4.piece = bf16[1,384,1024]{2,1,0:T(8,128)(2,1)S(1)} collective-permute-done((bf16[1,384,1024]{2,1,0:T(8,128)(2,1)S(1)}, bf16[1,384,1024]{2,1,0:T(8,128)(2,1)S(1)}, u32[]{:S(2)}, u32[]{:S(2)}) %collective-permute-start.4) | collective-permute-done | bytes 786464 | tf_op jit(solution)/shard_map/ppermute | solution.py:360
  68.8 3.1 %mirror.5 = (bf16[4,1024,1024]{2,1,0:T(8,128)(2,1)S(1)}, bf16[1024,1024]{1,0:T(8,128)(2,1)}) custom-call(s32[171]{0:T(256)S(1)} %get-tuple-element.39.scalars, bf16[1,384,1024]{2,1,0:T(8,128)(2,1)S(1)} %collective-permute-done.4.piece, bf16[4,8,256,128]{3,2,1,0:T(8,128)(2,1)S(1)} %get-tuple-element.42.spread_d, ...), custom_call_target="tpu_custom_call" | custom-call | tf_op jit(solution)/shard_map/mirror/pallas_call | solution.py:329
  71.9 13.7 %collective-permute-done.3.piece = bf16[1,384,1024]{2,1,0:T(8,128)(2,1)S(1)} collective-permute-done((bf16[1,384,1024]{2,1,0:T(8,128)(2,1)S(1)}, bf16[1,384,1024]{2,1,0:T(8,128)(2,1)S(1)}, u32[]{:S(2)}, u32[]{:S(2)}) %collective-permute-start.3) | collective-permute-done | bytes 786464 | tf_op jit(solution)/shard_map/ppermute | solution.py:360
  85.7 5.7 %mirror.6 = (bf16[4,1024,1024]{2,1,0:T(8,128)(2,1)S(1)}, bf16[1024,1024]{1,0:T(8,128)(2,1)}) custom-call(s32[171]{0:T(256)S(1)} %get-tuple-element.39.scalars, bf16[1,384,1024]{2,1,0:T(8,128)(2,1)S(1)} %collective-permute-done.3.piece, bf16[4,8,256,128]{3,2,1,0:T(8,128)(2,1)S(1)} %get-tuple-element.42.spread_d, ...), custom_call_target="tpu_custom_call", output_to_operand_aliasing={{0}: (5, {}), {1}: (6, {})} | custom-call | tf_op jit(solution)/shard_map/mirror/pallas_call | solution.py:329
  91.4 0.0 collective-permute-done.2.piece
  91.4 3.5 %mirror.7 = (bf16[4,1024,1024]{2,1,0:T(8,128)(2,1)S(1)}, bf16[1024,1024]{1,0:T(8,128)(2,1)}) custom-call(s32[171]{0:T(256)S(1)} %get-tuple-element.39.scalars, bf16[1,128,1024]{2,1,0:T(8,128)(2,1)S(1)} %collective-permute-done.2.piece, bf16[4,8,256,128]{3,2,1,0:T(8,128)(2,1)S(1)} %get-tuple-element.42.spread_d, ...), custom_call_target="tpu_custom_call", output_to_operand_aliasing={{0}: (5, {}), {1}: (6, {})} | custom-call | tf_op jit(solution)/shard_map/mirror/pallas_call | solution.py:329
  94.9 0.0 collective-permute-done.1.piece
  94.9 2.1 %mirror.8 = (bf16[4,1024,1024]{2,1,0:T(8,128)(2,1)S(1)}, bf16[1024,1024]{1,0:T(8,128)(2,1)}) custom-call(s32[171]{0:T(256)S(1)} %get-tuple-element.39.scalars, bf16[1,64,1024]{2,1,0:T(8,128)(2,1)S(1)} %collective-permute-done.1.piece, bf16[4,8,256,128]{3,2,1,0:T(8,128)(2,1)S(1)} %get-tuple-element.42.spread_d, ...), custom_call_target="tpu_custom_call", output_to_operand_aliasing={{0}: (5, {}), {1}: (6, {})} | custom-call | tf_op jit(solution)/shard_map/mirror/pallas_call | solution.py:329
  96.9 0.0 collective-permute-done.piece
  96.9 1.8 %mirror.9 = (bf16[4,1024,1024]{2,1,0:T(8,128)(2,1)S(1)}, bf16[1024,1024]{1,0:T(8,128)(2,1)}) custom-call(s32[171]{0:T(256)S(1)} %get-tuple-element.39.scalars, bf16[1,64,1024]{2,1,0:T(8,128)(2,1)S(1)} %collective-permute-done.piece, bf16[4,8,256,128]{3,2,1,0:T(8,128)(2,1)S(1)} %get-tuple-element.42.spread_d, ...), custom_call_target="tpu_custom_call", output_to_operand_aliasing={{0}: (5, {}), {1}: (6, {})} | custom-call | tf_op jit(solution)/shard_map/mirror/pallas_call | solution.py:329
  (1 shorter events, 0.0 us)
Async XLA Ops:
  1.4 5.8 %copy-start.2 = (s32[1,16]{1,0:T(1,128)S(1)}, s32[1,16]{1,0:T(1,128)}, u32[]{:S(2)}) copy-start(s32[1,16]{1,0:T(1,128)} %param.11) | copy-start | bytes 196
  1.4 5.8 %copy-start.3 = (s32[1,16]{1,0:T(1,128)S(1)}, s32[1,16]{1,0:T(1,128)}, u32[]{:S(2)}) copy-start(s32[1,16]{1,0:T(1,128)} %param.9) | copy-start | bytes 196
  1.4 13.9 %copy-start = (bf16[1,16,64,64]{3,2,1,0:T(8,128)(2,1)S(1)}, bf16[1,16,64,64]{3,2,1,0:T(8,128)(2,1)}, u32[]{:S(2)}) copy-start(bf16[1,16,64,64]{3,2,1,0:T(8,128)(2,1)} %param.8) | copy-start | bytes 393220
  1.4 67.4 %collective-permute-start.4 = (bf16[1,384,1024]{2,1,0:T(8,128)(2,1)S(1)}, bf16[1,384,1024]{2,1,0:T(8,128)(2,1)S(1)}, u32[]{:S(2)}, u32[]{:S(2)}) collective-permute-start(bf16[1,384,1024]{2,1,0:T(8,128)(2,1)S(1)} %turn.2), channel_id=1, source_target_pairs={{0,16},{4,20},{8,24},{12,28},{16,0},{20,4},{24,8},{28,12},{1,17},{... | collective-permute-start | bytes 2359304 | tf_op jit(solution)/shard_map/ppermute | solution.py:360
  7.1 21.1 %copy-start.1 = (bf16[1,16,64,64]{3,2,1,0:T(8,128)(2,1)S(1)}, bf16[1,16,64,64]{3,2,1,0:T(8,128)(2,1)}, u32[]{:S(2)}) copy-start(bf16[1,16,64,64]{3,2,1,0:T(8,128)(2,1)} %param.10) | copy-start | bytes 393220
  15.2 70.5 %collective-permute-start.3 = (bf16[1,384,1024]{2,1,0:T(8,128)(2,1)S(1)}, bf16[1,384,1024]{2,1,0:T(8,128)(2,1)S(1)}, u32[]{:S(2)}, u32[]{:S(2)}) collective-permute-start(bf16[1,384,1024]{2,1,0:T(8,128)(2,1)S(1)} %get-tuple-element.33), channel_id=1, source_target_pairs={{0,16},{4,20},{8,24},{12,28},{16,0},{20,4},{24,8},{28,12},{1,17},{... | collective-permute-start | bytes 2359304 | tf_op jit(solution)/shard_map/ppermute | solution.py:360
  25.6 65.8 %collective-permute-start.2 = (bf16[1,128,1024]{2,1,0:T(8,128)(2,1)S(1)}, bf16[1,128,1024]{2,1,0:T(8,128)(2,1)S(1)}, u32[]{:S(2)}, u32[]{:S(2)}) collective-permute-start(bf16[1,128,1024]{2,1,0:T(8,128)(2,1)S(1)} %get-tuple-element.45), channel_id=1, source_target_pairs={{0,16},{4,20},{8,24},{12,28},{16,0},{20,4},{24,8},{28,12},{1,17},{... | collective-permute-start | bytes 786440 | tf_op jit(solution)/shard_map/ppermute | solution.py:360
  38.1 56.8 %collective-permute-start.1 = (bf16[1,64,1024]{2,1,0:T(8,128)(2,1)S(1)}, bf16[1,64,1024]{2,1,0:T(8,128)(2,1)S(1)}, u32[]{:S(2)}, u32[]{:S(2)}) collective-permute-start(bf16[1,64,1024]{2,1,0:T(8,128)(2,1)S(1)} %get-tuple-element.44), channel_id=1, source_target_pairs={{0,16},{4,20},{8,24},{12,28},{16,0},{20,4},{24,8},{28,12},{1,17},{... | collective-permute-start | bytes 393224 | tf_op jit(solution)/shard_map/ppermute | solution.py:360
  59.0 37.9 %collective-permute-start = (bf16[1,64,1024]{2,1,0:T(8,128)(2,1)S(1)}, bf16[1,64,1024]{2,1,0:T(8,128)(2,1)S(1)}, u32[]{:S(2)}, u32[]{:S(2)}) collective-permute-start(bf16[1,64,1024]{2,1,0:T(8,128)(2,1)S(1)} %get-tuple-element.41), channel_id=1, source_target_pairs={{0,16},{4,20},{8,24},{12,28},{16,0},{20,4},{24,8},{28,12},{1,17},{... | collective-permute-start | bytes 393224 | tf_op jit(solution)/shard_map/ppermute | solution.py:360

commit v4 on v3

--- a/solution.py
+++ b/solution.py
@@ -58,55 +58,119 @@
     )(amplitudes)
 
 
-def pick_kernel(marks, columns, turned, place, *rest):
-    pieces, order, tally = rest[:-2], rest[-2], rest[-1]
+class Layout:
+    def __init__(self, blocks):
+        self.blocks = blocks
+        self.place = 0
+        self.used = blocks
+        self.slot = 2 * blocks + 1
+        self.block = self.slot + blocks * blocks
+        self.size = self.block + blocks * blocks
+
+
+def swap_halves(tile):
+    half = tile.shape[1] // 2
+    return jnp.concatenate([tile[:, half:], tile[:, :half]], axis=1)
+
+
+def join_halves(low, low_swapped, high, high_swapped):
+    low = jnp.where(low_swapped, swap_halves(low), low)
+    high = jnp.where(high_swapped, swap_halves(high), high)
+    lane = lax.broadcasted_iota(jnp.int32, low.shape, 1)
+    return jnp.where(lane < low.shape[1] // 2, low, high)
+
+
+def pack(start, piece, fixed, layout, scalars, turned):
+    blocks = layout.blocks
+    width = turned.shape[1] // (blocks - fixed)
+    tiles = piece.shape[2] // LANES
+    group = 4 if tiles % 4 == 0 else 2 if tiles % 2 == 0 else 1
+
+    def half(slot):
+        at = scalars[layout.block + slot]
+        row, k = at // blocks, at % blocks
+        return turned[0, aligned(row * width, width), aligned(k // 2 * LANES, LANES)], k % 2
+
+    def fill(i, carry):
+        for n in range(group):
+            tile = i * group + n
+            low, k_low = half(start + 2 * tile)
+            high, k_high = half(start + 2 * tile + 1)
+            piece[0, :, aligned(tile * LANES, LANES)] = join_halves(low, k_low == 1, high, k_high == 0)
+        return carry
+
+    lax.fori_loop(0, tiles // group, fill, 0)
+
+
+def pack_kernel(starts, fixed, layout, scalars, turned, *pieces):
+    for start, piece in zip(starts, pieces):
+        pack(start, piece, fixed, layout, scalars, turned)
+
+
+def pick_kernel(starts, fixed, layout, columns, turned, scalars, *rest):
+    pieces, tally = rest[:-1], rest[-1]
     factors, blocks = columns.shape[0], columns.shape[2]
-    fixed, width = marks[1], turned.shape[1] // (blocks - marks[1])
 
     def clear(c, carry):
         tally[c] = 0
-        place[c] = c
-        return carry
-
-    def count(r, carry):
+        scalars[layout.place + c] = c
+        scalars[layout.used + c] = 0
+        for k in range(blocks):
+            scalars[layout.block + c * blocks + k] = 0
+        return carry
+
+    def count(r, masks):
+        left, right = [], []
         for q in range(factors):
             c = columns[q, 1, r]
             tally[c] = tally[c] + 1
-        return carry
-
-    def select(at, carry):
+            left.append(masks[0][q] | jnp.left_shift(1, c))
+            right.append(masks[1][q] | jnp.left_shift(1, columns[q, 0, r]))
+        return left, right
+
+    lax.fori_loop(0, blocks, clear, 0)
+    none = [jnp.int32(0)] * factors
+    left, right = lax.fori_loop(0, blocks, count, (none, none))
+
+    def select(at, used):
         def better(c, best):
             wins = tally[c] > best[0]
             return jnp.where(wins, tally[c], best[0]), jnp.where(wins, c, best[1])
 
         c = lax.fori_loop(fixed, blocks, better, (jnp.int32(-1), jnp.int32(fixed)))[1]
         tally[c] = -2
-        place[c] = at
-        order[at] = c
-        return carry
-
-    lax.fori_loop(0, blocks, clear, 0)
-    lax.fori_loop(0, blocks, count, 0)
-    lax.fori_loop(fixed, blocks, select, 0)
-    for lo, hi, piece in zip(marks[1:], marks[2:], pieces):
-        for at in range(lo, hi):
-            source = aligned((order[at] - fixed) * width, width)
-            piece[0, (at - lo) * width : (at - lo + 1) * width, :] = turned[0, source, :]
-
-
-def pick(marks, columns, turned):
-    blocks, size = columns.shape[2], turned.shape[2]
-    rows = [(hi - lo) * turned.shape[1] // (blocks - marks[1]) for lo, hi in zip(marks[1:], marks[2:])]
+        scalars[layout.place + c] = at
+        scalars[layout.used + at] = used
+        read = jnp.int32(0)
+        for q in range(factors):
+            read = read | jnp.where(jnp.right_shift(left[q], c) & 1 == 1, right[q], 0)
+        for k in range(blocks):
+            bit = jnp.right_shift(read, k) & 1
+            scalars[layout.block + used] = (c - fixed) * blocks + k
+            scalars[layout.slot + at * blocks + k] = jnp.where(bit == 1, used, 0)
+            used = used + bit
+        return used
+
+    scalars[layout.used + blocks] = lax.fori_loop(fixed, blocks, select, jnp.int32(0))
+
+    pack_kernel(starts, fixed, layout, scalars, turned, *pieces)
+
+
+def pack_pieces(given, spans, fixed, layout, turned):
+    opening = given.ndim == 3
+    blocks = layout.blocks
+    width = turned.shape[1] // (blocks - fixed)
+    shapes = [jax.ShapeDtypeStruct((1, width, (hi - lo) * width), BF16) for lo, hi in spans]
+    kernel = functools.partial(pick_kernel if opening else pack_kernel, [lo for lo, _ in spans], fixed, layout)
     return pl.pallas_call(
-        functools.partial(pick_kernel, marks),
+        kernel,
         in_specs=[SCALARS, WHOLE],
-        out_specs=[SCALARS] + [WHOLE] * len(rows),
-        out_shape=[jax.ShapeDtypeStruct((blocks,), jnp.int32)]
-        + [jax.ShapeDtypeStruct((1, n, size), BF16) for n in rows],
-        scratch_shapes=[pltpu.SMEM((blocks,), jnp.int32), pltpu.SMEM((blocks,), jnp.int32)],
+        out_specs=[SCALARS] * opening + [WHOLE] * len(spans),
+        out_shape=[jax.ShapeDtypeStruct((layout.size,), jnp.int32)] * opening + shapes,
+        scratch_shapes=[pltpu.SMEM((blocks,), jnp.int32)] * opening,
         compiler_params=params(),
-        name="pick",
-    )(columns, turned)
+        name="pack",
+    )(given, turned)
 
 
 def spread_right(values, columns, side, spread):
@@ -153,38 +217,53 @@
         self.blocks = blocks
         self.lanes = 0
         self.rows = factors * blocks
-        self.order = 2 * factors * blocks
+        self.uses = 2 * factors * blocks
+        self.slot = 3 * factors * blocks
+        self.whole = self.slot + blocks * blocks
+        self.order = self.whole + pieces
         self.begin = self.order + blocks
-        self.slot = self.begin + pieces + 1
-        self.uses = self.slot + 1
-        self.size = self.uses + pieces * factors
-
-
-def make_plan(marks, plan, columns, place, slot, scalars):
+        self.mirror = self.begin + pieces + 1
+        self.size = self.mirror + 1
+
+
+def make_plan(fixed, ends, plan, layout, columns, packing, slot, scalars):
     factors, blocks = columns.shape[0], columns.shape[2]
-    spans = list(zip(marks, marks[1:]))
-
-    def offsets(s, uses):
+
+    def clear(i, carry):
+        scalars[plan.uses + i] = 0
+        return carry
+
+    def offsets(s, carry):
         for q in range(factors):
-            at = place[columns[q, 1, s]]
+            at = packing[layout.place + columns[q, 1, s]]
             scalars[plan.lanes + q * blocks + s] = columns[q, 0, s] // 2 * LANES
             scalars[plan.rows + q * blocks + s] = at * (LANES // 2)
-            here = [jnp.logical_and(at >= lo, at < hi).astype(jnp.int32) for lo, hi in spans]
-            uses = [n + here[i - q * len(spans)] if i // len(spans) == q else n for i, n in enumerate(uses)]
-        return uses
-
-    uses = lax.fori_loop(0, blocks, offsets, [jnp.int32(0)] * (factors * len(spans)))
-    for i, n in enumerate(uses):
-        scalars[plan.uses + i] = n
-    found = jnp.int32(0)
-    for j, (lo, hi) in enumerate(spans):
+            use = plan.uses + q * blocks + at
+            scalars[use] = scalars[use] + 1
+        return carry
+
+    def copy(i, carry):
+        scalars[plan.slot + i] = packing[layout.slot + i]
+        return carry
+
+    lax.fori_loop(0, factors * blocks, clear, 0)
+    lax.fori_loop(0, blocks, offsets, 0)
+    lax.fori_loop(fixed * blocks, blocks * blocks, copy, 0)
+    found, low = jnp.int32(0), jnp.int32(0)
+    for j, end in enumerate(ends):
+
+        def ready(at, n, end=end):
+            return n + (jnp.minimum(packing[layout.used + at + 1], ends[-1]) <= end).astype(jnp.int32)
+
+        high = lax.fori_loop(fixed, blocks, ready, jnp.int32(fixed)) if j else jnp.int32(fixed)
+        scalars[plan.whole + j] = high
         scalars[plan.begin + j] = found
 
-        def one(r, found, lo=lo, hi=hi):
-            last = place[columns[0, 1, r]]
+        def one(r, found, low=low, high=high):
+            last = packing[layout.place + columns[0, 1, r]]
             for q in range(1, factors):
-                last = jnp.maximum(last, place[columns[q, 1, r]])
-            here = jnp.logical_and(last >= lo, last < hi)
+                last = jnp.maximum(last, packing[layout.place + columns[q, 1, r]])
+            here = jnp.logical_and(last >= low, last < high)
 
             @pl.when(here)
             def _():
@@ -192,16 +271,18 @@
 
             return found + here.astype(jnp.int32)
 
-        found = lax.fori_loop(0, blocks, one, found)
-    scalars[plan.begin + len(spans)] = found
-    scalars[plan.slot] = slot[0]
+        found, low = lax.fori_loop(0, blocks, one, found), high
+    scalars[plan.begin + len(ends)] = found
+    scalars[plan.mirror] = slot[0]
 
 
 def own_kernel(
-    marks,
+    fixed,
+    ends,
     plan,
+    layout,
     columns,
-    place,
+    packing,
     slot,
     d_all,
     b_all,
@@ -216,7 +297,7 @@
 ):
     factors, blocks, width = d_all.shape[:3]
     size = source.shape[1]
-    make_plan(marks, plan, columns, place, slot, scalars)
+    make_plan(fixed, ends, plan, layout, columns, packing, slot, scalars)
     spread_right(b_all, columns, 1, spread_b)
     join_left(d_all, joined_d)
     spread_right(d_all, columns, 0, spread_d)
@@ -245,13 +326,13 @@
     lax.fori_loop(0, blocks, left, 0)
 
 
-def own_pair(marks, plan, columns, place, slot, d_all, b_all, amplitudes):
+def own_pair(fixed, ends, plan, layout, columns, packing, slot, d_all, b_all, amplitudes):
     factors, blocks, width = d_all.shape[:3]
     size = amplitudes.shape[1]
     spread = (factors, blocks // 2, 2 * LANES, LANES)
     joined = (blocks, width, factors * width)
     return pl.pallas_call(
-        functools.partial(own_kernel, marks, plan),
+        functools.partial(own_kernel, fixed, ends, plan, layout),
         in_specs=[SCALARS, SCALARS, SCALARS, WHOLE, WHOLE, WHOLE],
         out_specs=[WHOLE, WHOLE, WHOLE, SCALARS],
         out_shape=[
@@ -267,7 +348,7 @@
         ],
         compiler_params=params(),
         name="own",
-    )(columns, place, slot, d_all, b_all, amplitudes)
+    )(columns, packing, slot, d_all, b_all, amplitudes)
 
 
 def finish_rows(begin, end, plan, scalars, joined_b, dressed, middle, out, ready, sems):
@@ -293,53 +374,95 @@
     lax.fori_loop(begin, end, wait, 0)
 
 
-def take_in(q, piece, first, plan, scalars, spread_d, middle, step):
-    slot, blocks = scalars[plan.slot], 2 * spread_d.shape[1]
-    for m in range(0, piece.shape[1], step):
-        rows = min(step, piece.shape[1] - m)
+def opening_kernel(plan, scalars, piece, spread_d, joined_b, dressed, middle, packed, out, ready, sems):
+    slot, blocks = scalars[plan.mirror], joined_b.shape[0]
+    rows = piece.shape[1]
+    packed[...] = jnp.zeros(packed.shape, BF16)
+    for q in range(spread_d.shape[0]):
         apply_right(
-            lambda lane: piece[slot, m : m + rows, aligned(lane, LANES)],
+            lambda lane: piece[slot, :, aligned(lane, LANES)],
             lambda q, s: scalars[plan.lanes + q * blocks + s],
             spread_d,
             q,
             middle,
-            first + m,
+            0,
             rows,
         )
-
-
-def mirror_kernel(j, marks, plan, scalars, piece, spread_d, joined_b, dressed, *rest):
-    middle, out, ready, sems = rest[-4:]
-
-    factors, width = spread_d.shape[0], joined_b.shape[1]
-    for q in range(factors):
-
-        @pl.when(scalars[plan.uses + q * (len(marks) - 1) + j] > 0)
-        def _(q=q):
-            take_in(q, piece, marks[j] * width, plan, scalars, spread_d, middle, piece.shape[1])
-
+    end = scalars[plan.begin + 1]
+    finish_rows(0, end, plan, scalars, joined_b, dressed, middle, out, ready, sems)
+
+
+def packed_kernel(j, starts, plan, scalars, spread_d, joined_b, dressed, *rest):
+    pieces, rest = rest[: len(starts)], rest[len(starts) + 3 :]
+    middle, packed, out, row, ready, sems = rest
+    slot, factors = scalars[plan.mirror], spread_d.shape[0]
+    blocks, width = joined_b.shape[:2]
+    for start, piece in zip(starts, pieces):
+        for lane in range(0, piece.shape[2], LANES):
+            packed[:, start * width + lane : start * width + lane + LANES] = piece[slot, :, lane : lane + LANES]
+
+    fixed = scalars[plan.whole]
+    before, after = scalars[plan.whole + j - 1], scalars[plan.whole + j]
+
+    def take(i, carry):
+        first = jnp.maximum(jnp.minimum(before + 2 * i, after - 2), fixed)
+        for n in range(2):
+            for k in range(0, blocks, 2):
+                low, high = (scalars[plan.slot + (first + n) * blocks + k + i] for i in range(2))
+                tiles = [packed[:, aligned(slot // 2 * LANES, LANES)] for slot in (low, high)]
+                tile = join_halves(tiles[0], low % 2 == 1, tiles[1], high % 2 == 0)
+                row[n * width : (n + 1) * width, k * width : (k + 2) * width] = tile
+        for q in range(factors):
+            uses = plan.uses + q * blocks + first
+
+            @pl.when(scalars[uses] + scalars[uses + 1] > 0)
+            def _(q=q):
+                apply_right(
+                    lambda lane: row[:, aligned(lane, LANES)],
+                    lambda q, s: scalars[plan.lanes + q * blocks + s],
+                    spread_d,
+                    q,
+                    middle,
+                    pl.multiple_of(first * width, width),
+                    2 * width,
+                )
+
+        return carry
+
+    lax.fori_loop(0, (after - before + 1) // 2, take, 0)
     begin, end = scalars[plan.begin + j], scalars[plan.begin + j + 1]
     finish_rows(begin, end, plan, scalars, joined_b, dressed, middle, out, ready, sems)
 
 
-def mirror_piece(j, marks, plan, scalars, piece, spread_d, joined_b, dressed, state):
-    size = dressed.shape[0]
-    blocks, width = joined_b.shape[:2]
-    kept = pltpu.VMEM((spread_d.shape[0], size, size), BF16)
+def mirror_piece(j, starts, slots, plan, scalars, pieces, spread_d, joined_b, dressed, state):
+    size, (blocks, width) = dressed.shape[0], joined_b.shape[:2]
+    shapes = [
+        pltpu.VMEM((spread_d.shape[0], size, size), BF16),
+        pltpu.VMEM((width, slots * width), BF16),
+        jax.ShapeDtypeStruct((size, size), BF16),
+    ]
+    scratch = [pltpu.VMEM((blocks, width, size), BF16), pltpu.SemaphoreType.DMA((blocks,))]
+    if j == 0:
+        kernel, given = functools.partial(opening_kernel, plan), (scalars, *pieces, spread_d, joined_b, dressed)
+    else:
+        kernel, given = functools.partial(packed_kernel, j, starts, plan), (scalars, spread_d, joined_b, dressed, *pieces)
+        scratch = [pltpu.VMEM((2 * width, size), BF16)] + scratch
     return pl.pallas_call(
-        functools.partial(mirror_kernel, j, marks, plan),
-        in_specs=[SCALARS] + [WHOLE] * 4 + [WHOLE, FAR][: len(state)],
-        out_specs=[WHOLE, FAR],
-        out_shape=[kept, jax.ShapeDtypeStruct((size, size), BF16)],
-        scratch_shapes=[pltpu.VMEM((blocks, width, size), BF16), pltpu.SemaphoreType.DMA((blocks,))],
-        input_output_aliases={5: 0, 6: 1} if state else {},
+        kernel,
+        in_specs=[SCALARS] + [WHOLE] * (len(given) - 1) + [WHOLE, WHOLE, FAR][: len(state)],
+        out_specs=[WHOLE, WHOLE, FAR],
+        out_shape=shapes,
+        scratch_shapes=scratch,
+        input_output_aliases={len(given) + i: i for i in range(len(state))},
         compiler_params=params(),
         name="mirror",
-    )(scalars, piece, spread_d, joined_b, dressed, *state)
+    )(*given, *state)
 
 
 def cuts(blocks):
-    return [m * blocks // 16 for m in (0, 6, 12, 14, 15, 16)]
+    fixed = blocks // 4
+    slots = (blocks - fixed) * blocks
+    return fixed, [slots * m // 192 // 2 * 2 for m in (0, 64, 128, 160, 180)], slots
 
 
 def later(arrays, *after):
@@ -352,8 +475,10 @@
     assert amplitudes.shape[0] == 1
     blocks, width = d_values.shape[1], d_values.shape[2]
 
-    marks = cuts(blocks)
-    plan = Plan(lax.axis_size("fac") * d_cols.shape[0], blocks, len(marks) - 1)
+    fixed, marks, slots = cuts(blocks)
+    ends = [0] + marks[1:]
+    layout = Layout(blocks)
+    plan = Plan(lax.axis_size("fac") * d_cols.shape[0], blocks, len(ends))
     amplitudes = pltpu.with_memory_space_constraint(amplitudes, pltpu.HBM)
 
     def send(piece):
@@ -362,25 +487,29 @@
     def gather(array):
         return lax.all_gather(array, "fac", axis=0, tiled=True)
 
-    lanes = [m * width for m in marks]
-    head = turn(amplitudes, lanes[:2])[0]
-    pieces = [send(head)]
-    rest = turn(later(amplitudes, head), [lanes[1], lanes[-1]])[0]
+    head = turn(amplitudes, [0, fixed * width])[0]
+    pieces = [[send(head)]]
+    rest = turn(later(amplitudes, head), [fixed * width, blocks * width])[0]
     columns = gather(later(jnp.stack([d_cols, b_cols], axis=1), rest))
-    place, *picked = pick(marks, columns, rest)
-    pieces.append(send(picked[0]))
+    spans = list(zip(marks, marks[1:]))
+    packing, picked, over = pack_pieces(columns, [spans[0], (marks[-1], slots)], fixed, layout, rest)
+    over = lax.cond(packing[layout.used + blocks] > marks[-1], send, lambda piece: piece, over)
+    picked = later(picked, over)
+    pieces.append([send(picked), over])
+    picked = [picked, *pack_pieces(later(packing, picked), spans[1:], fixed, layout, rest)]
     d_all = gather(later(d_values, picked))
-    pieces.append(send(later(picked[1], d_all)))
+    pieces.append([send(later(picked[1], d_all))])
     b_all = gather(later(b_values, d_all))
-    pieces.append(send(later(picked[2], b_all)))
-    own = own_pair(marks, plan, columns, place, mirror_slot, d_all, b_all, amplitudes)
+    pieces.append([send(later(picked[2], b_all))])
+    own = own_pair(fixed, ends, plan, layout, columns, packing, mirror_slot, d_all, b_all, amplitudes)
     dressed, spread_d, joined_b, scalars = own
-    pieces.append(send(later(picked[3], dressed)))
+    pieces.append([send(later(picked[3], dressed))])
 
     state = ()
-    for j, piece in enumerate(pieces):
-        state = mirror_piece(j, marks, plan, scalars, piece, spread_d, joined_b, dressed, state)
-    return state[1][None]
+    for j, arrived in enumerate(pieces):
+        starts = [] if j == 0 else [marks[j - 1], marks[-1]][: len(arrived)]
+        state = mirror_piece(j, starts, slots, plan, scalars, arrived, spread_d, joined_b, dressed, state)
+    return state[2][None]
 
 
 def solution(mesh):

time: 98.6 us -> 96.9 us (0.983)
  waiting for transfers between devices: 20.9 us -> 5.44 us
  Pallas kernels: 41.9 us -> 55.1 us
    ppermute x5, waiting for transfers between devices: 20.9 us -> 5.44 us  [send(): return lax.ppermute(piece, 'pair', perm)]
    pallas_call x7 -> x8, Pallas kernels: 39 us -> 52.2 us  [the longest x5 22.1 us: mirror_piece(): pl.pallas_call(kernel, in_specs=[SCALARS] + [WHOLE] * (len(given) - 1) +...]
  transfers between devices with their start and end apart: 5 -> 5, of which waited for: 2 -> 1; matrix products, arithmetic and copies ran while one was open for 0% -> 1% of each run, Pallas kernels for 39% -> 52%
where the time goes in v4:
time: 96.9 us; the launch traced here: 97.9 us
  Pallas kernels  55.1 us (57%)
  blocking collectives  25.4 us (26%)
  starting transfers between devices  9.76 us (10%)
  waiting for transfers between devices  5.44 us (6%)
  between operations  1.47 us (2%)
    all_gather x3, blocking collectives, gather(): return lax.all_gather(array, 'fac', axis=0, tiled=True)  25.4 us
    pallas_call x5, Pallas kernels, mirror_piece(): pl.pallas_call(kernel, in_specs=[SCALARS] + [WHOLE] * (len(given) - 1) +...  22.1 us
    pallas_call x1, Pallas kernels, own_pair(): pl.pallas_call(functools.partial(own_kernel, fixed, ends, plan, layout),...  21.3 us
    ppermute x5, starting transfers between devices, send(): return lax.ppermute(piece, 'pair', perm)  9.76 us
    pallas_call x2, Pallas kernels, pack_pieces(): pl.pallas_call(kernel, in_specs=[SCALARS, WHOLE], out_specs=[SCALARS] * o...  8.74 us
    ppermute x5, waiting for transfers between devices, send(): return lax.ppermute(piece, 'pair', perm)  5.44 us
    pallas_call x2, Pallas kernels, turn(): pl.pallas_call(functools.partial(turn_kernel, marks), in_specs=[FAR], out...  2.95 us
  transfers between devices with their start and end apart: 5, of which 1 were waited for; matrix products, arithmetic and copies ran while one was open for 1% of the time, Pallas kernels for 52%

profile of v4, /device:TPU:0, one launch (start us, length us, event | category | flops | bytes accessed | tf_op | source)
XLA Modules:
  0.0 97.9 jit_solution(206785160433415677)
XLA Ops:
  0.0 1.2 %turn.2 = bf16[1,256,1024]{2,1,0:T(8,128)(2,1)S(1)} custom-call(bf16[1,1024,1024]{2,1,0:T(8,128)(2,1)} %source.4), custom_call_target="tpu_custom_call" | custom-call | tf_op jit(solution)/shard_map/turn/pallas_call | solution.py:50
  1.2 0.0 copy-start.2
  1.2 0.0 copy-start.3
  1.2 4.1 %collective-permute-start.5 = (bf16[1,256,1024]{2,1,0:T(8,128)(2,1)S(1)}, bf16[1,256,1024]{2,1,0:T(8,128)(2,1)S(1)}, u32[]{:S(2)}, u32[]{:S(2)}) collective-permute-start(bf16[1,256,1024]{2,1,0:T(8,128)(2,1)S(1)} %turn.2), channel_id=1, source_target_pairs={{0,16},{4,20},{8,24},{12,28},{16,0},{20,4},{24,8},{28,12},{1,17},{... | collective-permute-start | bytes 1572872 | tf_op jit(solution)/shard_map/ppermute | solution.py:485
  5.3 1.7 %turn.3.turned = bf16[1,768,1024]{2,1,0:T(8,128)(2,1)S(1)} custom-call(bf16[1,1024,1024]{2,1,0:T(8,128)(2,1)} %source.4), custom_call_target="tpu_custom_call" | custom-call | tf_op jit(solution)/shard_map/turn/pallas_call | solution.py:50
  7.1 0.0 copy-start
  7.1 0.0 copy-done.2
  7.1 0.0 copy-done.3
  7.1 5.2 %all_gather.9.columns = s32[4,2,16]{2,1,0:T(2,128)S(1)} all-gather(s32[1,2,16]{2,1,0:T(2,128)S(1)} %pad_add_fusion), channel_id=1, replica_groups=mesh['pair'=8,'fac'=4] {'fac'}, dimensions={0}, use_global_device_ids=true | all-gather | bytes 640 | tf_op jit(solution)/shard_map/all_gather | solution.py:488
  12.3 5.7 %pack.2 = (s32[545]{0:T(1024)S(1)}, bf16[1,64,4096]{2,1,0:T(8,128)(2,1)S(1)}, bf16[1,64,768]{2,1,0:T(8,128)(2,1)S(1)}) custom-call(s32[4,2,16]{2,1,0:T(2,128)S(1)} %all_gather.9.columns, bf16[1,768,1024]{2,1,0:T(8,128)(2,1)S(1)} %turn.3.turned), custom_call_target="tpu_custom_call" | custom-call | tf_op jit(solution)/shard_map/pack/pallas_call | solution.py:165
  18.0 0.6 slice.3
  19.3 0.0 copy-start.1
  19.3 0.1 collective-permute-start.4
  19.4 3.0 %pack.3 = (bf16[1,64,4096]{2,1,0:T(8,128)(2,1)S(1)}, bf16[1,64,2048]{2,1,0:T(8,128)(2,1)S(1)}, bf16[1,64,1280]{2,1,0:T(8,128)(2,1)S(1)}) custom-call(s32[545]{0:T(1024)S(1)} %get-tuple-element.48.scalars.packing, bf16[1,768,1024]{2,1,0:T(8,128)(2,1)S(1)} %turn.3.turned), custom_call_target="tpu_custom_call" | custom-call | tf_op jit(solution)/shard_map/pack/pallas_call | solution.py:165
  22.4 0.0 copy-done
  22.4 10.4 %all_gather.10.d_all = bf16[4,16,64,64]{3,2,1,0:T(8,128)(2,1)S(1)} all-gather(bf16[1,16,64,64]{3,2,1,0:T(8,128)(2,1)S(1)} %copy-done), channel_id=1, replica_groups=mesh['pair'=8,'fac'=4] {'fac'}, dimensions={0}, use_global_device_ids=true | all-gather | bytes 655360 | tf_op jit(solution)/shard_map/all_gather | solution.py:488
  32.8 2.6 %collective-permute-start.3 = (bf16[1,64,4096]{2,1,0:T(8,128)(2,1)S(1)}, bf16[1,64,4096]{2,1,0:T(8,128)(2,1)S(1)}, u32[]{:S(2)}, u32[]{:S(2)}) collective-permute-start(bf16[1,64,4096]{2,1,0:T(8,128)(2,1)S(1)} %get-tuple-element.60), channel_id=1, source_target_pairs={{0,16},{4,20},{8,24},{12,28},{16,0},{20,4},{24,8},{28,12},{1,17},{... | collective-permute-start | bytes 1572872 | tf_op jit(solution)/shard_map/ppermute | solution.py:485
  35.4 0.0 copy-done.1
  35.4 9.9 %all_gather.11.b_all = bf16[4,16,64,64]{3,2,1,0:T(8,128)(2,1)S(1)} all-gather(bf16[1,16,64,64]{3,2,1,0:T(8,128)(2,1)S(1)} %copy-done.1), channel_id=1, replica_groups=mesh['pair'=8,'fac'=4] {'fac'}, dimensions={0}, use_global_device_ids=true | all-gather | bytes 655360 | tf_op jit(solution)/shard_map/all_gather | solution.py:488
  45.3 0.3 collective-permute-start.2
  46.3 21.3 %own.1 = (bf16[1024,1024]{1,0:T(8,128)(2,1)S(1)}, bf16[4,8,256,128]{3,2,1,0:T(8,128)(2,1)S(1)}, bf16[16,64,256]{2,1,0:T(8,128)(2,1)S(1)}, s32[476]{0:T(512)S(1)}) custom-call(s32[4,2,16]{2,1,0:T(2,128)S(1)} %all_gather.9.columns, s32[545]{0:T(1024)S(1)} %get-tuple-element.48.scalars.packing, s32[1]{0:T(128)S(6)} %copy.33.slot, ...), custom_call_target="tpu_custom_call" | custom-call | tf_op jit(solution)/shard_map/own/pallas_call | solution.py:334
  67.6 2.7 %collective-permute-start.1 = (bf16[1,64,1280]{2,1,0:T(8,128)(2,1)S(1)}, bf16[1,64,1280]{2,1,0:T(8,128)(2,1)S(1)}, u32[]{:S(2)}, u32[]{:S(2)}) collective-permute-start(bf16[1,64,1280]{2,1,0:T(8,128)(2,1)S(1)} %get-tuple-element.58), channel_id=1, source_target_pairs={{0,16},{4,20},{8,24},{12,28},{16,0},{20,4},{24,8},{28,12},{1,17},{... | collective-permute-start | bytes 491528 | tf_op jit(solution)/shard_map/ppermute | solution.py:485
  70.2 0.0 collective-permute-done.5.piece
  70.2 3.0 %mirror.5 = (bf16[4,1024,1024]{2,1,0:T(8,128)(2,1)S(1)}, bf16[64,12288]{1,0:T(8,128)(2,1)S(1)}, bf16[1024,1024]{1,0:T(8,128)(2,1)}) custom-call(s32[476]{0:T(512)S(1)} %get-tuple-element.54.scalars, bf16[1,256,1024]{2,1,0:T(8,128)(2,1)S(1)} %collective-permute-done.5.piece, bf16[4,8,256,128]{3,2,1,0:T(8,128)(2,1)S(1)} %get-tuple-element.55.spread_d, ...), custom_call_target="tpu_custom_call" | custom-call | tf_op jit(solution)/shard_map/mirror/pallas_call | solution.py:450
  73.2 0.0 collective-permute-done.4.rest_0_
  73.2 4.7 %mirror.6 = (bf16[4,1024,1024]{2,1,0:T(8,128)(2,1)S(1)}, bf16[64,12288]{1,0:T(8,128)(2,1)S(1)}, bf16[1024,1024]{1,0:T(8,128)(2,1)}) custom-call(s32[476]{0:T(512)S(1)} %get-tuple-element.54.scalars, bf16[4,8,256,128]{3,2,1,0:T(8,128)(2,1)S(1)} %get-tuple-element.55.spread_d, ...), custom_call_target="tpu_custom_call", output_to_operand_aliasing={{0}: (6, {}), {1}: (7, {}), {2}: (8, {})} | custom-call | tf_op jit(solution)/shard_map/mirror/pallas_call | solution.py:450
  78.0 5.4 %collective-permute-done.3.rest_0_ = bf16[1,64,4096]{2,1,0:T(8,128)(2,1)S(1)} collective-permute-done((bf16[1,64,4096]{2,1,0:T(8,128)(2,1)S(1)}, bf16[1,64,4096]{2,1,0:T(8,128)(2,1)S(1)}, u32[]{:S(2)}, u32[]{:S(2)}) %collective-permute-start.3) | collective-permute-done | bytes 524320 | tf_op jit(solution)/shard_map/ppermute | solution.py:485
  83.4 7.3 %mirror.7 = (bf16[4,1024,1024]{2,1,0:T(8,128)(2,1)S(1)}, bf16[64,12288]{1,0:T(8,128)(2,1)S(1)}, bf16[1024,1024]{1,0:T(8,128)(2,1)}) custom-call(s32[476]{0:T(512)S(1)} %get-tuple-element.54.scalars, bf16[4,8,256,128]{3,2,1,0:T(8,128)(2,1)S(1)} %get-tuple-element.55.spread_d, ...), custom_call_target="tpu_custom_call", output_to_operand_aliasing={{0}: (5, {}), {1}: (6, {}), {2}: (7, {})} | custom-call | tf_op jit(solution)/shard_map/mirror/pallas_call | solution.py:450
  90.7 0.0 collective-permute-done.2.rest_0_
  90.7 3.8 %mirror.8 = (bf16[4,1024,1024]{2,1,0:T(8,128)(2,1)S(1)}, bf16[64,12288]{1,0:T(8,128)(2,1)S(1)}, bf16[1024,1024]{1,0:T(8,128)(2,1)}) custom-call(s32[476]{0:T(512)S(1)} %get-tuple-element.54.scalars, bf16[4,8,256,128]{3,2,1,0:T(8,128)(2,1)S(1)} %get-tuple-element.55.spread_d, ...), custom_call_target="tpu_custom_call", output_to_operand_aliasing={{0}: (5, {}), {1}: (6, {}), {2}: (7, {})} | custom-call | tf_op jit(solution)/shard_map/mirror/pallas_call | solution.py:450
  94.5 0.0 collective-permute-done.1.rest_0_
  94.5 3.3 %mirror.9 = (bf16[4,1024,1024]{2,1,0:T(8,128)(2,1)S(1)}, bf16[64,12288]{1,0:T(8,128)(2,1)S(1)}, bf16[1024,1024]{1,0:T(8,128)(2,1)}) custom-call(s32[476]{0:T(512)S(1)} %get-tuple-element.54.scalars, bf16[4,8,256,128]{3,2,1,0:T(8,128)(2,1)S(1)} %get-tuple-element.55.spread_d, ...), custom_call_target="tpu_custom_call", output_to_operand_aliasing={{0}: (5, {}), {1}: (6, {}), {2}: (7, {})} | custom-call | tf_op jit(solution)/shard_map/mirror/pallas_call | solution.py:450
  (2 shorter events, 0.0 us)
Async XLA Ops:
  1.2 5.9 %copy-start.2 = (s32[1,16]{1,0:T(1,128)S(1)}, s32[1,16]{1,0:T(1,128)}, u32[]{:S(2)}) copy-start(s32[1,16]{1,0:T(1,128)} %param.13) | copy-start | bytes 196
  1.2 5.9 %copy-start.3 = (s32[1,16]{1,0:T(1,128)S(1)}, s32[1,16]{1,0:T(1,128)}, u32[]{:S(2)}) copy-start(s32[1,16]{1,0:T(1,128)} %param.11) | copy-start | bytes 196
  1.2 69.0 %collective-permute-start.5 = (bf16[1,256,1024]{2,1,0:T(8,128)(2,1)S(1)}, bf16[1,256,1024]{2,1,0:T(8,128)(2,1)S(1)}, u32[]{:S(2)}, u32[]{:S(2)}) collective-permute-start(bf16[1,256,1024]{2,1,0:T(8,128)(2,1)S(1)} %turn.2), channel_id=1, source_target_pairs={{0,16},{4,20},{8,24},{12,28},{16,0},{20,4},{24,8},{28,12},{1,17},{... | collective-permute-start | bytes 1572872 | tf_op jit(solution)/shard_map/ppermute | solution.py:485
  7.1 15.3 %copy-start = (bf16[1,16,64,64]{3,2,1,0:T(8,128)(2,1)S(1)}, bf16[1,16,64,64]{3,2,1,0:T(8,128)(2,1)}, u32[]{:S(2)}) copy-start(bf16[1,16,64,64]{3,2,1,0:T(8,128)(2,1)} %param.10) | copy-start | bytes 393220
  19.3 16.1 %copy-start.1 = (bf16[1,16,64,64]{3,2,1,0:T(8,128)(2,1)S(1)}, bf16[1,16,64,64]{3,2,1,0:T(8,128)(2,1)}, u32[]{:S(2)}) copy-start(bf16[1,16,64,64]{3,2,1,0:T(8,128)(2,1)} %param.12) | copy-start | bytes 393220
  19.3 53.9 %collective-permute-start.4 = (bf16[1,64,4096]{2,1,0:T(8,128)(2,1)S(1)}, bf16[1,64,4096]{2,1,0:T(8,128)(2,1)S(1)}, u32[]{:S(2)}, u32[]{:S(2)}) collective-permute-start(bf16[1,64,4096]{2,1,0:T(8,128)(2,1)S(1)} %get-tuple-element.47), channel_id=1, source_target_pairs={{0,16},{4,20},{8,24},{12,28},{16,0},{20,4},{24,8},{28,12},{1,17},{... | collective-permute-start | bytes 1572872 | tf_op jit(solution)/shard_map/ppermute | solution.py:485
  32.8 50.6 %collective-permute-start.3 = (bf16[1,64,4096]{2,1,0:T(8,128)(2,1)S(1)}, bf16[1,64,4096]{2,1,0:T(8,128)(2,1)S(1)}, u32[]{:S(2)}, u32[]{:S(2)}) collective-permute-start(bf16[1,64,4096]{2,1,0:T(8,128)(2,1)S(1)} %get-tuple-element.60), channel_id=1, source_target_pairs={{0,16},{4,20},{8,24},{12,28},{16,0},{20,4},{24,8},{28,12},{1,17},{... | collective-permute-start | bytes 1572872 | tf_op jit(solution)/shard_map/ppermute | solution.py:485
  45.3 45.4 %collective-permute-start.2 = (bf16[1,64,2048]{2,1,0:T(8,128)(2,1)S(1)}, bf16[1,64,2048]{2,1,0:T(8,128)(2,1)S(1)}, u32[]{:S(2)}, u32[]{:S(2)}) collective-permute-start(bf16[1,64,2048]{2,1,0:T(8,128)(2,1)S(1)} %get-tuple-element.59), channel_id=1, source_target_pairs={{0,16},{4,20},{8,24},{12,28},{16,0},{20,4},{24,8},{28,12},{1,17},{... | collective-permute-start | bytes 786440 | tf_op jit(solution)/shard_map/ppermute | solution.py:485
  67.6 27.0 %collective-permute-start.1 = (bf16[1,64,1280]{2,1,0:T(8,128)(2,1)S(1)}, bf16[1,64,1280]{2,1,0:T(8,128)(2,1)S(1)}, u32[]{:S(2)}, u32[]{:S(2)}) collective-permute-start(bf16[1,64,1280]{2,1,0:T(8,128)(2,1)S(1)} %get-tuple-element.58), channel_id=1, source_target_pairs={{0,16},{4,20},{8,24},{12,28},{16,0},{20,4},{24,8},{28,12},{1,17},{... | collective-permute-start | bytes 491528 | tf_op jit(solution)/shard_map/ppermute | solution.py:485

commit v5 on v4

--- a/solution.py
+++ b/solution.py
@@ -213,8 +213,9 @@
 
 
 class Plan:
-    def __init__(self, factors, blocks, pieces):
+    def __init__(self, factors, blocks, pieces, other):
         self.blocks = blocks
+        self.other = other
         self.lanes = 0
         self.rows = factors * blocks
         self.uses = 2 * factors * blocks
@@ -242,13 +243,15 @@
             scalars[use] = scalars[use] + 1
         return carry
 
-    def copy(i, carry):
-        scalars[plan.slot + i] = packing[layout.slot + i]
+    def locate(i, carry):
+        for n in range(2):
+            at = packing[layout.slot + 2 * i + n]
+            scalars[plan.slot + 2 * i + n] = (at + n) % 2 * plan.other + at // 2 * LANES
         return carry
 
     lax.fori_loop(0, factors * blocks, clear, 0)
     lax.fori_loop(0, blocks, offsets, 0)
-    lax.fori_loop(fixed * blocks, blocks * blocks, copy, 0)
+    lax.fori_loop(fixed * blocks // 2, blocks * blocks // 2, locate, 0)
     found, low = jnp.int32(0), jnp.int32(0)
     for j, end in enumerate(ends):
 
@@ -339,7 +342,7 @@
             pltpu.VMEM((size, size), BF16),
             pltpu.VMEM(spread, BF16),
             pltpu.VMEM(joined, BF16),
-            jax.ShapeDtypeStruct((plan.size,), jnp.int32),
+            pltpu.SMEM((plan.size,), jnp.int32),
         ],
         scratch_shapes=[
             pltpu.VMEM(spread, BF16),
@@ -359,18 +362,27 @@
         return pltpu.make_async_copy(ready.at[r], out.at[aligned(r * width, width), :], sems.at[r])
 
     def left(i, carry):
-        r = scalars[plan.order + i]
-        mirrored = apply_left(r, joined_b, lambda q, r: scalars[plan.rows + q * blocks + r], middle)
-        own = dressed[aligned(r * width, width), :].astype(F32)
-        ready[r] = (own + mirrored.astype(BF16).astype(F32)).astype(BF16)
-        leave(i).start()
+        totals = []
+        for n in range(2):
+            r = scalars[plan.order + jnp.minimum(begin + 2 * i + n, end - 1)]
+            mirrored = apply_left(r, joined_b, lambda q, r: scalars[plan.rows + q * blocks + r], middle)
+            own = dressed[aligned(r * width, width), :].astype(F32)
+            totals.append((own + mirrored.astype(BF16).astype(F32)).astype(BF16))
+        for n, total in enumerate(totals):
+            at = begin + 2 * i + n
+            ready[jnp.where(at < end, scalars[plan.order + jnp.minimum(at, end - 1)], blocks)] = total
+
+            @pl.when(at < end)
+            def _(at=at):
+                leave(at).start()
+
         return carry
 
     def wait(i, carry):
         leave(i).wait()
         return carry
 
-    lax.fori_loop(begin, end, left, 0)
+    lax.fori_loop(0, (end - begin + 1) // 2, left, 0)
     lax.fori_loop(begin, end, wait, 0)
 
 
@@ -392,31 +404,32 @@
     finish_rows(0, end, plan, scalars, joined_b, dressed, middle, out, ready, sems)
 
 
-def packed_kernel(j, starts, plan, scalars, spread_d, joined_b, dressed, *rest):
+def packed_kernel(j, last, starts, plan, scalars, spread_d, joined_b, dressed, *rest):
     pieces, rest = rest[: len(starts)], rest[len(starts) + 3 :]
     middle, packed, out, row, ready, sems = rest
     slot, factors = scalars[plan.mirror], spread_d.shape[0]
     blocks, width = joined_b.shape[:2]
     for start, piece in zip(starts, pieces):
         for lane in range(0, piece.shape[2], LANES):
-            packed[:, start * width + lane : start * width + lane + LANES] = piece[slot, :, lane : lane + LANES]
+            tile, at = piece[slot, :, lane : lane + LANES], start * width + lane
+            packed[:, at : at + LANES] = tile
+            packed[:, plan.other + at : plan.other + at + LANES] = swap_halves(tile)
 
     fixed = scalars[plan.whole]
     before, after = scalars[plan.whole + j - 1], scalars[plan.whole + j]
+    left_half = lax.broadcasted_iota(jnp.int32, (width, LANES), 1) < width
 
     def take(i, carry):
         first = jnp.maximum(jnp.minimum(before + 2 * i, after - 2), fixed)
         for n in range(2):
             for k in range(0, blocks, 2):
-                low, high = (scalars[plan.slot + (first + n) * blocks + k + i] for i in range(2))
-                tiles = [packed[:, aligned(slot // 2 * LANES, LANES)] for slot in (low, high)]
-                tile = join_halves(tiles[0], low % 2 == 1, tiles[1], high % 2 == 0)
-                row[n * width : (n + 1) * width, k * width : (k + 2) * width] = tile
+                tiles = [packed[:, aligned(scalars[plan.slot + (first + n) * blocks + k + m], LANES)] for m in range(2)]
+                row[n * width : (n + 1) * width, k * width : (k + 2) * width] = jnp.where(left_half, *tiles)
         for q in range(factors):
             uses = plan.uses + q * blocks + first
-
-            @pl.when(scalars[uses] + scalars[uses + 1] > 0)
-            def _(q=q):
+            skip = last and scalars[uses] + scalars[uses + 1] == 0
+
+            def right(q=q):
                 apply_right(
                     lambda lane: row[:, aligned(lane, LANES)],
                     lambda q, s: scalars[plan.lanes + q * blocks + s],
@@ -427,6 +440,11 @@
                     2 * width,
                 )
 
+            if last:
+                pl.when(jnp.logical_not(skip))(right)
+            else:
+                right()
+
         return carry
 
     lax.fori_loop(0, (after - before + 1) // 2, take, 0)
@@ -434,18 +452,18 @@
     finish_rows(begin, end, plan, scalars, joined_b, dressed, middle, out, ready, sems)
 
 
-def mirror_piece(j, starts, slots, plan, scalars, pieces, spread_d, joined_b, dressed, state):
+def mirror_piece(j, last, starts, slots, plan, scalars, pieces, spread_d, joined_b, dressed, state):
     size, (blocks, width) = dressed.shape[0], joined_b.shape[:2]
     shapes = [
         pltpu.VMEM((spread_d.shape[0], size, size), BF16),
-        pltpu.VMEM((width, slots * width), BF16),
+        pltpu.VMEM((width, 2 * slots * width), BF16),
         jax.ShapeDtypeStruct((size, size), BF16),
     ]
-    scratch = [pltpu.VMEM((blocks, width, size), BF16), pltpu.SemaphoreType.DMA((blocks,))]
+    scratch = [pltpu.VMEM((blocks + 1, width, size), BF16), pltpu.SemaphoreType.DMA((blocks,))]
     if j == 0:
         kernel, given = functools.partial(opening_kernel, plan), (scalars, *pieces, spread_d, joined_b, dressed)
     else:
-        kernel, given = functools.partial(packed_kernel, j, starts, plan), (scalars, spread_d, joined_b, dressed, *pieces)
+        kernel, given = functools.partial(packed_kernel, j, last, starts, plan), (scalars, spread_d, joined_b, dressed, *pieces)
         scratch = [pltpu.VMEM((2 * width, size), BF16)] + scratch
     return pl.pallas_call(
         kernel,
@@ -478,7 +496,7 @@
     fixed, marks, slots = cuts(blocks)
     ends = [0] + marks[1:]
     layout = Layout(blocks)
-    plan = Plan(lax.axis_size("fac") * d_cols.shape[0], blocks, len(ends))
+    plan = Plan(lax.axis_size("fac") * d_cols.shape[0], blocks, len(ends), slots * width)
     amplitudes = pltpu.with_memory_space_constraint(amplitudes, pltpu.HBM)
 
     def send(piece):
@@ -508,7 +526,7 @@
     state = ()
     for j, arrived in enumerate(pieces):
         starts = [] if j == 0 else [marks[j - 1], marks[-1]][: len(arrived)]
-        state = mirror_piece(j, starts, slots, plan, scalars, arrived, spread_d, joined_b, dressed, state)
+        state = mirror_piece(j, j == len(pieces) - 1, starts, slots, plan, scalars, arrived, spread_d, joined_b, dressed, state)
     return state[2][None]
 
 

time: 96.9 us -> 94.6 us (0.976); the launches traced: 97.9 us -> 94.4 us
  Pallas kernels: 55.1 us -> 47.9 us
  waiting for transfers between devices: 5.44 us -> 9.21 us
    pallas_call x5, Pallas kernels: 22.1 us -> 14.5 us  [mirror_piece(): pl.pallas_call(kernel, in_specs=[SCALARS] + [WHOLE] * (len(given) - 1) +...]
    ppermute x5, waiting for transfers between devices: 5.44 us -> 9.21 us  [send(): return lax.ppermute(piece, 'pair', perm)]
  transfers between devices with their start and end apart: 5 -> 5, of which waited for: 1 -> 2; matrix products, arithmetic and copies ran while one was open for 1% -> 1% of each run, Pallas kernels for 52% -> 48%
where the time goes in v5:
time: 94.6 us; the launch traced here: 94.4 us
  Pallas kernels  47.9 us (51%)
  blocking collectives  25.5 us (27%)
  starting transfers between devices  9.77 us (10%)
  waiting for transfers between devices  9.21 us (10%)
  between operations  1.44 us (2%)
    all_gather x3, blocking collectives, gather(): return lax.all_gather(array, 'fac', axis=0, tiled=True)  25.5 us
    pallas_call x1, Pallas kernels, own_pair(): pl.pallas_call(functools.partial(own_kernel, fixed, ends, plan, layout),...  21.6 us
    pallas_call x5, Pallas kernels, mirror_piece(): pl.pallas_call(kernel, in_specs=[SCALARS] + [WHOLE] * (len(given) - 1) +...  14.5 us
    ppermute x5, starting transfers between devices, send(): return lax.ppermute(piece, 'pair', perm)  9.77 us
    ppermute x5, waiting for transfers between devices, send(): return lax.ppermute(piece, 'pair', perm)  9.21 us
    pallas_call x2, Pallas kernels, pack_pieces(): pl.pallas_call(kernel, in_specs=[SCALARS, WHOLE], out_specs=[SCALARS] * o...  8.74 us
    pallas_call x2, Pallas kernels, turn(): pl.pallas_call(functools.partial(turn_kernel, marks), in_specs=[FAR], out...  2.98 us
  transfers between devices with their start and end apart: 5, of which 2 were waited for; matrix products, arithmetic and copies ran while one was open for 1% of the time, Pallas kernels for 48%

profile of v5, /device:TPU:0, one launch (start us, length us, event | category | flops | bytes accessed | tf_op | source)
XLA Modules:
  0.0 94.4 jit_solution(11259948669865119994)
XLA Ops:
  0.0 0.0 copy-start.1
  0.0 0.0 copy-start.2
  0.0 1.2 %turn.2 = bf16[1,256,1024]{2,1,0:T(8,128)(2,1)S(1)} custom-call(bf16[1,1024,1024]{2,1,0:T(8,128)(2,1)} %source.4), custom_call_target="tpu_custom_call" | custom-call | tf_op jit(solution)/shard_map/turn/pallas_call | solution.py:50
  1.3 0.0 copy-start
  1.3 4.1 %collective-permute-start.5 = (bf16[1,256,1024]{2,1,0:T(8,128)(2,1)S(1)}, bf16[1,256,1024]{2,1,0:T(8,128)(2,1)S(1)}, u32[]{:S(2)}, u32[]{:S(2)}) collective-permute-start(bf16[1,256,1024]{2,1,0:T(8,128)(2,1)S(1)} %turn.2), channel_id=1, source_target_pairs={{0,16},{4,20},{8,24},{12,28},{16,0},{20,4},{24,8},{28,12},{1,17},{... | collective-permute-start | bytes 1572872 | tf_op jit(solution)/shard_map/ppermute | solution.py:503
  5.4 1.7 %turn.3.turned = bf16[1,768,1024]{2,1,0:T(8,128)(2,1)S(1)} custom-call(bf16[1,1024,1024]{2,1,0:T(8,128)(2,1)} %source.4), custom_call_target="tpu_custom_call" | custom-call | tf_op jit(solution)/shard_map/turn/pallas_call | solution.py:50
  7.1 0.0 copy-done.1
  7.1 0.0 copy-done.2
  7.1 5.1 %all_gather.9.columns = s32[4,2,16]{2,1,0:T(2,128)S(1)} all-gather(s32[1,2,16]{2,1,0:T(2,128)S(1)} %pad_add_fusion), channel_id=1, replica_groups=mesh['pair'=8,'fac'=4] {'fac'}, dimensions={0}, use_global_device_ids=true | all-gather | bytes 640 | tf_op jit(solution)/shard_map/all_gather | solution.py:506
  12.2 5.7 %pack.2 = (s32[545]{0:T(1024)S(1)}, bf16[1,64,4096]{2,1,0:T(8,128)(2,1)S(1)}, bf16[1,64,768]{2,1,0:T(8,128)(2,1)S(1)}) custom-call(s32[4,2,16]{2,1,0:T(2,128)S(1)} %all_gather.9.columns, bf16[1,768,1024]{2,1,0:T(8,128)(2,1)S(1)} %turn.3.turned), custom_call_target="tpu_custom_call" | custom-call | tf_op jit(solution)/shard_map/pack/pallas_call | solution.py:165
  17.9 0.6 slice.3
  19.2 0.1 collective-permute-start.4
  19.3 3.0 %pack.3 = (bf16[1,64,4096]{2,1,0:T(8,128)(2,1)S(1)}, bf16[1,64,2048]{2,1,0:T(8,128)(2,1)S(1)}, bf16[1,64,1280]{2,1,0:T(8,128)(2,1)S(1)}) custom-call(s32[545]{0:T(1024)S(1)} %get-tuple-element.48.scalars.packing, bf16[1,768,1024]{2,1,0:T(8,128)(2,1)S(1)} %turn.3.turned), custom_call_target="tpu_custom_call" | custom-call | tf_op jit(solution)/shard_map/pack/pallas_call | solution.py:165
  22.3 0.0 copy-done
  22.3 10.4 %all_gather.10.d_all = bf16[4,16,64,64]{3,2,1,0:T(8,128)(2,1)S(1)} all-gather(bf16[1,16,64,64]{3,2,1,0:T(8,128)(2,1)S(1)} %copy-done), channel_id=1, replica_groups=mesh['pair'=8,'fac'=4] {'fac'}, dimensions={0}, use_global_device_ids=true | all-gather | bytes 655360 | tf_op jit(solution)/shard_map/all_gather | solution.py:506
  32.7 2.6 %collective-permute-start.3 = (bf16[1,64,4096]{2,1,0:T(8,128)(2,1)S(1)}, bf16[1,64,4096]{2,1,0:T(8,128)(2,1)S(1)}, u32[]{:S(2)}, u32[]{:S(2)}) collective-permute-start(bf16[1,64,4096]{2,1,0:T(8,128)(2,1)S(1)} %get-tuple-element.60), channel_id=1, source_target_pairs={{0,16},{4,20},{8,24},{12,28},{16,0},{20,4},{24,8},{28,12},{1,17},{... | collective-permute-start | bytes 1572872 | tf_op jit(solution)/shard_map/ppermute | solution.py:503
  35.3 10.1 %all_gather.11.b_all = bf16[4,16,64,64]{3,2,1,0:T(8,128)(2,1)S(1)} all-gather(bf16[1,16,64,64]{3,2,1,0:T(8,128)(2,1)} %param.12), channel_id=1, replica_groups=mesh['pair'=8,'fac'=4] {'fac'}, dimensions={0}, use_global_device_ids=true | all-gather | bytes 655360 | tf_op jit(solution)/shard_map/all_gather | solution.py:506
  45.3 0.3 collective-permute-start.2
  46.3 21.6 %own.1 = (bf16[1024,1024]{1,0:T(8,128)(2,1)S(1)}, bf16[4,8,256,128]{3,2,1,0:T(8,128)(2,1)S(1)}, bf16[16,64,256]{2,1,0:T(8,128)(2,1)S(1)}, s32[476]{0:T(512)S(4)}) custom-call(s32[4,2,16]{2,1,0:T(2,128)S(1)} %all_gather.9.columns, s32[545]{0:T(1024)S(1)} %get-tuple-element.48.scalars.packing, s32[1]{0:T(128)S(6)} %copy.33.slot, ...), custom_call_target="tpu_custom_call" | custom-call | tf_op jit(solution)/shard_map/own/pallas_call | solution.py:337
  68.0 2.7 %collective-permute-start.1 = (bf16[1,64,1280]{2,1,0:T(8,128)(2,1)S(1)}, bf16[1,64,1280]{2,1,0:T(8,128)(2,1)S(1)}, u32[]{:S(2)}, u32[]{:S(2)}) collective-permute-start(bf16[1,64,1280]{2,1,0:T(8,128)(2,1)S(1)} %get-tuple-element.58), channel_id=1, source_target_pairs={{0,16},{4,20},{8,24},{12,28},{16,0},{20,4},{24,8},{28,12},{1,17},{... | collective-permute-start | bytes 491528 | tf_op jit(solution)/shard_map/ppermute | solution.py:503
  70.6 0.0 collective-permute-done.5.piece
  70.6 1.7 %mirror.5 = (bf16[4,1024,1024]{2,1,0:T(8,128)(2,1)S(1)}, bf16[64,24576]{1,0:T(8,128)(2,1)S(1)}, bf16[1024,1024]{1,0:T(8,128)(2,1)}) custom-call(s32[476]{0:T(512)S(4)} %get-tuple-element.54.scalars, bf16[1,256,1024]{2,1,0:T(8,128)(2,1)S(1)} %collective-permute-done.5.piece, bf16[4,8,256,128]{3,2,1,0:T(8,128)(2,1)S(1)} %get-tuple-element.55.spread_d, ...), custom_call_target="tpu_custom_call" | custom-call | tf_op jit(solution)/shard_map/mirror/pallas_call | solution.py:468
  72.3 0.0 collective-permute-done.4.rest_0_
  72.3 3.3 %mirror.6 = (bf16[4,1024,1024]{2,1,0:T(8,128)(2,1)S(1)}, bf16[64,24576]{1,0:T(8,128)(2,1)S(1)}, bf16[1024,1024]{1,0:T(8,128)(2,1)}) custom-call(s32[476]{0:T(512)S(4)} %get-tuple-element.54.scalars, bf16[4,8,256,128]{3,2,1,0:T(8,128)(2,1)S(1)} %get-tuple-element.55.spread_d, ...), custom_call_target="tpu_custom_call", output_to_operand_aliasing={{0}: (6, {}), {1}: (7, {}), {2}: (8, {})} | custom-call | tf_op jit(solution)/shard_map/mirror/pallas_call | solution.py:468
  75.6 7.8 %collective-permute-done.3.rest_0_ = bf16[1,64,4096]{2,1,0:T(8,128)(2,1)S(1)} collective-permute-done((bf16[1,64,4096]{2,1,0:T(8,128)(2,1)S(1)}, bf16[1,64,4096]{2,1,0:T(8,128)(2,1)S(1)}, u32[]{:S(2)}, u32[]{:S(2)}) %collective-permute-start.3) | collective-permute-done | bytes 524320 | tf_op jit(solution)/shard_map/ppermute | solution.py:503
  83.4 4.2 %mirror.7 = (bf16[4,1024,1024]{2,1,0:T(8,128)(2,1)S(1)}, bf16[64,24576]{1,0:T(8,128)(2,1)S(1)}, bf16[1024,1024]{1,0:T(8,128)(2,1)}) custom-call(s32[476]{0:T(512)S(4)} %get-tuple-element.54.scalars, bf16[4,8,256,128]{3,2,1,0:T(8,128)(2,1)S(1)} %get-tuple-element.55.spread_d, ...), custom_call_target="tpu_custom_call", output_to_operand_aliasing={{0}: (5, {}), {1}: (6, {}), {2}: (7, {})} | custom-call | tf_op jit(solution)/shard_map/mirror/pallas_call | solution.py:468
  87.6 1.4 %collective-permute-done.2.rest_0_ = bf16[1,64,2048]{2,1,0:T(8,128)(2,1)S(1)} collective-permute-done((bf16[1,64,2048]{2,1,0:T(8,128)(2,1)S(1)}, bf16[1,64,2048]{2,1,0:T(8,128)(2,1)S(1)}, u32[]{:S(2)}, u32[]{:S(2)}) %collective-permute-start.2) | collective-permute-done | bytes 262176 | tf_op jit(solution)/shard_map/ppermute | solution.py:503
  89.0 3.7 %mirror.8 = (bf16[4,1024,1024]{2,1,0:T(8,128)(2,1)S(1)}, bf16[64,24576]{1,0:T(8,128)(2,1)S(1)}, bf16[1024,1024]{1,0:T(8,128)(2,1)}) custom-call(s32[476]{0:T(512)S(4)} %get-tuple-element.54.scalars, bf16[4,8,256,128]{3,2,1,0:T(8,128)(2,1)S(1)} %get-tuple-element.55.spread_d, ...), custom_call_target="tpu_custom_call", output_to_operand_aliasing={{0}: (5, {}), {1}: (6, {}), {2}: (7, {})} | custom-call | tf_op jit(solution)/shard_map/mirror/pallas_call | solution.py:468
  92.8 0.0 collective-permute-done.1.rest_0_
  92.8 1.7 %mirror.9 = (bf16[4,1024,1024]{2,1,0:T(8,128)(2,1)S(1)}, bf16[64,24576]{1,0:T(8,128)(2,1)S(1)}, bf16[1024,1024]{1,0:T(8,128)(2,1)}) custom-call(s32[476]{0:T(512)S(4)} %get-tuple-element.54.scalars, bf16[4,8,256,128]{3,2,1,0:T(8,128)(2,1)S(1)} %get-tuple-element.55.spread_d, ...), custom_call_target="tpu_custom_call", output_to_operand_aliasing={{0}: (5, {}), {1}: (6, {}), {2}: (7, {})} | custom-call | tf_op jit(solution)/shard_map/mirror/pallas_call | solution.py:468
  (2 shorter events, 0.0 us)
Async XLA Ops:
  0.0 7.1 %copy-start.1 = (s32[1,16]{1,0:T(1,128)S(1)}, s32[1,16]{1,0:T(1,128)}, u32[]{:S(2)}) copy-start(s32[1,16]{1,0:T(1,128)} %param.13) | copy-start | bytes 196
  0.0 7.1 %copy-start.2 = (s32[1,16]{1,0:T(1,128)S(1)}, s32[1,16]{1,0:T(1,128)}, u32[]{:S(2)}) copy-start(s32[1,16]{1,0:T(1,128)} %param.11) | copy-start | bytes 196
  1.3 21.1 %copy-start = (bf16[1,16,64,64]{3,2,1,0:T(8,128)(2,1)S(1)}, bf16[1,16,64,64]{3,2,1,0:T(8,128)(2,1)}, u32[]{:S(2)}) copy-start(bf16[1,16,64,64]{3,2,1,0:T(8,128)(2,1)} %param.10) | copy-start | bytes 393220
  1.3 69.4 %collective-permute-start.5 = (bf16[1,256,1024]{2,1,0:T(8,128)(2,1)S(1)}, bf16[1,256,1024]{2,1,0:T(8,128)(2,1)S(1)}, u32[]{:S(2)}, u32[]{:S(2)}) collective-permute-start(bf16[1,256,1024]{2,1,0:T(8,128)(2,1)S(1)} %turn.2), channel_id=1, source_target_pairs={{0,16},{4,20},{8,24},{12,28},{16,0},{20,4},{24,8},{28,12},{1,17},{... | collective-permute-start | bytes 1572872 | tf_op jit(solution)/shard_map/ppermute | solution.py:503
  19.2 53.1 %collective-permute-start.4 = (bf16[1,64,4096]{2,1,0:T(8,128)(2,1)S(1)}, bf16[1,64,4096]{2,1,0:T(8,128)(2,1)S(1)}, u32[]{:S(2)}, u32[]{:S(2)}) collective-permute-start(bf16[1,64,4096]{2,1,0:T(8,128)(2,1)S(1)} %get-tuple-element.47), channel_id=1, source_target_pairs={{0,16},{4,20},{8,24},{12,28},{16,0},{20,4},{24,8},{28,12},{1,17},{... | collective-permute-start | bytes 1572872 | tf_op jit(solution)/shard_map/ppermute | solution.py:503
  32.7 50.7 %collective-permute-start.3 = (bf16[1,64,4096]{2,1,0:T(8,128)(2,1)S(1)}, bf16[1,64,4096]{2,1,0:T(8,128)(2,1)S(1)}, u32[]{:S(2)}, u32[]{:S(2)}) collective-permute-start(bf16[1,64,4096]{2,1,0:T(8,128)(2,1)S(1)} %get-tuple-element.60), channel_id=1, source_target_pairs={{0,16},{4,20},{8,24},{12,28},{16,0},{20,4},{24,8},{28,12},{1,17},{... | collective-permute-start | bytes 1572872 | tf_op jit(solution)/shard_map/ppermute | solution.py:503
  45.3 43.7 %collective-permute-start.2 = (bf16[1,64,2048]{2,1,0:T(8,128)(2,1)S(1)}, bf16[1,64,2048]{2,1,0:T(8,128)(2,1)S(1)}, u32[]{:S(2)}, u32[]{:S(2)}) collective-permute-start(bf16[1,64,2048]{2,1,0:T(8,128)(2,1)S(1)} %get-tuple-element.59), channel_id=1, source_target_pairs={{0,16},{4,20},{8,24},{12,28},{16,0},{20,4},{24,8},{28,12},{1,17},{... | collective-permute-start | bytes 786440 | tf_op jit(solution)/shard_map/ppermute | solution.py:503
  68.0 24.8 %collective-permute-start.1 = (bf16[1,64,1280]{2,1,0:T(8,128)(2,1)S(1)}, bf16[1,64,1280]{2,1,0:T(8,128)(2,1)S(1)}, u32[]{:S(2)}, u32[]{:S(2)}) collective-permute-start(bf16[1,64,1280]{2,1,0:T(8,128)(2,1)S(1)} %get-tuple-element.58), channel_id=1, source_target_pairs={{0,16},{4,20},{8,24},{12,28},{16,0},{20,4},{24,8},{28,12},{1,17},{... | collective-permute-start | bytes 491528 | tf_op jit(solution)/shard_map/ppermute | solution.py:503

commit v6 on v5

--- a/solution.py
+++ b/solution.py
@@ -386,10 +386,11 @@
     lax.fori_loop(begin, end, wait, 0)
 
 
-def opening_kernel(plan, scalars, piece, spread_d, joined_b, dressed, middle, packed, out, ready, sems):
+def opening_kernel(plan, scalars, piece, spread_d, joined_b, dressed, middle, packed, out, token, ready, sems):
     slot, blocks = scalars[plan.mirror], joined_b.shape[0]
     rows = piece.shape[1]
     packed[...] = jnp.zeros(packed.shape, BF16)
+    token[...] = jnp.zeros(token.shape, F32)
     for q in range(spread_d.shape[0]):
         apply_right(
             lambda lane: piece[slot, :, aligned(lane, LANES)],
@@ -461,6 +462,7 @@
     ]
     scratch = [pltpu.VMEM((blocks + 1, width, size), BF16), pltpu.SemaphoreType.DMA((blocks,))]
     if j == 0:
+        shapes.append(jax.ShapeDtypeStruct((8, LANES), F32))
         kernel, given = functools.partial(opening_kernel, plan), (scalars, *pieces, spread_d, joined_b, dressed)
     else:
         kernel, given = functools.partial(packed_kernel, j, last, starts, plan), (scalars, spread_d, joined_b, dressed, *pieces)
@@ -468,7 +470,7 @@
     return pl.pallas_call(
         kernel,
         in_specs=[SCALARS] + [WHOLE] * (len(given) - 1) + [WHOLE, WHOLE, FAR][: len(state)],
-        out_specs=[WHOLE, WHOLE, FAR],
+        out_specs=[WHOLE, WHOLE, FAR, WHOLE][: len(shapes)],
         out_shape=shapes,
         scratch_shapes=scratch,
         input_output_aliases={len(given) + i: i for i in range(len(state))},
@@ -478,9 +480,9 @@
 
 
 def cuts(blocks):
-    fixed = blocks // 4
+    fixed = 3 * blocks // 16
     slots = (blocks - fixed) * blocks
-    return fixed, [slots * m // 192 // 2 * 2 for m in (0, 64, 128, 160, 180)], slots
+    return fixed, [slots * m // 208 // 2 * 2 for m in (0, 48, 96, 144, 172, 192)], slots
 
 
 def later(arrays, *after):
@@ -524,9 +526,13 @@
     pieces.append([send(later(picked[3], dressed))])
 
     state = ()
-    for j, arrived in enumerate(pieces):
+    for j in range(len(ends)):
+        if j == 1:
+            *state, token = state
+            pieces.append([send(later(picked[4], token))])
+        arrived = pieces[j]
         starts = [] if j == 0 else [marks[j - 1], marks[-1]][: len(arrived)]
-        state = mirror_piece(j, j == len(pieces) - 1, starts, slots, plan, scalars, arrived, spread_d, joined_b, dressed, state)
+        state = mirror_piece(j, j == len(ends) - 1, starts, slots, plan, scalars, arrived, spread_d, joined_b, dressed, state)
     return state[2][None]
 
 

time: 94.6 us -> 93.2 us (0.985)
  waiting for transfers between devices: 9.21 us -> 3.97 us
  Pallas kernels: 47.9 us -> 51.4 us
    ppermute x5 -> x6, waiting for transfers between devices: 9.21 us -> 3.97 us  [send(): return lax.ppermute(piece, 'pair', perm)]
    pallas_call x5 -> x6, Pallas kernels: 14.5 us -> 16.5 us  [mirror_piece(): pl.pallas_call(kernel, in_specs=[SCALARS] + [WHOLE] * (len(given) - 1) +...]
    ppermute x5 -> x6, starting transfers between devices: 9.77 us -> 10.1 us  [send(): return lax.ppermute(piece, 'pair', perm)]
  transfers between devices with their start and end apart: 5 -> 6, of which waited for: 2 -> 3; matrix products, arithmetic and copies ran while one was open for 1% -> 1% of each run, Pallas kernels for 48% -> 51%
where the time goes in v6:
time: 93.2 us
  Pallas kernels  51.4 us (55%)
  blocking collectives  25.4 us (27%)
  starting transfers between devices  10.1 us (11%)
  waiting for transfers between devices  3.97 us (4%)
  between operations  1.62 us (2%)
    all_gather x3, blocking collectives, gather(): return lax.all_gather(array, 'fac', axis=0, tiled=True)  25.4 us
    pallas_call x1, Pallas kernels, own_pair(): pl.pallas_call(functools.partial(own_kernel, fixed, ends, plan, layout),...  22.3 us
    pallas_call x6, Pallas kernels, mirror_piece(): pl.pallas_call(kernel, in_specs=[SCALARS] + [WHOLE] * (len(given) - 1) +...  16.5 us
    ppermute x6, starting transfers between devices, send(): return lax.ppermute(piece, 'pair', perm)  10.1 us
    pallas_call x2, Pallas kernels, pack_pieces(): pl.pallas_call(kernel, in_specs=[SCALARS, WHOLE], out_specs=[SCALARS] * o...  9.54 us
    ppermute x6, waiting for transfers between devices, send(): return lax.ppermute(piece, 'pair', perm)  3.97 us
    pallas_call x2, Pallas kernels, turn(): pl.pallas_call(functools.partial(turn_kernel, marks), in_specs=[FAR], out...  3.1 us
  transfers between devices with their start and end apart: 6, of which 3 were waited for; matrix products, arithmetic and copies ran while one was open for 1% of the time, Pallas kernels for 51%

profile of v6, /device:TPU:0, one launch (start us, length us, event | category | flops | bytes accessed | tf_op | source)
XLA Modules:
  0.0 93.2 jit_solution(14589825938640084679)
XLA Ops:
  0.0 0.0 copy-start.2
  0.0 0.0 copy-start.3
  0.0 1.2 %turn.2 = bf16[1,192,1024]{2,1,0:T(8,128)(2,1)S(1)} custom-call(bf16[1,1024,1024]{2,1,0:T(8,128)(2,1)} %source.4), custom_call_target="tpu_custom_call" | custom-call | tf_op jit(solution)/shard_map/turn/pallas_call | solution.py:50
  1.2 0.0 copy-start
  1.3 4.1 %collective-permute-start.6 = (bf16[1,192,1024]{2,1,0:T(8,128)(2,1)S(1)}, bf16[1,192,1024]{2,1,0:T(8,128)(2,1)S(1)}, u32[]{:S(2)}, u32[]{:S(2)}) collective-permute-start(bf16[1,192,1024]{2,1,0:T(8,128)(2,1)S(1)} %turn.2), channel_id=1, source_target_pairs={{0,16},{4,20},{8,24},{12,28},{16,0},{20,4},{24,8},{28,12},{1,17},{... | collective-permute-start | bytes 1179656 | tf_op jit(solution)/shard_map/ppermute | solution.py:505
  5.4 1.9 %turn.3.turned = bf16[1,832,1024]{2,1,0:T(8,128)(2,1)S(1)} custom-call(bf16[1,1024,1024]{2,1,0:T(8,128)(2,1)} %source.4), custom_call_target="tpu_custom_call" | custom-call | tf_op jit(solution)/shard_map/turn/pallas_call | solution.py:50
  7.2 0.0 copy-start.1
  7.2 0.0 copy-done.2
  7.3 0.0 copy-done.3
  7.3 5.2 %all_gather.9.columns = s32[4,2,16]{2,1,0:T(2,128)S(1)} all-gather(s32[1,2,16]{2,1,0:T(2,128)S(1)} %pad_add_fusion), channel_id=1, replica_groups=mesh['pair'=8,'fac'=4] {'fac'}, dimensions={0}, use_global_device_ids=true | all-gather | bytes 640 | tf_op jit(solution)/shard_map/all_gather | solution.py:508
  12.5 5.7 %pack.2 = (s32[545]{0:T(1024)S(1)}, bf16[1,64,3072]{2,1,0:T(8,128)(2,1)S(1)}, bf16[1,64,1024]{2,1,0:T(8,128)(2,1)S(1)}) custom-call(s32[4,2,16]{2,1,0:T(2,128)S(1)} %all_gather.9.columns, bf16[1,832,1024]{2,1,0:T(8,128)(2,1)S(1)} %turn.3.turned), custom_call_target="tpu_custom_call" | custom-call | tf_op jit(solution)/shard_map/pack/pallas_call | solution.py:165
  18.2 0.6 slice.3
  19.4 0.1 collective-permute-start.5
  19.5 3.8 %pack.3 = (bf16[1,64,3072]{2,1,0:T(8,128)(2,1)S(1)}, bf16[1,64,3072]{2,1,0:T(8,128)(2,1)S(1)}, bf16[1,64,1792]{2,1,0:T(8,128)(2,1)S(1)}, bf16[1,64,1280]{2,1,0:T(8,128)(2,1)S(1)}) custom-call(s32[545]{0:T(1024)S(1)} %get-tuple-element.52.scalars.packing, bf16[1,832,1024]{2,1,0:T(8,128)(2,1)S(1)} %turn.3.turned), custom_call_target="tpu_custom_call" | custom-call | tf_op jit(solution)/shard_map/pack/pallas_call | solution.py:165
  23.4 0.0 copy-done
  23.4 10.4 %all_gather.10.d_all = bf16[4,16,64,64]{3,2,1,0:T(8,128)(2,1)S(1)} all-gather(bf16[1,16,64,64]{3,2,1,0:T(8,128)(2,1)S(1)} %copy-done), channel_id=1, replica_groups=mesh['pair'=8,'fac'=4] {'fac'}, dimensions={0}, use_global_device_ids=true | all-gather | bytes 655360 | tf_op jit(solution)/shard_map/all_gather | solution.py:508
  33.8 2.6 %collective-permute-start.4 = (bf16[1,64,3072]{2,1,0:T(8,128)(2,1)S(1)}, bf16[1,64,3072]{2,1,0:T(8,128)(2,1)S(1)}, u32[]{:S(2)}, u32[]{:S(2)}) collective-permute-start(bf16[1,64,3072]{2,1,0:T(8,128)(2,1)S(1)} %get-tuple-element.65), channel_id=1, source_target_pairs={{0,16},{4,20},{8,24},{12,28},{16,0},{20,4},{24,8},{28,12},{1,17},{... | collective-permute-start | bytes 1179656 | tf_op jit(solution)/shard_map/ppermute | solution.py:505
  36.3 0.0 copy-done.1
  36.3 9.9 %all_gather.11.b_all = bf16[4,16,64,64]{3,2,1,0:T(8,128)(2,1)S(1)} all-gather(bf16[1,16,64,64]{3,2,1,0:T(8,128)(2,1)S(1)} %copy-done.1), channel_id=1, replica_groups=mesh['pair'=8,'fac'=4] {'fac'}, dimensions={0}, use_global_device_ids=true | all-gather | bytes 655360 | tf_op jit(solution)/shard_map/all_gather | solution.py:508
  46.2 0.3 collective-permute-start.3
  47.2 22.3 %own.1 = (bf16[1024,1024]{1,0:T(8,128)(2,1)S(1)}, bf16[4,8,256,128]{3,2,1,0:T(8,128)(2,1)S(1)}, bf16[16,64,256]{2,1,0:T(8,128)(2,1)S(1)}, s32[478]{0:T(512)S(4)}) custom-call(s32[4,2,16]{2,1,0:T(2,128)S(1)} %all_gather.9.columns, s32[545]{0:T(1024)S(1)} %get-tuple-element.52.scalars.packing, s32[1]{0:T(128)S(6)} %copy.39.slot, ...), custom_call_target="tpu_custom_call" | custom-call | tf_op jit(solution)/shard_map/own/pallas_call | solution.py:337
  69.5 2.7 %collective-permute-start.2 = (bf16[1,64,1792]{2,1,0:T(8,128)(2,1)S(1)}, bf16[1,64,1792]{2,1,0:T(8,128)(2,1)S(1)}, u32[]{:S(2)}, u32[]{:S(2)}) collective-permute-start(bf16[1,64,1792]{2,1,0:T(8,128)(2,1)S(1)} %get-tuple-element.63), channel_id=1, source_target_pairs={{0,16},{4,20},{8,24},{12,28},{16,0},{20,4},{24,8},{28,12},{1,17},{... | collective-permute-start | bytes 688136 | tf_op jit(solution)/shard_map/ppermute | solution.py:505
  72.1 0.0 collective-permute-done.6.piece
  72.1 0.3 collective-permute-start.1
  72.5 2.0 %mirror.6 = (bf16[4,1024,1024]{2,1,0:T(8,128)(2,1)S(1)}, bf16[64,26624]{1,0:T(8,128)(2,1)S(1)}, bf16[1024,1024]{1,0:T(8,128)(2,1)}, f32[8,128]{1,0:T(8,128)}) custom-call(s32[478]{0:T(512)S(4)} %get-tuple-element.59.scalars, bf16[1,192,1024]{2,1,0:T(8,128)(2,1)S(1)} %collective-permute-done.6.piece, bf16[4,8,256,128]{3,2,1,0:T(8,128)(2,1)S(1)} %get-tuple-element.60.spread_d, ...), custom_call_target="tpu_custom_call" | custom-call | tf_op jit(solution)/shard_map/mirror/pallas_call | solution.py:470
  74.4 0.0 collective-permute-done.5.rest_0_
  74.5 2.3 %mirror.7 = (bf16[4,1024,1024]{2,1,0:T(8,128)(2,1)S(1)}, bf16[64,26624]{1,0:T(8,128)(2,1)S(1)}, bf16[1024,1024]{1,0:T(8,128)(2,1)}) custom-call(s32[478]{0:T(512)S(4)} %get-tuple-element.59.scalars, bf16[4,8,256,128]{3,2,1,0:T(8,128)(2,1)S(1)} %get-tuple-element.60.spread_d, ...), custom_call_target="tpu_custom_call", output_to_operand_aliasing={{0}: (6, {}), {1}: (7, {}), {2}: (8, {})} | custom-call | tf_op jit(solution)/shard_map/mirror/pallas_call | solution.py:470
  76.8 0.0 collective-permute-done.4.rest_0_
  76.8 3.2 %mirror.8 = (bf16[4,1024,1024]{2,1,0:T(8,128)(2,1)S(1)}, bf16[64,26624]{1,0:T(8,128)(2,1)S(1)}, bf16[1024,1024]{1,0:T(8,128)(2,1)}) custom-call(s32[478]{0:T(512)S(4)} %get-tuple-element.59.scalars, bf16[4,8,256,128]{3,2,1,0:T(8,128)(2,1)S(1)} %get-tuple-element.60.spread_d, ...), custom_call_target="tpu_custom_call", output_to_operand_aliasing={{0}: (5, {}), {1}: (6, {}), {2}: (7, {})} | custom-call | tf_op jit(solution)/shard_map/mirror/pallas_call | solution.py:470
  80.0 2.9 %collective-permute-done.3.rest_0_ = bf16[1,64,3072]{2,1,0:T(8,128)(2,1)S(1)} collective-permute-done((bf16[1,64,3072]{2,1,0:T(8,128)(2,1)S(1)}, bf16[1,64,3072]{2,1,0:T(8,128)(2,1)S(1)}, u32[]{:S(2)}, u32[]{:S(2)}) %collective-permute-start.3) | collective-permute-done | bytes 393248 | tf_op jit(solution)/shard_map/ppermute | solution.py:505
  82.9 4.1 %mirror.9 = (bf16[4,1024,1024]{2,1,0:T(8,128)(2,1)S(1)}, bf16[64,26624]{1,0:T(8,128)(2,1)S(1)}, bf16[1024,1024]{1,0:T(8,128)(2,1)}) custom-call(s32[478]{0:T(512)S(4)} %get-tuple-element.59.scalars, bf16[4,8,256,128]{3,2,1,0:T(8,128)(2,1)S(1)} %get-tuple-element.60.spread_d, ...), custom_call_target="tpu_custom_call", output_to_operand_aliasing={{0}: (5, {}), {1}: (6, {}), {2}: (7, {})} | custom-call | tf_op jit(solution)/shard_map/mirror/pallas_call | solution.py:470
  87.0 0.8 collective-permute-done.2.rest_0_
  87.8 2.7 %mirror.10 = (bf16[4,1024,1024]{2,1,0:T(8,128)(2,1)S(1)}, bf16[64,26624]{1,0:T(8,128)(2,1)S(1)}, bf16[1024,1024]{1,0:T(8,128)(2,1)}) custom-call(s32[478]{0:T(512)S(4)} %get-tuple-element.59.scalars, bf16[4,8,256,128]{3,2,1,0:T(8,128)(2,1)S(1)} %get-tuple-element.60.spread_d, ...), custom_call_target="tpu_custom_call", output_to_operand_aliasing={{0}: (5, {}), {1}: (6, {}), {2}: (7, {})} | custom-call | tf_op jit(solution)/shard_map/mirror/pallas_call | solution.py:470
  90.5 0.2 collective-permute-done.1.rest_0_
  90.7 2.3 %mirror.11 = (bf16[4,1024,1024]{2,1,0:T(8,128)(2,1)S(1)}, bf16[64,26624]{1,0:T(8,128)(2,1)S(1)}, bf16[1024,1024]{1,0:T(8,128)(2,1)}) custom-call(s32[478]{0:T(512)S(4)} %get-tuple-element.59.scalars, bf16[4,8,256,128]{3,2,1,0:T(8,128)(2,1)S(1)} %get-tuple-element.60.spread_d, ...), custom_call_target="tpu_custom_call", output_to_operand_aliasing={{0}: (5, {}), {1}: (6, {}), {2}: (7, {})} | custom-call | tf_op jit(solution)/shard_map/mirror/pallas_call | solution.py:470
  (2 shorter events, 0.0 us)
Async XLA Ops:
  0.0 7.2 %copy-start.2 = (s32[1,16]{1,0:T(1,128)S(1)}, s32[1,16]{1,0:T(1,128)}, u32[]{:S(2)}) copy-start(s32[1,16]{1,0:T(1,128)} %param.13) | copy-start | bytes 196
  0.0 7.3 %copy-start.3 = (s32[1,16]{1,0:T(1,128)S(1)}, s32[1,16]{1,0:T(1,128)}, u32[]{:S(2)}) copy-start(s32[1,16]{1,0:T(1,128)} %param.11) | copy-start | bytes 196
  1.2 22.1 %copy-start = (bf16[1,16,64,64]{3,2,1,0:T(8,128)(2,1)S(1)}, bf16[1,16,64,64]{3,2,1,0:T(8,128)(2,1)}, u32[]{:S(2)}) copy-start(bf16[1,16,64,64]{3,2,1,0:T(8,128)(2,1)} %param.10) | copy-start | bytes 393220
  1.3 70.9 %collective-permute-start.6 = (bf16[1,192,1024]{2,1,0:T(8,128)(2,1)S(1)}, bf16[1,192,1024]{2,1,0:T(8,128)(2,1)S(1)}, u32[]{:S(2)}, u32[]{:S(2)}) collective-permute-start(bf16[1,192,1024]{2,1,0:T(8,128)(2,1)S(1)} %turn.2), channel_id=1, source_target_pairs={{0,16},{4,20},{8,24},{12,28},{16,0},{20,4},{24,8},{28,12},{1,17},{... | collective-permute-start | bytes 1179656 | tf_op jit(solution)/shard_map/ppermute | solution.py:505
  7.2 29.1 %copy-start.1 = (bf16[1,16,64,64]{3,2,1,0:T(8,128)(2,1)S(1)}, bf16[1,16,64,64]{3,2,1,0:T(8,128)(2,1)}, u32[]{:S(2)}) copy-start(bf16[1,16,64,64]{3,2,1,0:T(8,128)(2,1)} %param.12) | copy-start | bytes 393220
  19.4 55.0 %collective-permute-start.5 = (bf16[1,64,3072]{2,1,0:T(8,128)(2,1)S(1)}, bf16[1,64,3072]{2,1,0:T(8,128)(2,1)S(1)}, u32[]{:S(2)}, u32[]{:S(2)}) collective-permute-start(bf16[1,64,3072]{2,1,0:T(8,128)(2,1)S(1)} %get-tuple-element.51), channel_id=1, source_target_pairs={{0,16},{4,20},{8,24},{12,28},{16,0},{20,4},{24,8},{28,12},{1,17},{... | collective-permute-start | bytes 1179656 | tf_op jit(solution)/shard_map/ppermute | solution.py:505
  33.8 43.0 %collective-permute-start.4 = (bf16[1,64,3072]{2,1,0:T(8,128)(2,1)S(1)}, bf16[1,64,3072]{2,1,0:T(8,128)(2,1)S(1)}, u32[]{:S(2)}, u32[]{:S(2)}) collective-permute-start(bf16[1,64,3072]{2,1,0:T(8,128)(2,1)S(1)} %get-tuple-element.65), channel_id=1, source_target_pairs={{0,16},{4,20},{8,24},{12,28},{16,0},{20,4},{24,8},{28,12},{1,17},{... | collective-permute-start | bytes 1179656 | tf_op jit(solution)/shard_map/ppermute | solution.py:505
  46.2 36.7 %collective-permute-start.3 = (bf16[1,64,3072]{2,1,0:T(8,128)(2,1)S(1)}, bf16[1,64,3072]{2,1,0:T(8,128)(2,1)S(1)}, u32[]{:S(2)}, u32[]{:S(2)}) collective-permute-start(bf16[1,64,3072]{2,1,0:T(8,128)(2,1)S(1)} %get-tuple-element.64), channel_id=1, source_target_pairs={{0,16},{4,20},{8,24},{12,28},{16,0},{20,4},{24,8},{28,12},{1,17},{... | collective-permute-start | bytes 1179656 | tf_op jit(solution)/shard_map/ppermute | solution.py:505
  69.5 18.4 %collective-permute-start.2 = (bf16[1,64,1792]{2,1,0:T(8,128)(2,1)S(1)}, bf16[1,64,1792]{2,1,0:T(8,128)(2,1)S(1)}, u32[]{:S(2)}, u32[]{:S(2)}) collective-permute-start(bf16[1,64,1792]{2,1,0:T(8,128)(2,1)S(1)} %get-tuple-element.63), channel_id=1, source_target_pairs={{0,16},{4,20},{8,24},{12,28},{16,0},{20,4},{24,8},{28,12},{1,17},{... | collective-permute-start | bytes 688136 | tf_op jit(solution)/shard_map/ppermute | solution.py:505
  72.1 18.6 %collective-permute-start.1 = (bf16[1,64,1280]{2,1,0:T(8,128)(2,1)S(1)}, bf16[1,64,1280]{2,1,0:T(8,128)(2,1)S(1)}, u32[]{:S(2)}, u32[]{:S(2)}) collective-permute-start(bf16[1,64,1280]{2,1,0:T(8,128)(2,1)S(1)} %get-tuple-element.56), channel_id=1, source_target_pairs={{0,16},{4,20},{8,24},{12,28},{16,0},{20,4},{24,8},{28,12},{1,17},{... | collective-permute-start | bytes 491528 | tf_op jit(solution)/shard_map/ppermute | solution.py:505

commit v7 on v6

--- a/solution.py
+++ b/solution.py
@@ -133,11 +133,10 @@
     left, right = lax.fori_loop(0, blocks, count, (none, none))
 
     def select(at, used):
-        def better(c, best):
-            wins = tally[c] > best[0]
-            return jnp.where(wins, tally[c], best[0]), jnp.where(wins, c, best[1])
-
-        c = lax.fori_loop(fixed, blocks, better, (jnp.int32(-1), jnp.int32(fixed)))[1]
+        most, c = tally[fixed], jnp.int32(fixed)
+        for other in range(fixed + 1, blocks):
+            n = tally[other]
+            most, c = jnp.maximum(most, n), jnp.where(n > most, other, c)
         tally[c] = -2
         scalars[layout.place + c] = at
         scalars[layout.used + at] = used
@@ -482,7 +481,7 @@
 def cuts(blocks):
     fixed = 3 * blocks // 16
     slots = (blocks - fixed) * blocks
-    return fixed, [slots * m // 208 // 2 * 2 for m in (0, 48, 96, 144, 172, 192)], slots
+    return fixed, [slots * m // 208 // 2 * 2 for m in (0, 48, 96, 144, 176, 196)], slots
 
 
 def later(arrays, *after):

time: 93.2 us -> 95.2 us (1.021)
  waiting for transfers between devices: 3.97 us -> 5.72 us
    ppermute x6, waiting for transfers between devices: 3.97 us -> 5.72 us  [send(): return lax.ppermute(piece, 'pair', perm)]
    pallas_call x2, Pallas kernels: 9.54 us -> 7.8 us  [pack_pieces(): pl.pallas_call(kernel, in_specs=[SCALARS, WHOLE], out_specs=[SCALARS] * o...]
    pallas_call x6, Pallas kernels: 16.5 us -> 18.1 us  [mirror_piece(): pl.pallas_call(kernel, in_specs=[SCALARS] + [WHOLE] * (len(given) - 1) +...]
  transfers between devices with their start and end apart: 6 -> 6, of which waited for: 3 -> 2; matrix products, arithmetic and copies ran while one was open for 1% -> 1% of each run, Pallas kernels for 51% -> 51%
where the time goes in v7:
time: 95.2 us; the launch traced here: 94.8 us
  Pallas kernels  51.3 us (54%)
  blocking collectives  25.4 us (27%)
  starting transfers between devices  10.1 us (11%)
  waiting for transfers between devices  5.72 us (6%)
  between operations  1.62 us (2%)
    all_gather x3, blocking collectives, gather(): return lax.all_gather(array, 'fac', axis=0, tiled=True)  25.4 us
    pallas_call x1, Pallas kernels, own_pair(): pl.pallas_call(functools.partial(own_kernel, fixed, ends, plan, layout),...  22.3 us
    pallas_call x6, Pallas kernels, mirror_piece(): pl.pallas_call(kernel, in_specs=[SCALARS] + [WHOLE] * (len(given) - 1) +...  18.1 us
    ppermute x6, starting transfers between devices, send(): return lax.ppermute(piece, 'pair', perm)  10.1 us
    pallas_call x2, Pallas kernels, pack_pieces(): pl.pallas_call(kernel, in_specs=[SCALARS, WHOLE], out_specs=[SCALARS] * o...  7.8 us
    ppermute x6, waiting for transfers between devices, send(): return lax.ppermute(piece, 'pair', perm)  5.72 us
    pallas_call x2, Pallas kernels, turn(): pl.pallas_call(functools.partial(turn_kernel, marks), in_specs=[FAR], out...  3.1 us
  transfers between devices with their start and end apart: 6, of which 2 were waited for; matrix products, arithmetic and copies ran while one was open for 1% of the time, Pallas kernels for 51%

profile of v7, /device:TPU:0, one launch (start us, length us, event | category | flops | bytes accessed | tf_op | source)
XLA Modules:
  0.0 94.8 jit_solution(3840151179654526878)
XLA Ops:
  0.0 0.0 copy-start.2
  0.0 0.0 copy-start.3
  0.0 1.2 %turn.2 = bf16[1,192,1024]{2,1,0:T(8,128)(2,1)S(1)} custom-call(bf16[1,1024,1024]{2,1,0:T(8,128)(2,1)} %source.4), custom_call_target="tpu_custom_call" | custom-call | tf_op jit(solution)/shard_map/turn/pallas_call | solution.py:50
  1.2 0.0 copy-start
  1.3 4.1 %collective-permute-start.6 = (bf16[1,192,1024]{2,1,0:T(8,128)(2,1)S(1)}, bf16[1,192,1024]{2,1,0:T(8,128)(2,1)S(1)}, u32[]{:S(2)}, u32[]{:S(2)}) collective-permute-start(bf16[1,192,1024]{2,1,0:T(8,128)(2,1)S(1)} %turn.2), channel_id=1, source_target_pairs={{0,16},{4,20},{8,24},{12,28},{16,0},{20,4},{24,8},{28,12},{1,17},{... | collective-permute-start | bytes 1179656 | tf_op jit(solution)/shard_map/ppermute | solution.py:504
  5.4 1.9 %turn.3.turned = bf16[1,832,1024]{2,1,0:T(8,128)(2,1)S(1)} custom-call(bf16[1,1024,1024]{2,1,0:T(8,128)(2,1)} %source.4), custom_call_target="tpu_custom_call" | custom-call | tf_op jit(solution)/shard_map/turn/pallas_call | solution.py:50
  7.2 0.0 copy-start.1
  7.2 0.0 copy-done.2
  7.3 0.0 copy-done.3
  7.3 5.2 %all_gather.9.columns = s32[4,2,16]{2,1,0:T(2,128)S(1)} all-gather(s32[1,2,16]{2,1,0:T(2,128)S(1)} %pad_add_fusion), channel_id=1, replica_groups=mesh['pair'=8,'fac'=4] {'fac'}, dimensions={0}, use_global_device_ids=true | all-gather | bytes 640 | tf_op jit(solution)/shard_map/all_gather | solution.py:507
  12.5 4.1 %pack.2 = (s32[545]{0:T(1024)S(1)}, bf16[1,64,3072]{2,1,0:T(8,128)(2,1)S(1)}, bf16[1,64,768]{2,1,0:T(8,128)(2,1)S(1)}) custom-call(s32[4,2,16]{2,1,0:T(2,128)S(1)} %all_gather.9.columns, bf16[1,832,1024]{2,1,0:T(8,128)(2,1)S(1)} %turn.3.turned), custom_call_target="tpu_custom_call" | custom-call | tf_op jit(solution)/shard_map/pack/pallas_call | solution.py:164
  16.6 0.6 slice.3
  17.9 0.1 collective-permute-start.5
  17.9 3.7 %pack.3 = (bf16[1,64,3072]{2,1,0:T(8,128)(2,1)S(1)}, bf16[1,64,3072]{2,1,0:T(8,128)(2,1)S(1)}, bf16[1,64,2048]{2,1,0:T(8,128)(2,1)S(1)}, bf16[1,64,1280]{2,1,0:T(8,128)(2,1)S(1)}) custom-call(s32[545]{0:T(1024)S(1)} %get-tuple-element.52.scalars.packing, bf16[1,832,1024]{2,1,0:T(8,128)(2,1)S(1)} %turn.3.turned), custom_call_target="tpu_custom_call" | custom-call | tf_op jit(solution)/shard_map/pack/pallas_call | solution.py:164
  21.6 0.0 copy-done
  21.6 10.4 %all_gather.10.d_all = bf16[4,16,64,64]{3,2,1,0:T(8,128)(2,1)S(1)} all-gather(bf16[1,16,64,64]{3,2,1,0:T(8,128)(2,1)S(1)} %copy-done), channel_id=1, replica_groups=mesh['pair'=8,'fac'=4] {'fac'}, dimensions={0}, use_global_device_ids=true | all-gather | bytes 655360 | tf_op jit(solution)/shard_map/all_gather | solution.py:507
  32.0 2.6 %collective-permute-start.4 = (bf16[1,64,3072]{2,1,0:T(8,128)(2,1)S(1)}, bf16[1,64,3072]{2,1,0:T(8,128)(2,1)S(1)}, u32[]{:S(2)}, u32[]{:S(2)}) collective-permute-start(bf16[1,64,3072]{2,1,0:T(8,128)(2,1)S(1)} %get-tuple-element.65), channel_id=1, source_target_pairs={{0,16},{4,20},{8,24},{12,28},{16,0},{20,4},{24,8},{28,12},{1,17},{... | collective-permute-start | bytes 1179656 | tf_op jit(solution)/shard_map/ppermute | solution.py:504
  34.6 0.0 copy-done.1
  34.6 9.9 %all_gather.11.b_all = bf16[4,16,64,64]{3,2,1,0:T(8,128)(2,1)S(1)} all-gather(bf16[1,16,64,64]{3,2,1,0:T(8,128)(2,1)S(1)} %copy-done.1), channel_id=1, replica_groups=mesh['pair'=8,'fac'=4] {'fac'}, dimensions={0}, use_global_device_ids=true | all-gather | bytes 655360 | tf_op jit(solution)/shard_map/all_gather | solution.py:507
  44.5 0.3 collective-permute-start.3
  45.4 22.3 %own.1 = (bf16[1024,1024]{1,0:T(8,128)(2,1)S(1)}, bf16[4,8,256,128]{3,2,1,0:T(8,128)(2,1)S(1)}, bf16[16,64,256]{2,1,0:T(8,128)(2,1)S(1)}, s32[478]{0:T(512)S(4)}) custom-call(s32[4,2,16]{2,1,0:T(2,128)S(1)} %all_gather.9.columns, s32[545]{0:T(1024)S(1)} %get-tuple-element.52.scalars.packing, s32[1]{0:T(128)S(6)} %copy.39.slot, ...), custom_call_target="tpu_custom_call" | custom-call | tf_op jit(solution)/shard_map/own/pallas_call | solution.py:336
  67.8 2.7 %collective-permute-start.2 = (bf16[1,64,2048]{2,1,0:T(8,128)(2,1)S(1)}, bf16[1,64,2048]{2,1,0:T(8,128)(2,1)S(1)}, u32[]{:S(2)}, u32[]{:S(2)}) collective-permute-start(bf16[1,64,2048]{2,1,0:T(8,128)(2,1)S(1)} %get-tuple-element.63), channel_id=1, source_target_pairs={{0,16},{4,20},{8,24},{12,28},{16,0},{20,4},{24,8},{28,12},{1,17},{... | collective-permute-start | bytes 786440 | tf_op jit(solution)/shard_map/ppermute | solution.py:504
  70.4 0.0 collective-permute-done.6.piece
  70.4 0.3 collective-permute-start.1
  70.8 2.0 %mirror.6 = (bf16[4,1024,1024]{2,1,0:T(8,128)(2,1)S(1)}, bf16[64,26624]{1,0:T(8,128)(2,1)S(1)}, bf16[1024,1024]{1,0:T(8,128)(2,1)}, f32[8,128]{1,0:T(8,128)}) custom-call(s32[478]{0:T(512)S(4)} %get-tuple-element.59.scalars, bf16[1,192,1024]{2,1,0:T(8,128)(2,1)S(1)} %collective-permute-done.6.piece, bf16[4,8,256,128]{3,2,1,0:T(8,128)(2,1)S(1)} %get-tuple-element.60.spread_d, ...), custom_call_target="tpu_custom_call" | custom-call | tf_op jit(solution)/shard_map/mirror/pallas_call | solution.py:469
  72.7 0.0 collective-permute-done.5.rest_0_
  72.8 3.2 %mirror.7 = (bf16[4,1024,1024]{2,1,0:T(8,128)(2,1)S(1)}, bf16[64,26624]{1,0:T(8,128)(2,1)S(1)}, bf16[1024,1024]{1,0:T(8,128)(2,1)}) custom-call(s32[478]{0:T(512)S(4)} %get-tuple-element.59.scalars, bf16[4,8,256,128]{3,2,1,0:T(8,128)(2,1)S(1)} %get-tuple-element.60.spread_d, ...), custom_call_target="tpu_custom_call", output_to_operand_aliasing={{0}: (6, {}), {1}: (7, {}), {2}: (8, {})} | custom-call | tf_op jit(solution)/shard_map/mirror/pallas_call | solution.py:469
  76.0 0.0 collective-permute-done.4.rest_0_
  76.0 3.5 %mirror.8 = (bf16[4,1024,1024]{2,1,0:T(8,128)(2,1)S(1)}, bf16[64,26624]{1,0:T(8,128)(2,1)S(1)}, bf16[1024,1024]{1,0:T(8,128)(2,1)}) custom-call(s32[478]{0:T(512)S(4)} %get-tuple-element.59.scalars, bf16[4,8,256,128]{3,2,1,0:T(8,128)(2,1)S(1)} %get-tuple-element.60.spread_d, ...), custom_call_target="tpu_custom_call", output_to_operand_aliasing={{0}: (5, {}), {1}: (6, {}), {2}: (7, {})} | custom-call | tf_op jit(solution)/shard_map/mirror/pallas_call | solution.py:469
  79.6 3.9 %collective-permute-done.3.rest_0_ = bf16[1,64,3072]{2,1,0:T(8,128)(2,1)S(1)} collective-permute-done((bf16[1,64,3072]{2,1,0:T(8,128)(2,1)S(1)}, bf16[1,64,3072]{2,1,0:T(8,128)(2,1)S(1)}, u32[]{:S(2)}, u32[]{:S(2)}) %collective-permute-start.3) | collective-permute-done | bytes 393248 | tf_op jit(solution)/shard_map/ppermute | solution.py:504
  83.4 3.8 %mirror.9 = (bf16[4,1024,1024]{2,1,0:T(8,128)(2,1)S(1)}, bf16[64,26624]{1,0:T(8,128)(2,1)S(1)}, bf16[1024,1024]{1,0:T(8,128)(2,1)}) custom-call(s32[478]{0:T(512)S(4)} %get-tuple-element.59.scalars, bf16[4,8,256,128]{3,2,1,0:T(8,128)(2,1)S(1)} %get-tuple-element.60.spread_d, ...), custom_call_target="tpu_custom_call", output_to_operand_aliasing={{0}: (5, {}), {1}: (6, {}), {2}: (7, {})} | custom-call | tf_op jit(solution)/shard_map/mirror/pallas_call | solution.py:469
  87.2 1.9 %collective-permute-done.2.rest_0_ = bf16[1,64,2048]{2,1,0:T(8,128)(2,1)S(1)} collective-permute-done((bf16[1,64,2048]{2,1,0:T(8,128)(2,1)S(1)}, bf16[1,64,2048]{2,1,0:T(8,128)(2,1)S(1)}, u32[]{:S(2)}, u32[]{:S(2)}) %collective-permute-start.2) | collective-permute-done | bytes 262176 | tf_op jit(solution)/shard_map/ppermute | solution.py:504
  89.0 3.6 %mirror.10 = (bf16[4,1024,1024]{2,1,0:T(8,128)(2,1)S(1)}, bf16[64,26624]{1,0:T(8,128)(2,1)S(1)}, bf16[1024,1024]{1,0:T(8,128)(2,1)}) custom-call(s32[478]{0:T(512)S(4)} %get-tuple-element.59.scalars, bf16[4,8,256,128]{3,2,1,0:T(8,128)(2,1)S(1)} %get-tuple-element.60.spread_d, ...), custom_call_target="tpu_custom_call", output_to_operand_aliasing={{0}: (5, {}), {1}: (6, {}), {2}: (7, {})} | custom-call | tf_op jit(solution)/shard_map/mirror/pallas_call | solution.py:469
  92.7 0.0 collective-permute-done.1.rest_0_
  92.7 2.0 %mirror.11 = (bf16[4,1024,1024]{2,1,0:T(8,128)(2,1)S(1)}, bf16[64,26624]{1,0:T(8,128)(2,1)S(1)}, bf16[1024,1024]{1,0:T(8,128)(2,1)}) custom-call(s32[478]{0:T(512)S(4)} %get-tuple-element.59.scalars, bf16[4,8,256,128]{3,2,1,0:T(8,128)(2,1)S(1)} %get-tuple-element.60.spread_d, ...), custom_call_target="tpu_custom_call", output_to_operand_aliasing={{0}: (5, {}), {1}: (6, {}), {2}: (7, {})} | custom-call | tf_op jit(solution)/shard_map/mirror/pallas_call | solution.py:469
  (2 shorter events, 0.0 us)
Async XLA Ops:
  0.0 7.2 %copy-start.2 = (s32[1,16]{1,0:T(1,128)S(1)}, s32[1,16]{1,0:T(1,128)}, u32[]{:S(2)}) copy-start(s32[1,16]{1,0:T(1,128)} %param.13) | copy-start | bytes 196
  0.0 7.3 %copy-start.3 = (s32[1,16]{1,0:T(1,128)S(1)}, s32[1,16]{1,0:T(1,128)}, u32[]{:S(2)}) copy-start(s32[1,16]{1,0:T(1,128)} %param.11) | copy-start | bytes 196
  1.2 20.4 %copy-start = (bf16[1,16,64,64]{3,2,1,0:T(8,128)(2,1)S(1)}, bf16[1,16,64,64]{3,2,1,0:T(8,128)(2,1)}, u32[]{:S(2)}) copy-start(bf16[1,16,64,64]{3,2,1,0:T(8,128)(2,1)} %param.10) | copy-start | bytes 393220
  1.3 69.2 %collective-permute-start.6 = (bf16[1,192,1024]{2,1,0:T(8,128)(2,1)S(1)}, bf16[1,192,1024]{2,1,0:T(8,128)(2,1)S(1)}, u32[]{:S(2)}, u32[]{:S(2)}) collective-permute-start(bf16[1,192,1024]{2,1,0:T(8,128)(2,1)S(1)} %turn.2), channel_id=1, source_target_pairs={{0,16},{4,20},{8,24},{12,28},{16,0},{20,4},{24,8},{28,12},{1,17},{... | collective-permute-start | bytes 1179656 | tf_op jit(solution)/shard_map/ppermute | solution.py:504
  7.2 27.4 %copy-start.1 = (bf16[1,16,64,64]{3,2,1,0:T(8,128)(2,1)S(1)}, bf16[1,16,64,64]{3,2,1,0:T(8,128)(2,1)}, u32[]{:S(2)}) copy-start(bf16[1,16,64,64]{3,2,1,0:T(8,128)(2,1)} %param.12) | copy-start | bytes 393220
  17.9 54.9 %collective-permute-start.5 = (bf16[1,64,3072]{2,1,0:T(8,128)(2,1)S(1)}, bf16[1,64,3072]{2,1,0:T(8,128)(2,1)S(1)}, u32[]{:S(2)}, u32[]{:S(2)}) collective-permute-start(bf16[1,64,3072]{2,1,0:T(8,128)(2,1)S(1)} %get-tuple-element.51), channel_id=1, source_target_pairs={{0,16},{4,20},{8,24},{12,28},{16,0},{20,4},{24,8},{28,12},{1,17},{... | collective-permute-start | bytes 1179656 | tf_op jit(solution)/shard_map/ppermute | solution.py:504
  32.0 44.0 %collective-permute-start.4 = (bf16[1,64,3072]{2,1,0:T(8,128)(2,1)S(1)}, bf16[1,64,3072]{2,1,0:T(8,128)(2,1)S(1)}, u32[]{:S(2)}, u32[]{:S(2)}) collective-permute-start(bf16[1,64,3072]{2,1,0:T(8,128)(2,1)S(1)} %get-tuple-element.65), channel_id=1, source_target_pairs={{0,16},{4,20},{8,24},{12,28},{16,0},{20,4},{24,8},{28,12},{1,17},{... | collective-permute-start | bytes 1179656 | tf_op jit(solution)/shard_map/ppermute | solution.py:504
  44.5 39.0 %collective-permute-start.3 = (bf16[1,64,3072]{2,1,0:T(8,128)(2,1)S(1)}, bf16[1,64,3072]{2,1,0:T(8,128)(2,1)S(1)}, u32[]{:S(2)}, u32[]{:S(2)}) collective-permute-start(bf16[1,64,3072]{2,1,0:T(8,128)(2,1)S(1)} %get-tuple-element.64), channel_id=1, source_target_pairs={{0,16},{4,20},{8,24},{12,28},{16,0},{20,4},{24,8},{28,12},{1,17},{... | collective-permute-start | bytes 1179656 | tf_op jit(solution)/shard_map/ppermute | solution.py:504
  67.8 21.3 %collective-permute-start.2 = (bf16[1,64,2048]{2,1,0:T(8,128)(2,1)S(1)}, bf16[1,64,2048]{2,1,0:T(8,128)(2,1)S(1)}, u32[]{:S(2)}, u32[]{:S(2)}) collective-permute-start(bf16[1,64,2048]{2,1,0:T(8,128)(2,1)S(1)} %get-tuple-element.63), channel_id=1, source_target_pairs={{0,16},{4,20},{8,24},{12,28},{16,0},{20,4},{24,8},{28,12},{1,17},{... | collective-permute-start | bytes 786440 | tf_op jit(solution)/shard_map/ppermute | solution.py:504
  70.4 22.3 %collective-permute-start.1 = (bf16[1,64,1280]{2,1,0:T(8,128)(2,1)S(1)}, bf16[1,64,1280]{2,1,0:T(8,128)(2,1)S(1)}, u32[]{:S(2)}, u32[]{:S(2)}) collective-permute-start(bf16[1,64,1280]{2,1,0:T(8,128)(2,1)S(1)} %get-tuple-element.56), channel_id=1, source_target_pairs={{0,16},{4,20},{8,24},{12,28},{16,0},{20,4},{24,8},{28,12},{1,17},{... | collective-permute-start | bytes 491528 | tf_op jit(solution)/shard_map/ppermute | solution.py:504

commit v8 on v7

--- a/solution.py
+++ b/solution.py
@@ -427,7 +427,7 @@
                 row[n * width : (n + 1) * width, k * width : (k + 2) * width] = jnp.where(left_half, *tiles)
         for q in range(factors):
             uses = plan.uses + q * blocks + first
-            skip = last and scalars[uses] + scalars[uses + 1] == 0
+            skip = last and jnp.where(first >= before, scalars[uses], 0) + scalars[uses + 1] == 0
 
             def right(q=q):
                 apply_right(

time: 95.2 us -> 93.7 us (0.984)
  Pallas kernels: 51.3 us -> 50.2 us
    pallas_call x6, Pallas kernels: 18.1 us -> 17.1 us  [mirror_piece(): pl.pallas_call(kernel, in_specs=[SCALARS] + [WHOLE] * (len(given) - 1) +...]
  transfers between devices with their start and end apart: 6 -> 6, of which waited for: 2 -> 2; matrix products, arithmetic and copies ran while one was open for 1% -> 1% of each run, Pallas kernels for 51% -> 50%
where the time goes in v8:
time: 93.7 us; the launch traced here: 93.8 us
  Pallas kernels  50.2 us (54%)
  blocking collectives  25.4 us (27%)
  starting transfers between devices  10.1 us (11%)
  waiting for transfers between devices  5.82 us (6%)
  between operations  1.62 us (2%)
    all_gather x3, blocking collectives, gather(): return lax.all_gather(array, 'fac', axis=0, tiled=True)  25.4 us
    pallas_call x1, Pallas kernels, own_pair(): pl.pallas_call(functools.partial(own_kernel, fixed, ends, plan, layout),...  22.3 us
    pallas_call x6, Pallas kernels, mirror_piece(): pl.pallas_call(kernel, in_specs=[SCALARS] + [WHOLE] * (len(given) - 1) +...  17.1 us
    ppermute x6, starting transfers between devices, send(): return lax.ppermute(piece, 'pair', perm)  10.1 us
    pallas_call x2, Pallas kernels, pack_pieces(): pl.pallas_call(kernel, in_specs=[SCALARS, WHOLE], out_specs=[SCALARS] * o...  7.8 us
    ppermute x6, waiting for transfers between devices, send(): return lax.ppermute(piece, 'pair', perm)  5.82 us
    pallas_call x2, Pallas kernels, turn(): pl.pallas_call(functools.partial(turn_kernel, marks), in_specs=[FAR], out...  3.1 us
  transfers between devices with their start and end apart: 6, of which 2 were waited for; matrix products, arithmetic and copies ran while one was open for 1% of the time, Pallas kernels for 50%

profile of v8, /device:TPU:0, one launch (start us, length us, event | category | flops | bytes accessed | tf_op | source)
XLA Modules:
  0.0 93.8 jit_solution(16582823990782962719)
XLA Ops:
  0.0 0.0 copy-start.2
  0.0 0.0 copy-start.3
  0.0 1.2 %turn.2 = bf16[1,192,1024]{2,1,0:T(8,128)(2,1)S(1)} custom-call(bf16[1,1024,1024]{2,1,0:T(8,128)(2,1)} %source.4), custom_call_target="tpu_custom_call" | custom-call | tf_op jit(solution)/shard_map/turn/pallas_call | solution.py:50
  1.2 0.0 copy-start
  1.3 4.1 %collective-permute-start.6 = (bf16[1,192,1024]{2,1,0:T(8,128)(2,1)S(1)}, bf16[1,192,1024]{2,1,0:T(8,128)(2,1)S(1)}, u32[]{:S(2)}, u32[]{:S(2)}) collective-permute-start(bf16[1,192,1024]{2,1,0:T(8,128)(2,1)S(1)} %turn.2), channel_id=1, source_target_pairs={{0,16},{4,20},{8,24},{12,28},{16,0},{20,4},{24,8},{28,12},{1,17},{... | collective-permute-start | bytes 1179656 | tf_op jit(solution)/shard_map/ppermute | solution.py:504
  5.4 1.9 %turn.3.turned = bf16[1,832,1024]{2,1,0:T(8,128)(2,1)S(1)} custom-call(bf16[1,1024,1024]{2,1,0:T(8,128)(2,1)} %source.4), custom_call_target="tpu_custom_call" | custom-call | tf_op jit(solution)/shard_map/turn/pallas_call | solution.py:50
  7.2 0.0 copy-start.1
  7.2 0.0 copy-done.2
  7.3 0.0 copy-done.3
  7.3 5.2 %all_gather.9.columns = s32[4,2,16]{2,1,0:T(2,128)S(1)} all-gather(s32[1,2,16]{2,1,0:T(2,128)S(1)} %pad_add_fusion), channel_id=1, replica_groups=mesh['pair'=8,'fac'=4] {'fac'}, dimensions={0}, use_global_device_ids=true | all-gather | bytes 640 | tf_op jit(solution)/shard_map/all_gather | solution.py:507
  12.5 4.1 %pack.2 = (s32[545]{0:T(1024)S(1)}, bf16[1,64,3072]{2,1,0:T(8,128)(2,1)S(1)}, bf16[1,64,768]{2,1,0:T(8,128)(2,1)S(1)}) custom-call(s32[4,2,16]{2,1,0:T(2,128)S(1)} %all_gather.9.columns, bf16[1,832,1024]{2,1,0:T(8,128)(2,1)S(1)} %turn.3.turned), custom_call_target="tpu_custom_call" | custom-call | tf_op jit(solution)/shard_map/pack/pallas_call | solution.py:164
  16.6 0.6 slice.3
  17.9 0.1 collective-permute-start.5
  17.9 3.7 %pack.3 = (bf16[1,64,3072]{2,1,0:T(8,128)(2,1)S(1)}, bf16[1,64,3072]{2,1,0:T(8,128)(2,1)S(1)}, bf16[1,64,2048]{2,1,0:T(8,128)(2,1)S(1)}, bf16[1,64,1280]{2,1,0:T(8,128)(2,1)S(1)}) custom-call(s32[545]{0:T(1024)S(1)} %get-tuple-element.52.scalars.packing, bf16[1,832,1024]{2,1,0:T(8,128)(2,1)S(1)} %turn.3.turned), custom_call_target="tpu_custom_call" | custom-call | tf_op jit(solution)/shard_map/pack/pallas_call | solution.py:164
  21.6 0.0 copy-done
  21.6 10.4 %all_gather.10.d_all = bf16[4,16,64,64]{3,2,1,0:T(8,128)(2,1)S(1)} all-gather(bf16[1,16,64,64]{3,2,1,0:T(8,128)(2,1)S(1)} %copy-done), channel_id=1, replica_groups=mesh['pair'=8,'fac'=4] {'fac'}, dimensions={0}, use_global_device_ids=true | all-gather | bytes 655360 | tf_op jit(solution)/shard_map/all_gather | solution.py:507
  32.0 2.6 %collective-permute-start.4 = (bf16[1,64,3072]{2,1,0:T(8,128)(2,1)S(1)}, bf16[1,64,3072]{2,1,0:T(8,128)(2,1)S(1)}, u32[]{:S(2)}, u32[]{:S(2)}) collective-permute-start(bf16[1,64,3072]{2,1,0:T(8,128)(2,1)S(1)} %get-tuple-element.65), channel_id=1, source_target_pairs={{0,16},{4,20},{8,24},{12,28},{16,0},{20,4},{24,8},{28,12},{1,17},{... | collective-permute-start | bytes 1179656 | tf_op jit(solution)/shard_map/ppermute | solution.py:504
  34.6 0.0 copy-done.1
  34.6 9.9 %all_gather.11.b_all = bf16[4,16,64,64]{3,2,1,0:T(8,128)(2,1)S(1)} all-gather(bf16[1,16,64,64]{3,2,1,0:T(8,128)(2,1)S(1)} %copy-done.1), channel_id=1, replica_groups=mesh['pair'=8,'fac'=4] {'fac'}, dimensions={0}, use_global_device_ids=true | all-gather | bytes 655360 | tf_op jit(solution)/shard_map/all_gather | solution.py:507
  44.5 0.3 collective-permute-start.3
  45.4 22.3 %own.1 = (bf16[1024,1024]{1,0:T(8,128)(2,1)S(1)}, bf16[4,8,256,128]{3,2,1,0:T(8,128)(2,1)S(1)}, bf16[16,64,256]{2,1,0:T(8,128)(2,1)S(1)}, s32[478]{0:T(512)S(4)}) custom-call(s32[4,2,16]{2,1,0:T(2,128)S(1)} %all_gather.9.columns, s32[545]{0:T(1024)S(1)} %get-tuple-element.52.scalars.packing, s32[1]{0:T(128)S(6)} %copy.39.slot, ...), custom_call_target="tpu_custom_call" | custom-call | tf_op jit(solution)/shard_map/own/pallas_call | solution.py:336
  67.7 2.6 %collective-permute-start.2 = (bf16[1,64,2048]{2,1,0:T(8,128)(2,1)S(1)}, bf16[1,64,2048]{2,1,0:T(8,128)(2,1)S(1)}, u32[]{:S(2)}, u32[]{:S(2)}) collective-permute-start(bf16[1,64,2048]{2,1,0:T(8,128)(2,1)S(1)} %get-tuple-element.63), channel_id=1, source_target_pairs={{0,16},{4,20},{8,24},{12,28},{16,0},{20,4},{24,8},{28,12},{1,17},{... | collective-permute-start | bytes 786440 | tf_op jit(solution)/shard_map/ppermute | solution.py:504
  70.4 0.0 collective-permute-done.6.piece
  70.4 0.3 collective-permute-start.1
  70.7 2.0 %mirror.6 = (bf16[4,1024,1024]{2,1,0:T(8,128)(2,1)S(1)}, bf16[64,26624]{1,0:T(8,128)(2,1)S(1)}, bf16[1024,1024]{1,0:T(8,128)(2,1)}, f32[8,128]{1,0:T(8,128)}) custom-call(s32[478]{0:T(512)S(4)} %get-tuple-element.59.scalars, bf16[1,192,1024]{2,1,0:T(8,128)(2,1)S(1)} %collective-permute-done.6.piece, bf16[4,8,256,128]{3,2,1,0:T(8,128)(2,1)S(1)} %get-tuple-element.60.spread_d, ...), custom_call_target="tpu_custom_call" | custom-call | tf_op jit(solution)/shard_map/mirror/pallas_call | solution.py:469
  72.7 0.0 collective-permute-done.5.rest_0_
  72.7 3.2 %mirror.7 = (bf16[4,1024,1024]{2,1,0:T(8,128)(2,1)S(1)}, bf16[64,26624]{1,0:T(8,128)(2,1)S(1)}, bf16[1024,1024]{1,0:T(8,128)(2,1)}) custom-call(s32[478]{0:T(512)S(4)} %get-tuple-element.59.scalars, bf16[4,8,256,128]{3,2,1,0:T(8,128)(2,1)S(1)} %get-tuple-element.60.spread_d, ...), custom_call_target="tpu_custom_call", output_to_operand_aliasing={{0}: (6, {}), {1}: (7, {}), {2}: (8, {})} | custom-call | tf_op jit(solution)/shard_map/mirror/pallas_call | solution.py:469
  75.9 0.0 collective-permute-done.4.rest_0_
  75.9 3.8 %mirror.8 = (bf16[4,1024,1024]{2,1,0:T(8,128)(2,1)S(1)}, bf16[64,26624]{1,0:T(8,128)(2,1)S(1)}, bf16[1024,1024]{1,0:T(8,128)(2,1)}) custom-call(s32[478]{0:T(512)S(4)} %get-tuple-element.59.scalars, bf16[4,8,256,128]{3,2,1,0:T(8,128)(2,1)S(1)} %get-tuple-element.60.spread_d, ...), custom_call_target="tpu_custom_call", output_to_operand_aliasing={{0}: (5, {}), {1}: (6, {}), {2}: (7, {})} | custom-call | tf_op jit(solution)/shard_map/mirror/pallas_call | solution.py:469
  79.7 3.7 %collective-permute-done.3.rest_0_ = bf16[1,64,3072]{2,1,0:T(8,128)(2,1)S(1)} collective-permute-done((bf16[1,64,3072]{2,1,0:T(8,128)(2,1)S(1)}, bf16[1,64,3072]{2,1,0:T(8,128)(2,1)S(1)}, u32[]{:S(2)}, u32[]{:S(2)}) %collective-permute-start.3) | collective-permute-done | bytes 393248 | tf_op jit(solution)/shard_map/ppermute | solution.py:504
  83.4 3.5 %mirror.9 = (bf16[4,1024,1024]{2,1,0:T(8,128)(2,1)S(1)}, bf16[64,26624]{1,0:T(8,128)(2,1)S(1)}, bf16[1024,1024]{1,0:T(8,128)(2,1)}) custom-call(s32[478]{0:T(512)S(4)} %get-tuple-element.59.scalars, bf16[4,8,256,128]{3,2,1,0:T(8,128)(2,1)S(1)} %get-tuple-element.60.spread_d, ...), custom_call_target="tpu_custom_call", output_to_operand_aliasing={{0}: (5, {}), {1}: (6, {}), {2}: (7, {})} | custom-call | tf_op jit(solution)/shard_map/mirror/pallas_call | solution.py:469
  86.9 2.1 %collective-permute-done.2.rest_0_ = bf16[1,64,2048]{2,1,0:T(8,128)(2,1)S(1)} collective-permute-done((bf16[1,64,2048]{2,1,0:T(8,128)(2,1)S(1)}, bf16[1,64,2048]{2,1,0:T(8,128)(2,1)S(1)}, u32[]{:S(2)}, u32[]{:S(2)}) %collective-permute-start.2) | collective-permute-done | bytes 262176 | tf_op jit(solution)/shard_map/ppermute | solution.py:504
  89.0 3.0 %mirror.10 = (bf16[4,1024,1024]{2,1,0:T(8,128)(2,1)S(1)}, bf16[64,26624]{1,0:T(8,128)(2,1)S(1)}, bf16[1024,1024]{1,0:T(8,128)(2,1)}) custom-call(s32[478]{0:T(512)S(4)} %get-tuple-element.59.scalars, bf16[4,8,256,128]{3,2,1,0:T(8,128)(2,1)S(1)} %get-tuple-element.60.spread_d, ...), custom_call_target="tpu_custom_call", output_to_operand_aliasing={{0}: (5, {}), {1}: (6, {}), {2}: (7, {})} | custom-call | tf_op jit(solution)/shard_map/mirror/pallas_call | solution.py:469
  92.0 0.0 collective-permute-done.1.rest_0_
  92.0 1.7 %mirror.11 = (bf16[4,1024,1024]{2,1,0:T(8,128)(2,1)S(1)}, bf16[64,26624]{1,0:T(8,128)(2,1)S(1)}, bf16[1024,1024]{1,0:T(8,128)(2,1)}) custom-call(s32[478]{0:T(512)S(4)} %get-tuple-element.59.scalars, bf16[4,8,256,128]{3,2,1,0:T(8,128)(2,1)S(1)} %get-tuple-element.60.spread_d, ...), custom_call_target="tpu_custom_call", output_to_operand_aliasing={{0}: (5, {}), {1}: (6, {}), {2}: (7, {})} | custom-call | tf_op jit(solution)/shard_map/mirror/pallas_call | solution.py:469
  (2 shorter events, 0.0 us)
Async XLA Ops:
  0.0 7.2 %copy-start.2 = (s32[1,16]{1,0:T(1,128)S(1)}, s32[1,16]{1,0:T(1,128)}, u32[]{:S(2)}) copy-start(s32[1,16]{1,0:T(1,128)} %param.13) | copy-start | bytes 196
  0.0 7.3 %copy-start.3 = (s32[1,16]{1,0:T(1,128)S(1)}, s32[1,16]{1,0:T(1,128)}, u32[]{:S(2)}) copy-start(s32[1,16]{1,0:T(1,128)} %param.11) | copy-start | bytes 196
  1.2 20.4 %copy-start = (bf16[1,16,64,64]{3,2,1,0:T(8,128)(2,1)S(1)}, bf16[1,16,64,64]{3,2,1,0:T(8,128)(2,1)}, u32[]{:S(2)}) copy-start(bf16[1,16,64,64]{3,2,1,0:T(8,128)(2,1)} %param.10) | copy-start | bytes 393220
  1.3 69.1 %collective-permute-start.6 = (bf16[1,192,1024]{2,1,0:T(8,128)(2,1)S(1)}, bf16[1,192,1024]{2,1,0:T(8,128)(2,1)S(1)}, u32[]{:S(2)}, u32[]{:S(2)}) collective-permute-start(bf16[1,192,1024]{2,1,0:T(8,128)(2,1)S(1)} %turn.2), channel_id=1, source_target_pairs={{0,16},{4,20},{8,24},{12,28},{16,0},{20,4},{24,8},{28,12},{1,17},{... | collective-permute-start | bytes 1179656 | tf_op jit(solution)/shard_map/ppermute | solution.py:504
  7.2 27.4 %copy-start.1 = (bf16[1,16,64,64]{3,2,1,0:T(8,128)(2,1)S(1)}, bf16[1,16,64,64]{3,2,1,0:T(8,128)(2,1)}, u32[]{:S(2)}) copy-start(bf16[1,16,64,64]{3,2,1,0:T(8,128)(2,1)} %param.12) | copy-start | bytes 393220
  17.9 54.9 %collective-permute-start.5 = (bf16[1,64,3072]{2,1,0:T(8,128)(2,1)S(1)}, bf16[1,64,3072]{2,1,0:T(8,128)(2,1)S(1)}, u32[]{:S(2)}, u32[]{:S(2)}) collective-permute-start(bf16[1,64,3072]{2,1,0:T(8,128)(2,1)S(1)} %get-tuple-element.51), channel_id=1, source_target_pairs={{0,16},{4,20},{8,24},{12,28},{16,0},{20,4},{24,8},{28,12},{1,17},{... | collective-permute-start | bytes 1179656 | tf_op jit(solution)/shard_map/ppermute | solution.py:504
  32.0 43.9 %collective-permute-start.4 = (bf16[1,64,3072]{2,1,0:T(8,128)(2,1)S(1)}, bf16[1,64,3072]{2,1,0:T(8,128)(2,1)S(1)}, u32[]{:S(2)}, u32[]{:S(2)}) collective-permute-start(bf16[1,64,3072]{2,1,0:T(8,128)(2,1)S(1)} %get-tuple-element.65), channel_id=1, source_target_pairs={{0,16},{4,20},{8,24},{12,28},{16,0},{20,4},{24,8},{28,12},{1,17},{... | collective-permute-start | bytes 1179656 | tf_op jit(solution)/shard_map/ppermute | solution.py:504
  44.5 39.0 %collective-permute-start.3 = (bf16[1,64,3072]{2,1,0:T(8,128)(2,1)S(1)}, bf16[1,64,3072]{2,1,0:T(8,128)(2,1)S(1)}, u32[]{:S(2)}, u32[]{:S(2)}) collective-permute-start(bf16[1,64,3072]{2,1,0:T(8,128)(2,1)S(1)} %get-tuple-element.64), channel_id=1, source_target_pairs={{0,16},{4,20},{8,24},{12,28},{16,0},{20,4},{24,8},{28,12},{1,17},{... | collective-permute-start | bytes 1179656 | tf_op jit(solution)/shard_map/ppermute | solution.py:504
  67.7 21.3 %collective-permute-start.2 = (bf16[1,64,2048]{2,1,0:T(8,128)(2,1)S(1)}, bf16[1,64,2048]{2,1,0:T(8,128)(2,1)S(1)}, u32[]{:S(2)}, u32[]{:S(2)}) collective-permute-start(bf16[1,64,2048]{2,1,0:T(8,128)(2,1)S(1)} %get-tuple-element.63), channel_id=1, source_target_pairs={{0,16},{4,20},{8,24},{12,28},{16,0},{20,4},{24,8},{28,12},{1,17},{... | collective-permute-start | bytes 786440 | tf_op jit(solution)/shard_map/ppermute | solution.py:504
  70.4 21.6 %collective-permute-start.1 = (bf16[1,64,1280]{2,1,0:T(8,128)(2,1)S(1)}, bf16[1,64,1280]{2,1,0:T(8,128)(2,1)S(1)}, u32[]{:S(2)}, u32[]{:S(2)}) collective-permute-start(bf16[1,64,1280]{2,1,0:T(8,128)(2,1)S(1)} %get-tuple-element.56), channel_id=1, source_target_pairs={{0,16},{4,20},{8,24},{12,28},{16,0},{20,4},{24,8},{28,12},{1,17},{... | collective-permute-start | bytes 491528 | tf_op jit(solution)/shard_map/ppermute | solution.py:504
